TPU v7x, 256 devices: a whole 4x4x8 slice. The times are simulated.
256 devices in a mesh: blk: 32 (over z, y_lo, core), pw: 8 (over y_hi, x).
Axes of the slice: x: 4, y: 4 (y_hi: 2, y_lo: 2; y = y_hi * 2 + y_lo), z: 8, core: 2. Of those that a mesh axis runs over, the one named last changes fastest.
Arguments:
- occupied_states: bfloat16 [2, 128, 72, 10368], P(None, 'blk', 'pw'), may hold values from -0.025512695 to 0.025512695
- empty_states: bfloat16 [2, 256, 72, 10368], P(None, 'blk', 'pw'), may hold values from -0.025512695 to 0.025512695
- occ_energy: bfloat16 [128], P('blk'), may hold values from -2 to -0.099609375
- empty_energy: bfloat16 [256], P('blk'), may hold values from 0.099609375 to 2
- gvectors: int32 [3, 4096], replicated, may hold values from -16 to 16
Outputs:
- response: float32 [4096, 2, 4096], P('blk', None, 'pw')
Inputs may be any that keep to these rules, and one draw needn't show every extreme that they name: `gvectors`: each plane wave's three components lie within 16 of zero.
All inputs are finite; a program needn't handle non-finite values.
Results may differ from a plain program's by a relative error of at most 0.011.
Values may be sent and summed in bfloat16 or wider, within the bound.
A program may use at most 192 MiB of HBM per device.

v0:
```python
import math

import jax
import jax.numpy as jnp
from jax import lax
from jax.sharding import PartitionSpec as P

GX = 72
GY = 72
GZ = 144
KMAX = 16


omega_shift = 0.5


def from_behind(value, axis, steps):
    count = lax.axis_size(axis)
    pairs = [(source, (source + steps) % count) for source in range(count)]
    return lax.ppermute(value, axis, pairs)


def axis_tables(length, count_half):
    grid_steps = jnp.arange(length, dtype=jnp.int32)
    values = jnp.arange(2 * count_half + 1, dtype=jnp.int32) - count_half
    phase_steps = grid_steps[:, None] * values[None, :] % length
    angles = phase_steps.astype(jnp.float32) * (2.0 * math.pi / length)
    return (jnp.cos(angles).astype(jnp.bfloat16), jnp.sin(angles).astype(jnp.bfloat16))


def depth_table():
    cosines, sine_table = axis_tables(GZ, KMAX)
    upper = jnp.concatenate([cosines, -sine_table], axis=1)
    lower = jnp.concatenate([sine_table, cosines], axis=1)
    return jnp.concatenate([upper, lower], axis=0)


def row_table():
    cosines, sine_table = axis_tables(GY, KMAX)
    from_real = jnp.stack([cosines, -sine_table], axis=1)
    from_imag = jnp.stack([sine_table, cosines], axis=1)
    return jnp.stack([from_real, from_imag], axis=0)


def pair_planes(occ_state, partners):
    occ_real = occ_state[0].astype(jnp.float32)[None]
    occ_imag = occ_state[1].astype(jnp.float32)[None]
    emp_real = partners[0].astype(jnp.float32)
    emp_imag = partners[1].astype(jnp.float32)
    real_part = occ_real * emp_real + occ_imag * emp_imag
    imag_part = occ_real * emp_imag - occ_imag * emp_real
    line_total = partners.shape[1] * partners.shape[2] * GY
    joined = jnp.concatenate(
        [real_part.reshape(line_total, GZ), imag_part.reshape(line_total, GZ)], axis=1
    )
    return joined.astype(jnp.bfloat16)


def plane_sections(occ_state, partners, z_table, y_table):
    pair_rows = pair_planes(occ_state, partners)
    depth_out = jnp.dot(pair_rows, z_table, preferred_element_type=jnp.float32).astype(jnp.bfloat16)
    pair_count = partners.shape[1]
    plane_count = partners.shape[2]
    side = 2 * KMAX + 1
    depth_out = depth_out.reshape(pair_count, plane_count, GY, 2, side)
    row_out = jnp.einsum(
        "kxyiq,iyop->kxopq", depth_out, y_table, preferred_element_type=jnp.float32
    )
    return row_out.astype(jnp.bfloat16).reshape(pair_count, plane_count, 2, side * side)


def wave_picks(planes, wave_rows, first_plane):
    side = 2 * KMAX + 1
    pair_count = planes.shape[0]
    plane_count = planes.shape[1]
    wave_count = wave_rows.shape[1]
    pick_index = (wave_rows[1] + KMAX) * side + (wave_rows[2] + KMAX)
    selector = (jnp.arange(side * side, dtype=jnp.int32)[:, None] == pick_index[None, :]).astype(
        jnp.bfloat16
    )
    flat_rows = planes.reshape(pair_count * plane_count * 2, side * side)
    picked = jnp.dot(flat_rows, selector, preferred_element_type=jnp.float32)
    picked = picked.reshape(pair_count, plane_count, 2, wave_count)
    plane_ids = first_plane + jnp.arange(plane_count, dtype=jnp.int32)
    phase_steps = plane_ids[:, None] * wave_rows[0][None, :] % GX
    angles = phase_steps.astype(jnp.float32) * (2.0 * math.pi / GX)
    cosines = jnp.cos(angles)
    sine_table = jnp.sin(angles)
    real_part = jnp.sum(picked[:, :, 0] * cosines + picked[:, :, 1] * sine_table, axis=1)
    imag_part = jnp.sum(picked[:, :, 1] * cosines - picked[:, :, 0] * sine_table, axis=1)
    return jnp.stack([real_part, imag_part], axis=1)


def pair_weights(occ_level, emp_level):
    energy_gap = (
        emp_level.astype(jnp.float32)[None, :]
        - occ_level.astype(jnp.float32)[:, None]
        + omega_shift
    )
    return (-2.0 / energy_gap).reshape(-1)


def right_rows(weighted):
    turned = jnp.stack([weighted[:, 1], -weighted[:, 0]], axis=1)
    joined = jnp.stack([weighted, turned], axis=2)
    return joined.reshape(weighted.shape[0] * 2, 2 * weighted.shape[2])


def product_rows(left_part, right_side):
    row_total = left_part.shape[2]
    left_side = left_part.reshape(-1, row_total)
    product = lax.dot_general(
        left_side, right_side, (((0,), (0,)), ((), ())), preferred_element_type=jnp.float32
    )
    return product.reshape(row_total, 2, -1)


def shards(occupied_states, empty_states, occ_energy, empty_energy, gvectors):
    pw_place = lax.axis_index("pw")
    planes_here = occupied_states.shape[2]
    received = []
    moving = (empty_states, empty_energy)
    for distance in range(2):
        moving = from_behind((moving[0], moving[1]), "blk", 1)
        received.append(moving)
    partners = jnp.concatenate([received[0][0], received[1][0]], axis=1)
    partner_levels = jnp.concatenate([received[0][1], received[1][1]], axis=0)
    factor = pair_weights(occ_energy, partner_levels)
    z_table = depth_table()
    y_table = row_table()

    def one_state(state_index):
        occ_state = lax.dynamic_index_in_dim(occupied_states, state_index, 1, keepdims=False)
        return plane_sections(occ_state, partners, z_table, y_table)

    section_out = lax.map(one_state, jnp.arange(occupied_states.shape[1], dtype=jnp.int32))
    pair_total = section_out.shape[0] * section_out.shape[1]
    side_square = section_out.shape[4]
    planes = section_out.reshape(pair_total, planes_here, 2, side_square)
    first_plane = pw_place * planes_here
    partial_sums = wave_picks(planes, gvectors, first_plane)
    density = lax.psum_scatter(partial_sums, "pw", scatter_dimension=2, tiled=True)
    density_low = density.astype(jnp.bfloat16)
    density_all = lax.all_gather(density_low, "pw", axis=2, tiled=True)
    weighted = (density_low.astype(jnp.float32) * factor[:, None, None]).astype(jnp.bfloat16)
    right_side = right_rows(weighted)
    return lax.psum_scatter(
        product_rows(density_all, right_side), "blk", scatter_dimension=0, tiled=True
    )


def solution(mesh):
    return jax.shard_map(
        shards,
        mesh=mesh,
        in_specs=(P(None, "blk", "pw", None), P(None, "blk", "pw", None), P("blk"), P("blk"), P()),
        out_specs=P("blk", None, "pw"),
        check_vma=False,
    )
```

profile of v0, /device:TPU:26, one launch (start us, length us, event | category | flops | bytes accessed | tf_op | source)
XLA Modules:
  0.0 919.3 jit_solution(17713091323238573138)
XLA Ops:
  6.5 35.2 %collective-permute-done = bf16[2,8,9,10368]{3,1,2,0:T(8,128)(2,1)S(1)} collective-permute-done((bf16[2,8,9,10368]{3,1,2,0:T(8,128)(2,1)}, bf16[2,8,9,10368]{3,1,2,0:T(8,128)(2,1)S(1)}, u32[]{:S(2)}, u32[]{:S(2)}) %collective-permute-start) | collective-permute-done | bytes 2986016 | tf_op jit(solution)/shard_map/ppermute | solution.py:20
  49.5 27.3 %collective-permute-done.1 = bf16[2,8,9,10368]{3,1,2,0:T(8,128)(2,1)} collective-permute-done((bf16[2,8,9,10368]{3,1,2,0:T(8,128)(2,1)S(1)}, bf16[2,8,9,10368]{3,1,2,0:T(8,128)(2,1)}, u32[]{:S(2)}, u32[]{:S(2)}) %collective-permute-start.1) | collective-permute-done | bytes 2986016 | tf_op jit(solution)/shard_map/ppermute | solution.py:20
  81.6 8.2 copy.39
  89.7 461.0 %while.10 = (s32[]{:T(128)}, bf16[4,16,9,2,1089]{4,1,0,3,2:T(8,128)(2,1)}, s32[4]{0:T(128)S(1)}, bf16[2,4,9,10368]{3,2,1,0:T(8,128)(2,1)}, bf16[2,16,9,10368]{3,...) while((s32[]{:T(128)}, ...), condition=%wide.region_1.2_spmd, body=%wide.region_0.1_spmd.sunk | while | flops 512534304 | bytes 125329072 | solution.py:136
  98.6 12.5 %mul.446 = f32[10368,144]{1,0:T(8,128)} reshape(f32[16,9,10368]{2,1,0:T(8,128)} %mul.445) | data formatting | bytes 11943936 | tf_op jit(solution)/shard_map/while/body/eval_jaxpr/mul | solution.py:50
  115.7 12.5 %mul.448 = f32[10368,144]{1,0:T(8,128)} reshape(f32[16,9,10368]{2,1,0:T(8,128)} %mul.447) | data formatting | bytes 11943936 | tf_op jit(solution)/shard_map/while/body/eval_jaxpr/mul | solution.py:50
  128.2 10.7 %slice_convert_fusion.3 = (f32[1,16,9,10368]{3,2,1,0:T(8,128)}, f32[1,16,9,10368]{3,2,1,0:T(8,128)}) fusion(bf16[2,16,9,10368]{3,2,1,0:T(8,128)(2,1)} %get-tuple-element.181), kind=kLoop, calls=%fused_computation.7.clone.1 | loop fusion | flops 2985984 | bytes 17915904 | tf_op jit(solution)/shard_map/while/body/eval_jaxpr/convert_element_type | solution.py:49
  138.9 12.5 %reshape.281 = f32[10368,144]{1,0:T(8,128)} reshape(f32[1,16,9,10368]{3,2,1,0:T(8,128)} %get-tuple-element.150) | data formatting | bytes 11943936 | tf_op jit(solution)/shard_map/while/body/eval_jaxpr/convert_element_type | solution.py:49
  151.4 12.5 %reshape.282 = f32[10368,144]{1,0:T(8,128)} reshape(f32[1,16,9,10368]{3,2,1,0:T(8,128)} %get-tuple-element.152) | data formatting | bytes 11943936 | tf_op jit(solution)/shard_map/while/body/eval_jaxpr/convert_element_type | solution.py:48
  163.9 14.5 %add_convert_fusion.2 = (bf16[10368,144]{1,0:T(8,128)(2,1)S(1)}, bf16[10368,144]{1,0:T(8,128)(2,1)S(1)}) fusion(f32[10368,144]{1,0:T(8,128)} %mul.446, f32[10368,144]{1,0:T(8,128)} %reshape.281, f32[10368,144]{1,0:T(8,128)} %mul.448, f32[10368,144]{1,0:T(8,128)} %reshape.282), kind=kLoop, calls=%fused_computation.2.clone.1 | loop fusion | flops 11943936 | bytes 29859840 | tf_op jit(solution)/shard_map/convert.4
  211.7 12.5 %mul.446 = f32[10368,144]{1,0:T(8,128)} reshape(f32[16,9,10368]{2,1,0:T(8,128)} %mul.445) | data formatting | bytes 11943936 | tf_op jit(solution)/shard_map/while/body/eval_jaxpr/mul | solution.py:50
  228.8 12.5 %mul.448 = f32[10368,144]{1,0:T(8,128)} reshape(f32[16,9,10368]{2,1,0:T(8,128)} %mul.447) | data formatting | bytes 11943936 | tf_op jit(solution)/shard_map/while/body/eval_jaxpr/mul | solution.py:50
  241.2 10.7 %slice_convert_fusion.3 = (f32[1,16,9,10368]{3,2,1,0:T(8,128)}, f32[1,16,9,10368]{3,2,1,0:T(8,128)}) fusion(bf16[2,16,9,10368]{3,2,1,0:T(8,128)(2,1)} %get-tuple-element.181), kind=kLoop, calls=%fused_computation.7.clone.1 | loop fusion | flops 2985984 | bytes 17915904 | tf_op jit(solution)/shard_map/while/body/eval_jaxpr/convert_element_type | solution.py:49
  251.9 12.5 %reshape.281 = f32[10368,144]{1,0:T(8,128)} reshape(f32[1,16,9,10368]{3,2,1,0:T(8,128)} %get-tuple-element.150) | data formatting | bytes 11943936 | tf_op jit(solution)/shard_map/while/body/eval_jaxpr/convert_element_type | solution.py:49
  264.4 12.5 %reshape.282 = f32[10368,144]{1,0:T(8,128)} reshape(f32[1,16,9,10368]{3,2,1,0:T(8,128)} %get-tuple-element.152) | data formatting | bytes 11943936 | tf_op jit(solution)/shard_map/while/body/eval_jaxpr/convert_element_type | solution.py:48
  276.9 14.5 %add_convert_fusion.2 = (bf16[10368,144]{1,0:T(8,128)(2,1)S(1)}, bf16[10368,144]{1,0:T(8,128)(2,1)S(1)}) fusion(f32[10368,144]{1,0:T(8,128)} %mul.446, f32[10368,144]{1,0:T(8,128)} %reshape.281, f32[10368,144]{1,0:T(8,128)} %mul.448, f32[10368,144]{1,0:T(8,128)} %reshape.282), kind=kLoop, calls=%fused_computation.2.clone.1 | loop fusion | flops 11943936 | bytes 29859840 | tf_op jit(solution)/shard_map/convert.4
  324.7 12.5 %mul.446 = f32[10368,144]{1,0:T(8,128)} reshape(f32[16,9,10368]{2,1,0:T(8,128)} %mul.445) | data formatting | bytes 11943936 | tf_op jit(solution)/shard_map/while/body/eval_jaxpr/mul | solution.py:50
  341.8 12.5 %mul.448 = f32[10368,144]{1,0:T(8,128)} reshape(f32[16,9,10368]{2,1,0:T(8,128)} %mul.447) | data formatting | bytes 11943936 | tf_op jit(solution)/shard_map/while/body/eval_jaxpr/mul | solution.py:50
  354.3 10.7 %slice_convert_fusion.3 = (f32[1,16,9,10368]{3,2,1,0:T(8,128)}, f32[1,16,9,10368]{3,2,1,0:T(8,128)}) fusion(bf16[2,16,9,10368]{3,2,1,0:T(8,128)(2,1)} %get-tuple-element.181), kind=kLoop, calls=%fused_computation.7.clone.1 | loop fusion | flops 2985984 | bytes 17915904 | tf_op jit(solution)/shard_map/while/body/eval_jaxpr/convert_element_type | solution.py:49
  364.9 12.5 %reshape.281 = f32[10368,144]{1,0:T(8,128)} reshape(f32[1,16,9,10368]{3,2,1,0:T(8,128)} %get-tuple-element.150) | data formatting | bytes 11943936 | tf_op jit(solution)/shard_map/while/body/eval_jaxpr/convert_element_type | solution.py:49
  377.5 12.5 %reshape.282 = f32[10368,144]{1,0:T(8,128)} reshape(f32[1,16,9,10368]{3,2,1,0:T(8,128)} %get-tuple-element.152) | data formatting | bytes 11943936 | tf_op jit(solution)/shard_map/while/body/eval_jaxpr/convert_element_type | solution.py:48
  390.0 14.5 %add_convert_fusion.2 = (bf16[10368,144]{1,0:T(8,128)(2,1)S(1)}, bf16[10368,144]{1,0:T(8,128)(2,1)S(1)}) fusion(f32[10368,144]{1,0:T(8,128)} %mul.446, f32[10368,144]{1,0:T(8,128)} %reshape.281, f32[10368,144]{1,0:T(8,128)} %mul.448, f32[10368,144]{1,0:T(8,128)} %reshape.282), kind=kLoop, calls=%fused_computation.2.clone.1 | loop fusion | flops 11943936 | bytes 29859840 | tf_op jit(solution)/shard_map/convert.4
  437.7 12.5 %mul.446 = f32[10368,144]{1,0:T(8,128)} reshape(f32[16,9,10368]{2,1,0:T(8,128)} %mul.445) | data formatting | bytes 11943936 | tf_op jit(solution)/shard_map/while/body/eval_jaxpr/mul | solution.py:50
  454.8 12.5 %mul.448 = f32[10368,144]{1,0:T(8,128)} reshape(f32[16,9,10368]{2,1,0:T(8,128)} %mul.447) | data formatting | bytes 11943936 | tf_op jit(solution)/shard_map/while/body/eval_jaxpr/mul | solution.py:50
  467.3 10.7 %slice_convert_fusion.3 = (f32[1,16,9,10368]{3,2,1,0:T(8,128)}, f32[1,16,9,10368]{3,2,1,0:T(8,128)}) fusion(bf16[2,16,9,10368]{3,2,1,0:T(8,128)(2,1)} %get-tuple-element.181), kind=kLoop, calls=%fused_computation.7.clone.1 | loop fusion | flops 2985984 | bytes 17915904 | tf_op jit(solution)/shard_map/while/body/eval_jaxpr/convert_element_type | solution.py:49
  478.0 12.5 %reshape.281 = f32[10368,144]{1,0:T(8,128)} reshape(f32[1,16,9,10368]{3,2,1,0:T(8,128)} %get-tuple-element.150) | data formatting | bytes 11943936 | tf_op jit(solution)/shard_map/while/body/eval_jaxpr/convert_element_type | solution.py:49
  490.5 12.5 %reshape.282 = f32[10368,144]{1,0:T(8,128)} reshape(f32[1,16,9,10368]{3,2,1,0:T(8,128)} %get-tuple-element.152) | data formatting | bytes 11943936 | tf_op jit(solution)/shard_map/while/body/eval_jaxpr/convert_element_type | solution.py:48
  503.0 14.5 %add_convert_fusion.2 = (bf16[10368,144]{1,0:T(8,128)(2,1)S(1)}, bf16[10368,144]{1,0:T(8,128)(2,1)S(1)}) fusion(f32[10368,144]{1,0:T(8,128)} %mul.446, f32[10368,144]{1,0:T(8,128)} %reshape.281, f32[10368,144]{1,0:T(8,128)} %mul.448, f32[10368,144]{1,0:T(8,128)} %reshape.282), kind=kLoop, calls=%fused_computation.2.clone.1 | loop fusion | flops 11943936 | bytes 29859840 | tf_op jit(solution)/shard_map/convert.4
  550.8 14.3 %fusion.13 = f32[64,9,2,4096]{3,0,2,1:T(8,128)S(1)} fusion(bf16[64,9,2,1089]{3,0,2,1:T(8,128)(2,1)} %bitcast.100, s32[4096]{0:T(1024)S(1)} %bitcast.99), kind=kOutput, calls=%fused_computation.21 | convolution fusion | flops 10281553920 | bytes 21399808 | tf_op jit(solution)/shard_map/dot_general | solution.py:82
  579.7 76.0 %reduce-scatter.3.cloned.1.call-done = f32[64,2,512]{2,0,1:T(8,128)} async-done(((f32[64,2,4096]{2,0,1:T(8,128)}), f32[64,2,512]{2,0,1:T(8,128)}) %reduce-scatter.3.cloned.1.call-update) | async-done | bytes 262160 | tf_op jit(solution)/shard_map/reduce_scatter | solution.py:142
  657.9 52.7 %all-gather.2.cloned.1.call-done = bf16[64,2,4096]{2,0,1:T(8,128)(2,1)} async-done(((bf16[64,2,512]{2,0,1:T(8,128)(2,1)}), bf16[64,2,4096]{2,0,1:T(8,128)(2,1)}) %all-gather.2.cloned.1.call-update) | async-done | bytes 1048592 | tf_op jit(solution)/shard_map/all_gather | solution.py:144
  721.5 188.8 %reduce-scatter.5.cloned.1.call-done = f32[128,2,512]{2,0,1:T(8,128)} async-done(((f32[4096,2,512]{2,0,1:T(8,128)}), f32[128,2,512]{2,0,1:T(8,128)}) %reduce-scatter.5.cloned.1.call-update) | async-done | bytes 524304 | tf_op jit(solution)/shard_map/reduce_scatter | solution.py:147
  (94 shorter events, 185.7 us)
Async XLA Ops:
  6.5 649.1 %reduce-scatter.3.cloned.1.call-start = ((), (), s32[]{:S(2)}) async-start(), calls=%async_computation.2 | async-start | bytes 2359296 | tf_op jit(solution)/shard_map/reduce_scatter | solution.py:142
  6.5 35.2 %collective-permute-start = (bf16[2,8,9,10368]{3,1,2,0:T(8,128)(2,1)}, bf16[2,8,9,10368]{3,1,2,0:T(8,128)(2,1)S(1)}, u32[]{:S(2)}, u32[]{:S(2)}) collective-permute-start(bf16[2,8,9,10368]{3,1,2,0:T(8,128)(2,1)} %param.8), channel_id=1, source_target_pairs={{0,8},{8,16},{16,24},{24,32},{32,40},{40,48},{48,56},{56,64},{64,7... | collective-permute-start | bytes 8957960 | tf_op jit(solution)/shard_map/ppermute | solution.py:20
  41.7 35.1 %collective-permute-start.1 = (bf16[2,8,9,10368]{3,1,2,0:T(8,128)(2,1)S(1)}, bf16[2,8,9,10368]{3,1,2,0:T(8,128)(2,1)}, u32[]{:S(2)}, u32[]{:S(2)}) collective-permute-start(bf16[2,8,9,10368]{3,1,2,0:T(8,128)(2,1)S(1)} %collective-permute-done), channel_id=1, source_target_pairs={{0,8},{8,16},{16,24},{24,32},{32,40},{40,48},{48,56},{56,64},{64,7... | collective-permute-start | bytes 8957960 | tf_op jit(solution)/shard_map/ppermute | solution.py:20
  89.7 461.1 %copy-start.2 = (s32[1,4096]{1,0:T(1,128)S(1)}, s32[1,4096]{1,0:T(1,128)}, u32[]{:S(2)}) copy-start(s32[1,4096]{1,0:T(1,128)} %get-tuple-element.91) | copy-start | bytes 49156
  550.8 14.3 %copy-start = (f32[9,4096]{1,0:T(8,128)S(1)}, f32[9,4096]{1,0:T(8,128)}, u32[]{:S(2)}) copy-start(f32[9,4096]{1,0:T(8,128)} %get-tuple-element.92) | copy-start | bytes 442372
  550.8 14.3 %copy-start.1 = (f32[9,4096]{1,0:T(8,128)S(1)}, f32[9,4096]{1,0:T(8,128)}, u32[]{:S(2)}) copy-start(f32[9,4096]{1,0:T(8,128)} %get-tuple-element.93) | copy-start | bytes 442372
  568.5 1.6 copy-start.4
  568.5 2.4 copy-start.3
  570.1 140.5 %all-gather.2.cloned.1.call-start = ((), (), s32[]{:S(2)}) async-start(), calls=%async_computation.3 | async-start | bytes 1179648 | tf_op jit(solution)/shard_map/all_gather | solution.py:144
  570.1 3.2 collective-permute-start.2
  573.3 6.1 collective-permute-start.3
  657.3 252.9 %reduce-scatter.5.cloned.1.call-start = ((), (), s32[]{:S(2)}) async-start(), calls=%async_computation.4 | async-start | bytes 17301504 | tf_op jit(solution)/shard_map/reduce_scatter | solution.py:147
Sparse Core Ops, SparseCore 0:
  570.2 85.4 reduce-scatter.2
  658.5 52.1 all-gather.1
  721.6 188.5 reduce-scatter.4
where the time goes:
time: 931 us; the launch traced here: 919 us
  waiting for transfers between devices  387 us (42%)
  local copies, waits for them, and re-layouts  313 us (34%)
  other arithmetic  121 us (13%)
  matrix products  65.2 us (7%)
  loops' own time  17.1 us (2%)
  between operations  13.5 us (1%)
    reduce_scatter x1, waiting for transfers between devices, shards(): lax.psum_scatter(product_rows(density_all, right_side), 'blk', scatter_di...  189 us
    mul x16, local copies, waits for them, and re-layouts, pair_planes(): real_part = occ_real * emp_real + occ_imag * emp_imag  137 us
    reduce_scatter x1, waiting for transfers between devices, shards(): lax.psum_scatter(partial_sums, 'pw', scatter_dimension=2, tiled=True)  76 us
    ppermute x4, waiting for transfers between devices, from_behind(): return lax.ppermute(value, axis, pairs)  69.2 us
    another operation x4, other arithmetic  58 us
    all_gather x1, waiting for transfers between devices, shards(): density_all = lax.all_gather(density_low, 'pw', axis=2, tiled=True)  52.7 us
    convert_element_type x4, local copies, waits for them, and re-layouts, pair_planes(): emp_imag = partners[1].astype(jnp.float32)  50.1 us
    convert_element_type x4, local copies, waits for them, and re-layouts, pair_planes(): emp_real = partners[0].astype(jnp.float32)  49.9 us
  transfers between devices with their start and end apart: 7, of which 7 were waited for; matrix products, arithmetic and copies ran while one was open for 1% of the time, Pallas kernels for 0%

commit v1 on v0

v1 whole, which is shorter than its diff:
```python
import functools
import math

import jax
import jax.numpy as jnp
import numpy as np
from jax import lax
from jax.experimental import pallas as pl
from jax.experimental.pallas import tpu as pltpu
from jax.sharding import PartitionSpec as P
import ml_dtypes

GX = 72
GY = 72
GZ = 144
KMAX = 16
SIDE = 2 * KMAX + 1
PLANES = 9
CELLS = GY * GZ
NG = 4096
GROUPS = 9
GROUP_CELLS = 8 * GZ
Z_ROWS = SIDE * 8
ROWS_X = 80
DEPTH = PLANES * ROWS_X
HALF = (SIDE * SIDE + 1) // 2
WAVE_ROWS = 1104
Q_SLOTS = 34
LANES = 128
omega_shift = 0.5


def z_table():
    z = np.arange(GZ)
    out = np.zeros((Z_ROWS, GROUP_CELLS), np.float64)
    for q in range(KMAX + 1):
        angle = 2 * np.pi * ((q * z) % GZ) / GZ
        for y in range(8):
            out[q * 8 + y, y * GZ : (y + 1) * GZ] = np.cos(angle)
            if q:
                out[(KMAX + q) * 8 + y, y * GZ : (y + 1) * GZ] = np.sin(angle)
    return out.astype(np.float32).astype(ml_dtypes.bfloat16)


def plane_table(groups):
    h = np.arange(HALF)
    p = (h + KMAX) // SIDE
    a = h - SIDE * p
    out = np.zeros((groups, WAVE_ROWS, PLANES, ROWS_X), np.float64)
    y = np.arange(GY)
    for group in range(groups):
        for plane in range(PLANES):
            x = group * PLANES + plane
            steps = (p[:, None] * y[None, :] + a[:, None] * x) % GX
            out[group, 0 : 2 * HALF : 2, plane, :GY] = np.cos(2 * np.pi * steps / GX)
            out[group, 1 : 2 * HALF : 2, plane, :GY] = np.sin(2 * np.pi * steps / GX)
    return out.reshape(groups, WAVE_ROWS, DEPTH).astype(np.float32).astype(ml_dtypes.bfloat16)


def turned(value):
    lane = lax.broadcasted_iota(jnp.int32, value.shape, 1)
    ahead = pltpu.roll(value, LANES - 8, 1)
    behind = pltpu.roll(value, 8, 1)
    return jnp.where((lane & 8) == 0, ahead, -behind)


def density_kernel(
    index_ref, emp_ref, near_ref, far_ref, ztab_ref, xytab_ref, sign_ref, scale_ref,
    out_ref, occ_f, pairs, depth_out, sections, waves, picked,
):
    plane = pl.program_id(0)

    occ_f[0:8, :] = near_ref[0].astype(jnp.float32)
    occ_f[8:16, :] = far_ref[0].astype(jnp.float32)

    def group_pairs(group, carry):
        for part in range(3):
            start = pl.multiple_of(group * GROUP_CELLS + part * 384, 128)
            cells = pl.ds(start, 384)
            emp = emp_ref[0, :, cells].astype(jnp.float32)
            emp_re, emp_im = emp[0:8], emp[8:16]
            for v in range(8):
                row = v if v < 4 else v + 4
                occ_re = occ_f[row : row + 1, cells]
                occ_im = occ_f[row + 4 : row + 5, cells]
                both = jnp.concatenate(
                    [occ_re * emp_re + occ_im * emp_im, occ_re * emp_im - occ_im * emp_re], axis=0
                )
                rows = pl.ds(pl.multiple_of(group * LANES + v * 16, 16), 16)
                pairs[rows, part * 384 : part * 384 + 384] = both.astype(jnp.bfloat16)
        return carry

    lax.fori_loop(0, GROUPS, group_pairs, 0)
    depth_out[...] = lax.dot_general(
        ztab_ref[...], pairs[...], (((1,), (1,)), ((), ())), preferred_element_type=jnp.float32
    )
    spot = pl.ds(pl.multiple_of(plane * ROWS_X, 16), ROWS_X)
    blank = jnp.zeros((ROWS_X - GY, LANES), jnp.float32)

    def rows_of(first):
        parts = [depth_out[first : first + 8, t * LANES : (t + 1) * LANES] for t in range(GROUPS)]
        return jnp.concatenate(parts + [blank], axis=0)

    def put(slot, value):
        half = slot % 2
        sections[slot // 2, spot, half * LANES : (half + 1) * LANES] = value.astype(jnp.bfloat16)

    put(KMAX, rows_of(0))
    for q in range(1, KMAX + 1):
        cosine = rows_of(q * 8)
        sine = turned(rows_of((KMAX + q) * 8))
        put(KMAX + q, cosine + sine)
        put(KMAX - q, cosine - sine)

    @pl.when(plane == PLANES - 1)
    def _():
        sections[Q_SLOTS // 2 - 1, :, LANES:] = jnp.zeros((DEPTH, LANES), jnp.bfloat16)

        def slot_pair(k, carry):
            product = jnp.dot(xytab_ref[...], sections[k], preferred_element_type=jnp.float32)
            first = pl.multiple_of(k * 2 * WAVE_ROWS, 16)
            waves[pl.ds(first, WAVE_ROWS), :] = product[:, :LANES]
            waves[pl.ds(first + WAVE_ROWS, WAVE_ROWS), :] = product[:, LANES:]
            return carry

        lax.fori_loop(0, Q_SLOTS // 2, slot_pair, 0)

        def pick(step, carry):
            first = step * 16
            for i in range(16):
                picked[pl.ds((first + i) * 2, 2), :] = waves[pl.ds(index_ref[first + i], 2), :]
            return carry

        lax.fori_loop(0, NG // 16, pick, 0)

        def finish(step, carry):
            first = step * 128
            cosine = picked[pl.ds(first * 2, 128, stride=2), :]
            sine = picked[pl.ds(first * 2 + 1, 128, stride=2), :]
            rows = pl.ds(pl.multiple_of(first, 128), 128)
            total = (cosine + sign_ref[rows, :] * turned(sine)) * scale_ref[...]
            out_ref[rows, :] = total.astype(out_ref.dtype)
            return carry

        lax.fori_loop(0, NG // 128, finish, 0)


def partial_density(index, emp, near, far, ztab, xytab, sign, scale, interpret=False):
    whole = lambda *shape: pl.BlockSpec(shape, lambda i: (0,) * len(shape))
    plane = lambda rows: pl.BlockSpec((1, rows, CELLS), lambda i: (i, 0, 0))
    return pl.pallas_call(
        density_kernel,
        grid=(PLANES,),
        out_shape=jax.ShapeDtypeStruct((NG, LANES), jnp.float32),
        in_specs=[
            pl.BlockSpec(memory_space=pltpu.SMEM),
            plane(16),
            plane(8),
            plane(8),
            whole(Z_ROWS, GROUP_CELLS),
            whole(WAVE_ROWS, DEPTH),
            whole(NG, 1),
            whole(1, LANES),
        ],
        out_specs=whole(NG, LANES),
        scratch_shapes=[
            pltpu.VMEM((16, CELLS), jnp.float32),
            pltpu.VMEM((GROUPS * LANES, GROUP_CELLS), jnp.bfloat16),
            pltpu.VMEM((Z_ROWS, GROUPS * LANES), jnp.float32),
            pltpu.VMEM((Q_SLOTS // 2, DEPTH, 2 * LANES), jnp.bfloat16),
            pltpu.VMEM((Q_SLOTS * WAVE_ROWS, LANES), jnp.float32),
            pltpu.VMEM((2 * NG, LANES), jnp.float32),
        ],
        compiler_params=pltpu.CompilerParams(vmem_limit_bytes=60 * 2**20),
        cost_estimate=pl.CostEstimate(
            flops=15_000_000_000, bytes_accessed=12_000_000, transcendentals=0
        ),
        interpret=interpret,
    )(index, emp, near, far, ztab, xytab, sign, scale)


def from_ahead(value, axis, steps):
    count = lax.axis_size(axis)
    pairs = [((target + steps) % count, target) for target in range(count)]
    return lax.ppermute(value, axis, pairs)


def plane_rows(states):
    moved = jnp.transpose(states, (2, 0, 1, 3))
    return moved.reshape(moved.shape[0], -1, moved.shape[3])


def pair_scale(occ_levels, emp_level):
    gap = (
        emp_level.astype(jnp.float32)[None, :]
        - occ_levels.astype(jnp.float32)[:, None]
        + omega_shift
    )
    root = jnp.sqrt(2.0 / gap)
    return jnp.broadcast_to(root[:, None, :], (8, 2, 8)).reshape(1, LANES)


def wave_index(gvectors):
    flat = SIDE * gvectors[1] + gvectors[0]
    index = (gvectors[2] + KMAX) * WAVE_ROWS + 2 * jnp.abs(flat)
    sign = jnp.where(flat < 0, -1.0, 1.0).astype(jnp.float32)
    return index, sign[:, None]


def shards(ztab, xytabs, occupied_states, empty_states, occ_energy, empty_energy, gvectors):
    occ = plane_rows(occupied_states)
    emp = plane_rows(empty_states)
    near, near_level = from_ahead(occ, "blk", 1), from_ahead(occ_energy, "blk", 1)
    far, far_level = from_ahead(occ, "blk", 2), from_ahead(occ_energy, "blk", 2)
    scale = pair_scale(jnp.concatenate([near_level, far_level]), empty_energy)
    index, sign = wave_index(gvectors)
    xytab = lax.dynamic_index_in_dim(xytabs, lax.axis_index("pw"), 0, keepdims=False)
    partial_sums = partial_density(index, emp, near, far, ztab, xytab, sign, scale)
    rho = lax.psum_scatter(partial_sums, "pw", scatter_dimension=0, tiled=True)
    rho = rho.astype(jnp.bfloat16)
    right = lax.all_gather(rho, "blk", axis=1, tiled=True)
    column = lax.all_gather(rho, "pw", axis=0, tiled=True)
    left = lax.all_to_all(column, "blk", split_axis=0, concat_axis=1, tiled=True)
    parts = left.reshape(left.shape[0], -1, 2, 8)
    side = jnp.stack([-parts[:, :, 1], parts[:, :, 0]], axis=2).reshape(left.shape)
    both = jnp.stack([left, side], axis=1).reshape(-1, left.shape[1])
    product = lax.dot_general(
        -both, right, (((1,), (1,)), ((), ())), preferred_element_type=jnp.float32
    )
    return product.reshape(left.shape[0], 2, -1)


def solution(mesh):
    ztab = z_table()
    xytabs = plane_table(mesh.shape["pw"])
    return jax.shard_map(
        lambda *args: shards(jnp.asarray(ztab), jnp.asarray(xytabs), *args),
        mesh=mesh,
        in_specs=(P(None, "blk", "pw", None), P(None, "blk", "pw", None), P("blk"), P("blk"), P()),
        out_specs=P("blk", None, "pw"),
        check_vma=False,
    )
```

time: 931 us -> 345 us (0.37)
  local copies, waits for them, and re-layouts: 313 us -> 21.8 us
  waiting for transfers between devices: 387 us -> 206 us
  other arithmetic: 121 us -> 4.96 us
  matrix products: 65.2 us -> 4.11 us
  blocking collectives: 0 us -> 42.6 us
  Pallas kernels: 0 us -> 42.1 us
  loops' own time: 17.1 us -> 0 us
    reduce_scatter x2 -> x1, waiting for transfers between devices: 265 us -> 77.5 us  [shards(): rho = lax.psum_scatter(partial_sums, 'pw', scatter_dimension=0, tiled=True)]
    mul x16 -> x0, local copies, waits for them, and re-layouts: 137 us -> none  [pair_planes(): real_part = occ_real * emp_real + occ_imag * emp_imag]
    convert_element_type x12 -> x0, local copies, waits for them, and re-layouts: 116 us -> none  [the longest x4 50.1 us: pair_planes(): emp_imag = partners[1].astype(jnp.float32)]
    dot_general x10 -> x1, matrix products: 65.2 us -> 4.11 us  [shards(): lax.dot_general(-both, right, (((1,), (1,)), ((), ())), preferred_element...]
    another operation x9 -> x1, other arithmetic: 59.6 us -> 1.18 us  [shards(): jnp.stack([-parts[:, :, 1], parts[:, :, 0]], axis=2).reshape(left.shape)]
    convert_element_type x13 -> x3, other arithmetic: 49.5 us -> 1.7 us  [the longest x1 1.62 us: shards(): rho = rho.astype(jnp.bfloat16)]
    all_to_all x0 -> x1, blocking collectives: none -> 42.6 us  [shards(): lax.all_to_all(column, 'blk', split_axis=0, concat_axis=1, tiled=True)]
    pallas_call x0 -> x1, Pallas kernels: none -> 42.1 us  [partial_density(): pl.pallas_call(density_kernel, grid=(PLANES,), out_shape=jax.ShapeDtypeSt...]
  transfers between devices with their start and end apart: 7 -> 7, of which waited for: 7 -> 5; matrix products, arithmetic and copies ran while one was open for 1% -> 7% of each run, Pallas kernels for 0% -> 0%
where the time goes in v1:
time: 345 us; the launch traced here: 342 us
  waiting for transfers between devices  206 us (60%)
  blocking collectives  42.6 us (12%)
  Pallas kernels  42.1 us (12%)
  local copies, waits for them, and re-layouts  21.8 us (6%)
  between operations  13.1 us (4%)
  starting transfers between devices  7.98 us (2%)
  other arithmetic  4.96 us (1%)
  matrix products  4.11 us (1%)
    reduce_scatter x1, waiting for transfers between devices, shards(): rho = lax.psum_scatter(partial_sums, 'pw', scatter_dimension=0, tiled=True)  77.5 us
    all_gather x1, waiting for transfers between devices, shards(): column = lax.all_gather(rho, 'pw', axis=0, tiled=True)  52 us
    all_to_all x1, blocking collectives, shards(): lax.all_to_all(column, 'blk', split_axis=0, concat_axis=1, tiled=True)  42.6 us
    pallas_call x1, Pallas kernels, partial_density(): pl.pallas_call(density_kernel, grid=(PLANES,), out_shape=jax.ShapeDtypeSt...  42.1 us
    ppermute x4, waiting for transfers between devices, from_ahead(): return lax.ppermute(value, axis, pairs)  40.2 us
    all_gather x1, waiting for transfers between devices, shards(): right = lax.all_gather(rho, 'blk', axis=1, tiled=True)  35.3 us
    ppermute x4, starting transfers between devices, from_ahead(): return lax.ppermute(value, axis, pairs)  7.9 us
  transfers between devices with their start and end apart: 7, of which 5 were waited for; matrix products, arithmetic and copies ran while one was open for 7% of the time, Pallas kernels for 0%

profile of v1, /device:TPU:26, one launch (start us, length us, event | category | flops | bytes accessed | tf_op | source)
XLA Modules:
  0.0 342.4 jit_solution(18044441735611932505)
XLA Ops:
  6.5 0.7 collective-permute-start.3
  7.3 5.7 %collective-permute-start.2 = (bf16[4]{0:T(256)(128)(2,1)}, bf16[4]{0:T(256)(128)(2,1)S(1)}, u32[]{:S(2)}, u32[]{:S(2)}) collective-permute-start(bf16[4]{0:T(256)(128)(2,1)} %param.9), channel_id=1, source_target_pairs={{8,0},{16,8},{24,16},{32,24},{40,32},{48,40},{56,48},{64,56},{72,6... | collective-permute-start | bytes 32 | tf_op jit(solution)/shard_map/ppermute | solution.py:185
  13.0 3.0 copy.13
  16.0 3.4 %reshape.106 = bf16[9,8,10368]{2,1,0:T(8,128)(2,1)} reshape(bf16[9,2,4,10368]{3,2,1,0:T(4,128)(2,1)} %copy.13) | data formatting | bytes 2985984 | tf_op jit(solution)/shard_map/reshape | solution.py:190
  19.5 0.8 collective-permute-start.1
  20.3 0.6 collective-permute-start
  20.9 2.0 copy.14.sign_ref
  22.9 1.8 copy_bitcast_fusion.emp_ref
  24.7 2.8 dynamic-slice_bitcast_fusion.xytab_ref
  27.6 0.6 multiply_add_fusion
  28.2 0.1 maximum_convert_fusion
  28.3 0.1 divide_sqrt_fusion
  28.4 0.7 reshape.107.scale_ref
  29.1 24.2 %collective-permute-done.1.far_ref = bf16[9,8,10368]{2,1,0:T(8,128)(2,1)} collective-permute-done((bf16[9,8,10368]{2,1,0:T(8,128)(2,1)}, bf16[9,8,10368]{2,1,0:T(8,128)(2,1)}, u32[]{:S(2)}, u32[]{:S(2)}) %collective-permute-start.1) | collective-permute-done | bytes 1493024 | tf_op jit(solution)/shard_map/ppermute | solution.py:185
  53.2 16.0 %collective-permute-done.near_ref = bf16[9,8,10368]{2,1,0:T(8,128)(2,1)} collective-permute-done((bf16[9,8,10368]{2,1,0:T(8,128)(2,1)}, bf16[9,8,10368]{2,1,0:T(8,128)(2,1)}, u32[]{:S(2)}, u32[]{:S(2)}) %collective-permute-start) | collective-permute-done | bytes 1493024 | tf_op jit(solution)/shard_map/ppermute | solution.py:185
  69.2 42.1 %shard_map.73 = f32[4096,128]{1,0:T(8,128)} custom-call(s32[4096]{0:T(1024)} %bitcast.26, bf16[9,16,10368]{2,1,0:T(8,128)(2,1)} %copy_bitcast_fusion.emp_ref, bf16[9,8,10368]{2,1,0:T(8,128)(2,1)} %collective-permute-done.near_ref, bf16[9,8,10368]{2,1,0:T(8,128)(2,1)} %collective-permute-done.1.far_ref, bf16[264,1152]{1,0:T(8,128)(2,1)} %constant.31.clone.ztab_ref, ...), custom_call_target="tpu_custom_call" | custom-call | flops 15000000512 | bytes 12000000 | tf_op jit(solution)/shard_map/pallas_call | solution.py:151
  111.3 0.0 all-gather.3.cloned.1.call-start
  111.4 77.5 %reduce-scatter.2.cloned.1.call-done = f32[512,128]{1,0:T(8,128)} async-done(((f32[4096,128]{1,0:T(8,128)}), f32[512,128]{1,0:T(8,128)}) %reduce-scatter.2.cloned.1.call-update) | async-done | bytes 262160 | tf_op jit(solution)/shard_map/reduce_scatter | solution.py:219
  188.9 1.6 convert_element_type.15
  190.5 0.0 all-gather.3.cloned.1.call-update
  190.6 0.0 all-gather.5.cloned.1.call-start
  190.6 0.7 all-gather.5.cloned.1.call-update
  191.3 52.0 %all-gather.3.cloned.1.call-done = bf16[4096,128]{1,0:T(8,128)(2,1)} async-done(((bf16[512,128]{1,0:T(8,128)(2,1)}), bf16[4096,128]{1,0:T(8,128)(2,1)}) %all-gather.3.cloned.1.call-update) | async-done | bytes 1048592 | tf_op jit(solution)/shard_map/all_gather | solution.py:222
  243.3 2.3 copy.15
  245.5 42.6 %all_to_all.16 = bf16[32,128,128]{1,2,0:T(8,128)(2,1)} all-to-all(bf16[32,128,128]{1,2,0:T(8,128)(2,1)} %copy.15), channel_id=1, replica_groups=mesh['blk'=32,'pw'=8] {'blk'}, dimensions={0} | all-to-all | bytes 2097152 | tf_op jit(solution)/shard_map/all_to_all | solution.py:223
  288.2 2.3 copy.19
  290.5 1.3 slice_negate_fusion
  291.8 1.2 pad_maximum_fusion
  293.0 2.3 copy.17
  295.3 35.3 %all-gather.5.cloned.1.call-done = bf16[512,4096]{1,0:T(8,128)(2,1)} async-done(((bf16[512,128]{1,0:T(8,128)(2,1)}), bf16[512,4096]{1,0:T(8,128)(2,1)}) %all-gather.5.cloned.1.call-update) | async-done | bytes 4194320 | tf_op jit(solution)/shard_map/all_gather | solution.py:221
  330.5 4.1 %fusion = f32[128,2,512]{2,0,1:T(8,128)S(1)} fusion(bf16[512,4096]{1,0:T(8,128)(2,1)} %all-gather.5.cloned.1.call-done, bf16[128,1,4096]{2,0,1:T(8,128)(2,1)} %copy.17, bf16[128,1,4096]{2,0,1:T(8,128)(2,1)} %copy.19), kind=kOutput, calls=%fused_computation | convolution fusion | flops 1075838976 | bytes 6815744 | tf_op jit(solution)/shard_map/dot_general | solution.py:227
  334.7 1.2 copy.18
  (13 shorter events, 0.1 us)
Async XLA Ops:
  6.5 16.4 %copy-start = (bf16[2,8,9,10368]{3,1,2,0:T(8,128)(2,1)S(1)}, bf16[2,8,9,10368]{3,1,2,0:T(8,128)(2,1)}, u32[]{:S(2)}) copy-start(bf16[2,8,9,10368]{3,1,2,0:T(8,128)(2,1)} %param.8) | copy-start | bytes 8957956
  6.5 182.4 %reduce-scatter.2.cloned.1.call-start = ((), (), s32[]{:S(2)}) async-start(), calls=%async_computation.2 | async-start | bytes 2359296 | tf_op jit(solution)/shard_map/reduce_scatter | solution.py:219
  6.5 21.7 %collective-permute-start.3 = (bf16[4]{0:T(256)(128)(2,1)}, bf16[4]{0:T(256)(128)(2,1)S(1)}, u32[]{:S(2)}, u32[]{:S(2)}) collective-permute-start(bf16[4]{0:T(256)(128)(2,1)} %param.9), channel_id=1, source_target_pairs={{16,0},{24,8},{32,16},{40,24},{48,32},{56,40},{64,48},{72,56},{80,... | collective-permute-start | bytes 32 | tf_op jit(solution)/shard_map/ppermute | solution.py:185
  7.3 20.9 %collective-permute-start.2 = (bf16[4]{0:T(256)(128)(2,1)}, bf16[4]{0:T(256)(128)(2,1)S(1)}, u32[]{:S(2)}, u32[]{:S(2)}) collective-permute-start(bf16[4]{0:T(256)(128)(2,1)} %param.9), channel_id=1, source_target_pairs={{8,0},{16,8},{24,16},{32,24},{40,32},{48,40},{56,48},{64,56},{72,6... | collective-permute-start | bytes 32 | tf_op jit(solution)/shard_map/ppermute | solution.py:185
  16.0 4.9 %copy-start.2 = (bf16[8]{0:T(256)(128)(2,1)S(1)}, bf16[8]{0:T(256)(128)(2,1)}, u32[]{:S(2)}) copy-start(bf16[8]{0:T(256)(128)(2,1)} %param.10) | copy-start | bytes 52
  16.0 4.9 %copy-start.1 = (s32[3,4096]{1,0:T(4,128)S(1)}, s32[3,4096]{1,0:T(4,128)}, u32[]{:S(2)}) copy-start(s32[3,4096]{1,0:T(4,128)} %param.11) | copy-start | bytes 147460
  19.5 33.8 %collective-permute-start.1 = (bf16[9,8,10368]{2,1,0:T(8,128)(2,1)}, bf16[9,8,10368]{2,1,0:T(8,128)(2,1)}, u32[]{:S(2)}, u32[]{:S(2)}) collective-permute-start(bf16[9,8,10368]{2,1,0:T(8,128)(2,1)} %reshape.106), channel_id=1, source_target_pairs={{16,0},{24,8},{32,16},{40,24},{48,32},{56,40},{64,48},{72,56},{80,... | collective-permute-start | bytes 4478984 | tf_op jit(solution)/shard_map/ppermute | solution.py:185
  20.3 48.9 %collective-permute-start = (bf16[9,8,10368]{2,1,0:T(8,128)(2,1)}, bf16[9,8,10368]{2,1,0:T(8,128)(2,1)}, u32[]{:S(2)}, u32[]{:S(2)}) collective-permute-start(bf16[9,8,10368]{2,1,0:T(8,128)(2,1)} %reshape.106), channel_id=1, source_target_pairs={{8,0},{16,8},{24,16},{32,24},{40,32},{48,40},{56,48},{64,56},{72,6... | collective-permute-start | bytes 4478984 | tf_op jit(solution)/shard_map/ppermute | solution.py:185
  111.3 131.9 %all-gather.3.cloned.1.call-start = ((), (), s32[]{:S(2)}) async-start(), calls=%async_computation.3 | async-start | bytes 1179648 | tf_op jit(solution)/shard_map/all_gather | solution.py:222
  190.6 140.0 %all-gather.5.cloned.1.call-start = ((), (), s32[]{:S(2)}) async-start(), calls=%async_computation.4 | async-start | bytes 4325376 | tf_op jit(solution)/shard_map/all_gather | solution.py:221
Sparse Core Ops, SparseCore 0:
  111.5 77.4 reduce-scatter.1
  191.9 51.3 all-gather.2
  245.2 85.3 all-gather.4

commit v2 on v1

--- a/solution.py
+++ b/solution.py
@@ -151,7 +151,7 @@
     return pl.pallas_call(
         density_kernel,
         grid=(PLANES,),
-        out_shape=jax.ShapeDtypeStruct((NG, LANES), jnp.float32),
+        out_shape=jax.ShapeDtypeStruct((NG, LANES), jnp.bfloat16),
         in_specs=[
             pl.BlockSpec(memory_space=pltpu.SMEM),
             plane(16),
@@ -179,6 +179,275 @@
     )(index, emp, near, far, ztab, xytab, sign, scale)
 
 
+def share_kernel(rows, part_ref, out_ref, everyone, left, relay, passed, arrived, plane_sum, other,
+                 send_sems, sum_sems, ring_sems, side_sems, left_sems):
+    half_rows, quarter = rows // 2, rows // 4
+    blk, pw = lax.axis_index("blk"), lax.axis_index("pw")
+    z, y, core = blk // 4, (blk // 2) % 2, blk % 2
+    x, y_hi = pw % 4, pw // 4
+    n_z = lax.axis_size("blk") // 4
+
+    def place(z=z, y=y, core=core, x=x, y_hi=y_hi):
+        return {"blk": z * 4 + y * 2 + core, "pw": y_hi * 4 + x}
+
+    x_next, x_last = place(x=(x + 1) % 4), place(x=(x + 3) % 4)
+    z_next, z_last = place(z=(z + 1) % n_z), place(z=(z + n_z - 1) % n_z)
+    sibling, beside = place(core=1 - core), place(y=1 - y)
+    facing, across = place(y_hi=1 - y_hi), place(y=1 - y, y_hi=1 - y_hi)
+
+    sends = []
+
+    def copy(source, target, arrival, device):
+        return pltpu.make_async_remote_copy(
+            src_ref=source, dst_ref=target, send_sem=send_sems.at[len(sends)], recv_sem=arrival,
+            device_id=device, device_id_type=pl.DeviceIdType.MESH,
+        )
+
+    def send(source, target, arrival, device):
+        moving = copy(source, target, arrival, device)
+        moving.start()
+        sends.append(moving)
+
+    def landed(target, arrival):
+        pltpu.make_async_copy(target, target, arrival).wait()
+
+    barrier = pltpu.get_barrier_semaphore()
+    neighbours = (x_next, x_last, z_next, z_last, sibling, beside, facing, across)
+    for device in neighbours:
+        pl.semaphore_signal(barrier, inc=1, device_id=device, device_id_type=pl.DeviceIdType.MESH)
+    pl.semaphore_wait(barrier, len(neighbours))
+
+    xn, xl, xo = (x + 1) % 4, (x + 3) % 4, (x + 2) % 4
+    send(part_ref.at[:, xo, 0], relay.at[0], sum_sems.at[0], x_next)
+    send(part_ref.at[:, xo, 1], relay.at[1], sum_sems.at[1], x_last)
+    send(part_ref.at[:, xn, 1], arrived.at[0], sum_sems.at[2], x_next)
+    send(part_ref.at[:, xl, 0], arrived.at[1], sum_sems.at[3], x_last)
+    f32 = jnp.float32
+    landed(relay.at[0], sum_sems.at[0])
+    passed[0] = (part_ref[:, xn, 0].astype(f32) + relay[0].astype(f32)).astype(jnp.bfloat16)
+    send(passed.at[0], arrived.at[2], sum_sems.at[4], x_next)
+    landed(relay.at[1], sum_sems.at[1])
+    passed[1] = (part_ref[:, xl, 1].astype(f32) + relay[1].astype(f32)).astype(jnp.bfloat16)
+    send(passed.at[1], arrived.at[3], sum_sems.at[5], x_last)
+    landed(arrived.at[0], sum_sems.at[2])
+    landed(arrived.at[1], sum_sems.at[3])
+    landed(arrived.at[2], sum_sems.at[4])
+    landed(arrived.at[3], sum_sems.at[5])
+
+    def x_total(y_hi, half):
+        first, second = (2, 1) if half == 0 else (0, 3)
+        return (
+            part_ref[y_hi, x, half].astype(f32)
+            + arrived[first, y_hi].astype(f32)
+            + arrived[second, y_hi].astype(f32)
+        )
+
+    for half in range(2):
+        plane_sum[half] = x_total(1 - y_hi, half).astype(jnp.bfloat16)
+    send(plane_sum, other, sum_sems.at[6], facing)
+    landed(other, sum_sems.at[6])
+    mine = everyone.at[z, y, core]
+    for half in range(2):
+        total = x_total(y_hi, half) + other[half].astype(f32)
+        everyone[z, y, core, half] = total.astype(jnp.bfloat16)
+
+    send(mine, mine, side_sems.at[0], beside)
+    send(mine, mine, side_sems.at[1], sibling)
+    upper = lambda zz: everyone.at[zz, :, core, 0]
+    lower = lambda zz, yy: everyone.at[zz, yy, core, 1]
+    send(lower(z, y), lower(z, y), ring_sems.at[1, 0, 1], z_next)
+    send(lower(z, y), lower(z, y), ring_sems.at[1, 1, 1], z_last)
+    theirs = everyone.at[z, 1 - y, core]
+    landed(theirs, side_sems.at[0])
+    send(upper(z), upper(z), ring_sems.at[0, 0, 1], z_next)
+    send(upper(z), upper(z), ring_sems.at[0, 1, 1], z_last)
+    send(theirs, theirs, side_sems.at[2], sibling)
+
+    longest = {(0, 0): n_z // 2, (0, 1): n_z // 2 - 1, (1, 0): n_z // 2 - 1, (1, 1): n_z // 2}
+
+    def ring_step(step):
+        for half in (1, 0):
+            for way in (0, 1):
+                if step > longest[half, way]:
+                    continue
+                origin = (z + n_z - step) % n_z if way == 0 else (z + step) % n_z
+                piece = upper(origin) if half == 0 else lower(origin, y)
+                landed(piece, ring_sems.at[half, way, step])
+                if step < longest[half, way]:
+                    send(piece, piece, ring_sems.at[half, way, step + 1], z_next if way == 0 else z_last)
+                if half == 1:
+                    send(piece, piece, ring_sems.at[2, way, step], beside)
+                send(piece, piece, ring_sems.at[3 + half, way, step], sibling)
+
+    def side_step(step):
+        for way in (0, 1):
+            if step > longest[1, way]:
+                continue
+            origin = (z + n_z - step) % n_z if way == 0 else (z + step) % n_z
+            piece = lower(origin, 1 - y)
+            landed(piece, ring_sems.at[2, way, step])
+            send(piece, piece, ring_sems.at[5, way, step], sibling)
+
+    def rest_step(step):
+        if step == 0:
+            for yy, spot in ((y, 1), (1 - y, 2)):
+                landed(everyone.at[z, yy, 1 - core], side_sems.at[spot])
+            return
+        for way in (0, 1):
+            origin = (z + n_z - step) % n_z if way == 0 else (z + step) % n_z
+            if step <= longest[0, way]:
+                landed(everyone.at[origin, :, 1 - core, 0], ring_sems.at[3, way, step])
+            if step <= longest[1, way]:
+                landed(everyone.at[origin, y, 1 - core, 1], ring_sems.at[4, way, step])
+                landed(everyone.at[origin, 1 - y, 1 - core, 1], ring_sems.at[5, way, step])
+
+    dx = (x + 4 - z % 4) % 4
+    root = z // 4 == y_hi
+    first = core * quarter
+    eighth = quarter // 2
+
+    def group_origins(step):
+        if step == 0:
+            return ((z, 0),)
+        if step == n_z // 2:
+            return (((z + step) % n_z, step),)
+        return (((z + n_z - step) % n_z, step), ((z + step) % n_z, n_z - step))
+
+    held = lambda zz, part: left.at[zz, :, :, pl.ds(part * eighth, eighth)]
+    late = []
+
+    def left_step(step):
+        for zz, tag in group_origins(step):
+            base = len(sends)
+
+            def numbered(source, target, arrival, device, offset):
+                return pltpu.make_async_remote_copy(
+                    src_ref=source, dst_ref=target, send_sem=send_sems.at[base + offset],
+                    recv_sem=arrival, device_id=device, device_id_type=pl.DeviceIdType.MESH,
+                )
+
+            rows_at = lambda half, start, count: everyone.at[zz, :, :, half, pl.ds(start, count)]
+            to_next = numbered(held(zz, 0), held(zz, 0), left_sems.at[0, tag], x_next, 0)
+            to_last = numbered(held(zz, 1), held(zz, 1), left_sems.at[1, tag], x_last, 1)
+            to_across = numbered(
+                rows_at(1 - y, first, quarter), left.at[zz], left_sems.at[2, tag], across, 2
+            )
+
+            @pl.when(dx == 0)
+            def _():
+                @pl.when(root)
+                def _():
+                    to_across.start()
+                    left[zz] = everyone[zz, :, :, y, pl.ds(first, quarter)]
+
+                @pl.when(jnp.logical_not(root))
+                def _():
+                    landed(left.at[zz], left_sems.at[2, tag])
+
+                to_next.start()
+                to_last.start()
+
+            @pl.when((dx == 1) | (dx == 2))
+            def _():
+                landed(held(zz, 0), left_sems.at[0, tag])
+                to_next.start()
+
+            @pl.when((dx == 3) | (dx == 2))
+            def _():
+                landed(held(zz, 1), left_sems.at[1, tag])
+                to_last.start()
+
+            late.append((zz, tag, to_next, to_last, to_across))
+            sends.extend([None] * 3)
+
+    def left_end():
+        for zz, tag, to_next, to_last, to_across in late:
+            pl.when(dx == 1)(lambda: landed(held(zz, 1), left_sems.at[1, tag]))
+            pl.when(dx == 3)(lambda: landed(held(zz, 0), left_sems.at[0, tag]))
+
+    rest_step(0)
+    ring_step(1)
+    left_step(0)
+    ring_step(2)
+    side_step(1)
+    rest_step(1)
+    left_step(1)
+    ring_step(3)
+    side_step(2)
+    rest_step(2)
+    left_step(2)
+    ring_step(4)
+    side_step(3)
+    rest_step(3)
+    left_step(3)
+    side_step(4)
+    rest_step(4)
+    left_step(4)
+    left_end()
+
+    def joined(value):
+        return jnp.concatenate([value[0, 0], value[0, 1], value[1, 0], value[1, 1]], axis=1)
+
+    def group_product(zz, carry):
+        straight = [left[zz, i // 2, i % 2].astype(f32) for i in range(4)]
+        side = jnp.concatenate([turned(value) for value in straight], axis=1)
+        both = jnp.concatenate([-jnp.concatenate(straight, axis=1), side], axis=0)
+        both = both.astype(jnp.bfloat16)
+        for half in range(2):
+            right = jnp.concatenate([everyone[zz, i // 2, i % 2, half] for i in range(4)], axis=1)
+            product = lax.dot_general(
+                both, right, (((1,), (1,)), ((), ())), preferred_element_type=f32
+            )
+            for part in range(2):
+                spot = (part, slice(None), slice(half * half_rows, (half + 1) * half_rows))
+                out_ref[spot] += product[part * quarter : (part + 1) * quarter]
+        return carry
+
+    out_ref[...] = jnp.zeros_like(out_ref)
+    lax.fori_loop(0, n_z, group_product, 0)
+
+    for moving in sends:
+        if moving is not None:
+            moving.wait_send()
+    for zz, tag, to_next, to_last, to_across in late:
+        pl.when(dx != 3)(lambda: to_next.wait_send())
+        pl.when(dx != 1)(lambda: to_last.wait_send())
+        pl.when((dx == 0) & root)(lambda: to_across.wait_send())
+
+
+def shared_response(partial_sums, n_z):
+    rows = partial_sums.shape[0] // 8
+    half = rows // 2
+    bf16 = jnp.bfloat16
+    part = partial_sums.reshape(2, 4, 2, half, LANES)
+    return pl.pallas_call(
+        functools.partial(share_kernel, rows),
+        out_shape=jax.ShapeDtypeStruct((2, rows // 4, rows), jnp.float32),
+        in_specs=[pl.BlockSpec(memory_space=pltpu.VMEM)],
+        out_specs=pl.BlockSpec(memory_space=pltpu.VMEM),
+        scratch_shapes=[
+            pltpu.VMEM((n_z, 2, 2, 2, half, LANES), bf16),
+            pltpu.VMEM((n_z, 2, 2, rows // 4, LANES), bf16),
+            pltpu.VMEM((2, 2, half, LANES), bf16),
+            pltpu.VMEM((2, 2, half, LANES), bf16),
+            pltpu.VMEM((4, 2, half, LANES), bf16),
+            pltpu.VMEM((2, half, LANES), bf16),
+            pltpu.VMEM((2, half, LANES), bf16),
+            pltpu.SemaphoreType.DMA((128,)),
+            pltpu.SemaphoreType.DMA((8,)),
+            pltpu.SemaphoreType.DMA((6, 2, n_z // 2 + 1)),
+            pltpu.SemaphoreType.DMA((3,)),
+            pltpu.SemaphoreType.DMA((3, n_z)),
+        ],
+        compiler_params=pltpu.CompilerParams(
+            collective_id=0, has_side_effects=True, vmem_limit_bytes=40 * 2**20
+        ),
+        cost_estimate=pl.CostEstimate(
+            flops=1_100_000_000, bytes_accessed=2_000_000, transcendentals=0
+        ),
+    )(part)
+
+
 def from_ahead(value, axis, steps):
     count = lax.axis_size(axis)
     pairs = [((target + steps) % count, target) for target in range(count)]
@@ -216,18 +485,8 @@
     index, sign = wave_index(gvectors)
     xytab = lax.dynamic_index_in_dim(xytabs, lax.axis_index("pw"), 0, keepdims=False)
     partial_sums = partial_density(index, emp, near, far, ztab, xytab, sign, scale)
-    rho = lax.psum_scatter(partial_sums, "pw", scatter_dimension=0, tiled=True)
-    rho = rho.astype(jnp.bfloat16)
-    right = lax.all_gather(rho, "blk", axis=1, tiled=True)
-    column = lax.all_gather(rho, "pw", axis=0, tiled=True)
-    left = lax.all_to_all(column, "blk", split_axis=0, concat_axis=1, tiled=True)
-    parts = left.reshape(left.shape[0], -1, 2, 8)
-    side = jnp.stack([-parts[:, :, 1], parts[:, :, 0]], axis=2).reshape(left.shape)
-    both = jnp.stack([left, side], axis=1).reshape(-1, left.shape[1])
-    product = lax.dot_general(
-        -both, right, (((1,), (1,)), ((), ())), preferred_element_type=jnp.float32
-    )
-    return product.reshape(left.shape[0], 2, -1)
+    n_z = lax.axis_size("blk") // 4
+    return jnp.transpose(shared_response(partial_sums, n_z), (1, 0, 2))
 
 
 def solution(mesh):

time: 345 us -> 184 us (0.53)
  waiting for transfers between devices: 206 us -> 40.1 us
  Pallas kernels: 42.1 us -> 119 us
  blocking collectives: 42.6 us -> 0 us
  between operations: 13.1 us -> 0.03 us
  local copies, waits for them, and re-layouts: 21.8 us -> 16.3 us
  other arithmetic: 4.96 us -> 0.84 us
  matrix products: 4.11 us -> 0 us
    all_gather x2 -> x0, waiting for transfers between devices: 87.3 us -> none  [the longest x1 52 us: shards(): column = lax.all_gather(rho, 'pw', axis=0, tiled=True)]
    reduce_scatter x1 -> x0, waiting for transfers between devices: 77.5 us -> none  [shards(): rho = lax.psum_scatter(partial_sums, 'pw', scatter_dimension=0, tiled=True)]
    pallas_call x0 -> x1, Pallas kernels: none -> 77.1 us  [shared_response(): pl.pallas_call(functools.partial(share_kernel, rows), out_shape=jax.Shape...]
    all_to_all x1 -> x0, blocking collectives: 42.6 us -> none  [shards(): lax.all_to_all(column, 'blk', split_axis=0, concat_axis=1, tiled=True)]
    another operation x2 -> x0, local copies, waits for them, and re-layouts: 4.55 us -> none  [shards(): both = jnp.stack([left, side], axis=1).reshape(-1, left.shape[1])]
    dot_general x1 -> x0, matrix products: 4.11 us -> none  [shards(): lax.dot_general(-both, right, (((1,), (1,)), ((), ())), preferred_element...]
  transfers between devices with their start and end apart: 7 -> 4, of which waited for: 5 -> 2; matrix products, arithmetic and copies ran while one was open for 7% -> 8% of each run, Pallas kernels for 0% -> 0%
where the time goes in v2:
time: 184 us
  Pallas kernels  119 us (65%)
  waiting for transfers between devices  40.1 us (22%)
  local copies, waits for them, and re-layouts  16.3 us (9%)
  starting transfers between devices  7.9 us (4%)
    pallas_call x1, Pallas kernels, shared_response(): pl.pallas_call(functools.partial(share_kernel, rows), out_shape=jax.Shape...  77.1 us
    pallas_call x1, Pallas kernels, partial_density(): pl.pallas_call(density_kernel, grid=(PLANES,), out_shape=jax.ShapeDtypeSt...  41.7 us
    ppermute x4, waiting for transfers between devices, from_ahead(): return lax.ppermute(value, axis, pairs)  40.1 us
    ppermute x4, starting transfers between devices, from_ahead(): return lax.ppermute(value, axis, pairs)  7.9 us
    reshape x2, local copies, waits for them, and re-layouts, plane_rows(): return moved.reshape(moved.shape[0], -1, moved.shape[3])  5.23 us
  transfers between devices with their start and end apart: 4, of which 2 were waited for; matrix products, arithmetic and copies ran while one was open for 8% of the time, Pallas kernels for 0%

profile of v2, /device:TPU:26, one launch (start us, length us, event | category | flops | bytes accessed | tf_op | source)
XLA Modules:
  0.0 184.0 jit_solution(8780082502816942106)
XLA Ops:
  0.0 0.0 copy-start
  0.0 0.7 collective-permute-start.3
  0.7 5.7 %collective-permute-start.2 = (bf16[4]{0:T(256)(128)(2,1)}, bf16[4]{0:T(256)(128)(2,1)S(1)}, u32[]{:S(2)}, u32[]{:S(2)}) collective-permute-start(bf16[4]{0:T(256)(128)(2,1)} %param.9), channel_id=1, source_target_pairs={{8,0},{16,8},{24,16},{32,24},{40,32},{48,40},{56,48},{64,56},{72,6... | collective-permute-start | bytes 32 | tf_op jit(solution)/shard_map/ppermute | solution.py:454
  6.5 0.0 copy-start.3
  6.5 0.0 copy-start.2
  6.5 3.1 %copy.12 = bf16[9,2,4,10368]{3,2,1,0:T(4,128)(2,1)} copy(bf16[9,2,4,10368]{3,2,0,1:T(4,128)(2,1)} %bitcast.15) | data formatting | bytes 2985984 | tf_op jit(solution)/shard_map/transpose | solution.py:458
  9.6 3.4 %reshape.98 = bf16[9,8,10368]{2,1,0:T(8,128)(2,1)} reshape(bf16[9,2,4,10368]{3,2,1,0:T(4,128)(2,1)} %copy.12) | data formatting | bytes 2985984 | tf_op jit(solution)/shard_map/reshape | solution.py:459
  13.0 0.8 collective-permute-start.1
  13.8 0.6 collective-permute-start
  14.4 0.0 copy-done.3
  14.4 0.0 copy-done.2
  14.4 2.0 %copy.13.sign_ref = f32[4096,1]{1,0:T(8,128)} copy(f32[4096,1]{0,1:T(1,128)S(1)} %get-tuple-element.5) | data formatting | bytes 32768 | tf_op jit(solution)/shard_map/jit(_where)/select_n | solution.py:475
  16.5 0.0 copy-done
  16.5 1.8 copy_bitcast_fusion.emp_ref
  18.3 2.8 %dynamic-slice_bitcast_fusion.xytab_ref = bf16[1104,720]{1,0:T(8,128)(2,1)} fusion(bf16[8,1104,720]{2,1,0:T(8,128)(2,1)} %constant.32.clone, s32[]{:T(128)S(6)} %select_n.18), kind=kLoop, calls=%fused_computation.1 | loop fusion | bytes 3179524 | tf_op jit(solution)/shard_map/jit(dynamic_index_in_dim)/squeeze | solution.py:486
  21.1 0.6 multiply_add_fusion
  21.7 0.0 collective-permute-done.3
  21.8 0.0 collective-permute-done.2
  21.8 0.1 maximum_convert_fusion
  21.8 0.1 divide_sqrt_fusion
  21.9 0.7 reshape.99.scale_ref
  22.6 24.1 %collective-permute-done.1.far_ref = bf16[9,8,10368]{2,1,0:T(8,128)(2,1)} collective-permute-done((bf16[9,8,10368]{2,1,0:T(8,128)(2,1)}, bf16[9,8,10368]{2,1,0:T(8,128)(2,1)}, u32[]{:S(2)}, u32[]{:S(2)}) %collective-permute-start.1) | collective-permute-done | bytes 1493024 | tf_op jit(solution)/shard_map/ppermute | solution.py:454
  46.7 16.0 %collective-permute-done.near_ref = bf16[9,8,10368]{2,1,0:T(8,128)(2,1)} collective-permute-done((bf16[9,8,10368]{2,1,0:T(8,128)(2,1)}, bf16[9,8,10368]{2,1,0:T(8,128)(2,1)}, u32[]{:S(2)}, u32[]{:S(2)}) %collective-permute-start) | collective-permute-done | bytes 1493024 | tf_op jit(solution)/shard_map/ppermute | solution.py:454
  62.7 41.7 %shard_map.73 = bf16[4096,128]{1,0:T(8,128)(2,1)} custom-call(s32[4096]{0:T(1024)} %bitcast.16, bf16[9,16,10368]{2,1,0:T(8,128)(2,1)} %copy_bitcast_fusion.emp_ref, bf16[9,8,10368]{2,1,0:T(8,128)(2,1)} %collective-permute-done.near_ref, bf16[9,8,10368]{2,1,0:T(8,128)(2,1)} %collective-permute-done.1.far_ref, bf16[264,1152]{1,0:T(8,128)(2,1)} %constant.31.clone.ztab_ref, ...), custom_call_target="tpu_custom_call" | custom-call | flops 15000000512 | bytes 12000000 | tf_op jit(solution)/shard_map/pallas_call | solution.py:151
  104.4 0.0 copy-start.1
  104.4 1.2 copy-done.1
  105.6 77.1 %shard_map.74 = f32[2,128,512]{2,1,0:T(8,128)S(1)} custom-call(bf16[2,4,2,256,128]{4,3,2,1,0:T(8,128)(2,1)S(1)} %bitcast.14), custom_call_target="tpu_custom_call" | custom-call | flops 1100000000 | bytes 2000000 | tf_op jit(solution)/shard_map/pallas_call | solution.py:423
  182.8 1.2 copy.14
  (3 shorter events, 0.0 us)
Async XLA Ops:
  0.0 16.5 %copy-start = (bf16[2,8,9,10368]{3,1,2,0:T(8,128)(2,1)S(1)}, bf16[2,8,9,10368]{3,1,2,0:T(8,128)(2,1)}, u32[]{:S(2)}) copy-start(bf16[2,8,9,10368]{3,1,2,0:T(8,128)(2,1)} %param.8) | copy-start | bytes 8957956
  0.0 21.7 %collective-permute-start.3 = (bf16[4]{0:T(256)(128)(2,1)}, bf16[4]{0:T(256)(128)(2,1)S(1)}, u32[]{:S(2)}, u32[]{:S(2)}) collective-permute-start(bf16[4]{0:T(256)(128)(2,1)} %param.9), channel_id=1, source_target_pairs={{16,0},{24,8},{32,16},{40,24},{48,32},{56,40},{64,48},{72,56},{80,... | collective-permute-start | bytes 32 | tf_op jit(solution)/shard_map/ppermute | solution.py:454
  0.7 21.0 %collective-permute-start.2 = (bf16[4]{0:T(256)(128)(2,1)}, bf16[4]{0:T(256)(128)(2,1)S(1)}, u32[]{:S(2)}, u32[]{:S(2)}) collective-permute-start(bf16[4]{0:T(256)(128)(2,1)} %param.9), channel_id=1, source_target_pairs={{8,0},{16,8},{24,16},{32,24},{40,32},{48,40},{56,48},{64,56},{72,6... | collective-permute-start | bytes 32 | tf_op jit(solution)/shard_map/ppermute | solution.py:454
  6.5 7.9 %copy-start.3 = (bf16[8]{0:T(256)(128)(2,1)S(1)}, bf16[8]{0:T(256)(128)(2,1)}, u32[]{:S(2)}) copy-start(bf16[8]{0:T(256)(128)(2,1)} %param.10) | copy-start | bytes 52
  6.5 7.9 %copy-start.2 = (s32[3,4096]{1,0:T(4,128)S(1)}, s32[3,4096]{1,0:T(4,128)}, u32[]{:S(2)}) copy-start(s32[3,4096]{1,0:T(4,128)} %param.11) | copy-start | bytes 147460
  13.0 33.8 %collective-permute-start.1 = (bf16[9,8,10368]{2,1,0:T(8,128)(2,1)}, bf16[9,8,10368]{2,1,0:T(8,128)(2,1)}, u32[]{:S(2)}, u32[]{:S(2)}) collective-permute-start(bf16[9,8,10368]{2,1,0:T(8,128)(2,1)} %reshape.98), channel_id=1, source_target_pairs={{16,0},{24,8},{32,16},{40,24},{48,32},{56,40},{64,48},{72,56},{80,... | collective-permute-start | bytes 4478984 | tf_op jit(solution)/shard_map/ppermute | solution.py:454
  13.8 48.9 %collective-permute-start = (bf16[9,8,10368]{2,1,0:T(8,128)(2,1)}, bf16[9,8,10368]{2,1,0:T(8,128)(2,1)}, u32[]{:S(2)}, u32[]{:S(2)}) collective-permute-start(bf16[9,8,10368]{2,1,0:T(8,128)(2,1)} %reshape.98), channel_id=1, source_target_pairs={{8,0},{16,8},{24,16},{32,24},{40,32},{48,40},{56,48},{64,56},{72,6... | collective-permute-start | bytes 4478984 | tf_op jit(solution)/shard_map/ppermute | solution.py:454
  104.4 1.2 copy-start.1

commit v3 on v2

--- a/solution.py
+++ b/solution.py
@@ -22,9 +22,10 @@
 GROUP_CELLS = 8 * GZ
 Z_ROWS = SIDE * 8
 ROWS_X = 80
-DEPTH = PLANES * ROWS_X
+BATCH = 3
+DEPTH = BATCH * ROWS_X
 HALF = (SIDE * SIDE + 1) // 2
-WAVE_ROWS = 1104
+WAVE_ROWS = 1096
 Q_SLOTS = 34
 LANES = 128
 omega_shift = 0.5
@@ -54,7 +55,8 @@
             steps = (p[:, None] * y[None, :] + a[:, None] * x) % GX
             out[group, 0 : 2 * HALF : 2, plane, :GY] = np.cos(2 * np.pi * steps / GX)
             out[group, 1 : 2 * HALF : 2, plane, :GY] = np.sin(2 * np.pi * steps / GX)
-    return out.reshape(groups, WAVE_ROWS, DEPTH).astype(np.float32).astype(ml_dtypes.bfloat16)
+    out = out.reshape(groups, WAVE_ROWS, PLANES // BATCH, DEPTH).transpose(0, 2, 1, 3)
+    return out.astype(np.float32).astype(ml_dtypes.bfloat16)
 
 
 def turned(value):
@@ -64,21 +66,84 @@
     return jnp.where((lane & 8) == 0, ahead, -behind)
 
 
+MESH = pl.DeviceIdType.MESH
+
+
 def density_kernel(
-    index_ref, emp_ref, near_ref, far_ref, ztab_ref, xytab_ref, sign_ref, scale_ref,
-    out_ref, occ_f, pairs, depth_out, sections, waves, picked,
+    occ_ref, emp_ref, wave_ref, level_ref, ztab_ref, xytab_ref, out_ref,
+    near, far, near_level, far_level, emp, ztab, xytab, occ_f, pairs, depth_out, sections, waves,
+    picked, index_v, index_s, sign_v, ahead_sems, far_sems, pass_sems, near_sems, load_sems,
 ):
-    plane = pl.program_id(0)
-
-    occ_f[0:8, :] = near_ref[0].astype(jnp.float32)
-    occ_f[8:16, :] = far_ref[0].astype(jnp.float32)
-
-    def group_pairs(group, carry):
+    blk, pw = lax.axis_index("blk"), lax.axis_index("pw")
+    count = lax.axis_size("blk")
+    core = blk % 2
+    behind, ahead = {"blk": (blk + count - 2) % count}, {"blk": (blk + 2) % count}
+    sibling = {"blk": blk + 1 - 2 * core}
+    barrier = pltpu.get_barrier_semaphore()
+    for device in (behind, ahead, sibling):
+        pl.semaphore_signal(barrier, inc=1, device_id=device, device_id_type=MESH)
+    pl.semaphore_wait(barrier, 3)
+
+    def to_behind(source, target, spot):
+        return pltpu.make_async_remote_copy(
+            src_ref=source, dst_ref=target, send_sem=ahead_sems.at[spot],
+            recv_sem=far_sems.at[spot], device_id=behind, device_id_type=MESH,
+        )
+
+    def to_sibling(source, target, spot):
+        return pltpu.make_async_remote_copy(
+            src_ref=source, dst_ref=target, send_sem=pass_sems.at[spot],
+            recv_sem=near_sems.at[spot], device_id=sibling, device_id_type=MESH,
+        )
+
+    def landed(target, arrival):
+        pltpu.make_async_copy(target, target, arrival).wait()
+
+    def send_plane(x, carry):
+        to_behind(occ_ref.at[:, x], far.at[x], x).start()
+        return carry
+
+    def pass_plane(x, carry):
+        to_sibling(occ_ref.at[:, x], near.at[x], x).start()
+        return carry
+
+    to_behind(level_ref, far_level, PLANES).start()
+    lax.fori_loop(0, PLANES, send_plane, 0)
+
+    @pl.when(core == 1)
+    def _():
+        to_sibling(level_ref, near_level, PLANES).start()
+        lax.fori_loop(0, PLANES, pass_plane, 0)
+
+    loads = [
+        pltpu.make_async_copy(emp_ref, emp, load_sems.at[0]),
+        pltpu.make_async_copy(ztab_ref, ztab, load_sems.at[1]),
+        pltpu.make_async_copy(xytab_ref.at[pw], xytab, load_sems.at[2]),
+    ]
+    for load in loads:
+        load.start()
+
+    flat = SIDE * wave_ref[1:2, :] + wave_ref[0:1, :]
+    index_v[...] = (wave_ref[2:3, :] + KMAX) * WAVE_ROWS + 2 * jnp.abs(flat)
+    sign_v[...] = jnp.where(flat < 0, -1.0, 1.0).astype(jnp.float32)
+    index_move = pltpu.make_async_copy(index_v, index_s, load_sems.at[3])
+    index_move.start()
+    landed(far_level, far_sems.at[PLANES])
+
+    @pl.when(core == 0)
+    def _():
+        to_sibling(far_level, near_level, PLANES).start()
+
+    for load in loads:
+        load.wait()
+    index_move.wait()
+
+    def group_pairs(x, group):
         for part in range(3):
             start = pl.multiple_of(group * GROUP_CELLS + part * 384, 128)
             cells = pl.ds(start, 384)
-            emp = emp_ref[0, :, cells].astype(jnp.float32)
-            emp_re, emp_im = emp[0:8], emp[8:16]
+            emp_re = emp[0, x, :, cells].astype(jnp.float32)
+            emp_im = emp[1, x, :, cells].astype(jnp.float32)
             for v in range(8):
                 row = v if v < 4 else v + 4
                 occ_re = occ_f[row : row + 1, cells]
@@ -88,95 +153,155 @@
                 )
                 rows = pl.ds(pl.multiple_of(group * LANES + v * 16, 16), 16)
                 pairs[rows, part * 384 : part * 384 + 384] = both.astype(jnp.bfloat16)
-        return carry
-
-    lax.fori_loop(0, GROUPS, group_pairs, 0)
-    depth_out[...] = lax.dot_general(
-        ztab_ref[...], pairs[...], (((1,), (1,)), ((), ())), preferred_element_type=jnp.float32
-    )
-    spot = pl.ds(pl.multiple_of(plane * ROWS_X, 16), ROWS_X)
+
     blank = jnp.zeros((ROWS_X - GY, LANES), jnp.float32)
 
     def rows_of(first):
         parts = [depth_out[first : first + 8, t * LANES : (t + 1) * LANES] for t in range(GROUPS)]
         return jnp.concatenate(parts + [blank], axis=0)
 
-    def put(slot, value):
-        half = slot % 2
-        sections[slot // 2, spot, half * LANES : (half + 1) * LANES] = value.astype(jnp.bfloat16)
-
-    put(KMAX, rows_of(0))
-    for q in range(1, KMAX + 1):
-        cosine = rows_of(q * 8)
-        sine = turned(rows_of((KMAX + q) * 8))
-        put(KMAX + q, cosine + sine)
-        put(KMAX - q, cosine - sine)
-
-    @pl.when(plane == PLANES - 1)
-    def _():
-        sections[Q_SLOTS // 2 - 1, :, LANES:] = jnp.zeros((DEPTH, LANES), jnp.bfloat16)
+    def one_plane(x, spot):
+        landed(far.at[x], far_sems.at[x])
+
+        @pl.when(core == 0)
+        def _():
+            to_sibling(far.at[x], near.at[x], x).start()
+
+        landed(near.at[x], near_sems.at[x])
+        for part in range(2):
+            occ_f[part * 4 : part * 4 + 4, :] = near[x, part].astype(jnp.float32)
+            occ_f[part * 4 + 8 : part * 4 + 12, :] = far[x, part].astype(jnp.float32)
+
+        def each_group(group, carry):
+            group_pairs(x, group)
+            return carry
+
+        lax.fori_loop(0, GROUPS, each_group, 0)
+        depth_out[...] = lax.dot_general(
+            ztab[...], pairs[...], (((1,), (1,)), ((), ())), preferred_element_type=jnp.float32
+        )
+        rows = pl.ds(pl.multiple_of(spot * ROWS_X, 16), ROWS_X)
+
+        def put(slot, value):
+            half = slot % 2
+            sections[slot // 2, rows, half * LANES : (half + 1) * LANES] = value.astype(jnp.bfloat16)
+
+        put(KMAX, rows_of(0))
+        for q in range(1, KMAX + 1):
+            cosine = rows_of(q * 8)
+            sine = turned(rows_of((KMAX + q) * 8))
+            put(KMAX + q, cosine + sine)
+            put(KMAX - q, cosine - sine)
+
+    sections[Q_SLOTS // 2 - 1, :, LANES:] = jnp.zeros((DEPTH, LANES), jnp.bfloat16)
+    for batch in range(PLANES // BATCH):
+
+        def each_plane(spot, carry):
+            one_plane(batch * BATCH + spot, spot)
+            return carry
+
+        lax.fori_loop(0, BATCH, each_plane, 0)
 
         def slot_pair(k, carry):
-            product = jnp.dot(xytab_ref[...], sections[k], preferred_element_type=jnp.float32)
-            first = pl.multiple_of(k * 2 * WAVE_ROWS, 16)
-            waves[pl.ds(first, WAVE_ROWS), :] = product[:, :LANES]
-            waves[pl.ds(first + WAVE_ROWS, WAVE_ROWS), :] = product[:, LANES:]
+            product = jnp.dot(xytab[batch], sections[k], preferred_element_type=jnp.float32)
+            first = pl.multiple_of(k * 2 * WAVE_ROWS, 8)
+            for half in range(2):
+                rows = pl.ds(first + half * WAVE_ROWS, WAVE_ROWS)
+                value = product[:, half * LANES : (half + 1) * LANES]
+                waves[rows, :] = value if batch == 0 else waves[rows, :] + value
             return carry
 
         lax.fori_loop(0, Q_SLOTS // 2, slot_pair, 0)
 
+    landed(near_level, near_sems.at[PLANES])
+    lane = lax.broadcasted_iota(jnp.int32, (1, LANES), 1)
+    occ_level = jnp.where(lane < LANES // 2, near_level[0:1, :], far_level[0:1, :])
+    scale = jnp.sqrt(2.0 / (level_ref[1:2, :] - occ_level + omega_shift))
+
+    def chunk(w, carry):
         def pick(step, carry):
             first = step * 16
             for i in range(16):
-                picked[pl.ds((first + i) * 2, 2), :] = waves[pl.ds(index_ref[first + i], 2), :]
+                row = index_s[0, w * 512 + first + i]
+                picked[pl.ds((first + i) * 2, 2), :] = waves[pl.ds(row, 2), :]
             return carry
 
-        lax.fori_loop(0, NG // 16, pick, 0)
-
-        def finish(step, carry):
-            first = step * 128
-            cosine = picked[pl.ds(first * 2, 128, stride=2), :]
-            sine = picked[pl.ds(first * 2 + 1, 128, stride=2), :]
-            rows = pl.ds(pl.multiple_of(first, 128), 128)
-            total = (cosine + sign_ref[rows, :] * turned(sine)) * scale_ref[...]
-            out_ref[rows, :] = total.astype(out_ref.dtype)
-            return carry
-
-        lax.fori_loop(0, NG // 128, finish, 0)
-
-
-def partial_density(index, emp, near, far, ztab, xytab, sign, scale, interpret=False):
-    whole = lambda *shape: pl.BlockSpec(shape, lambda i: (0,) * len(shape))
-    plane = lambda rows: pl.BlockSpec((1, rows, CELLS), lambda i: (i, 0, 0))
+        lax.fori_loop(0, 32, pick, 0)
+        for part in range(4):
+            cosine = picked[pl.ds(part * 256, 128, stride=2), :]
+            sine = picked[pl.ds(part * 256 + 1, 128, stride=2), :]
+            first = pl.multiple_of(w * 512 + part * 128, 128)
+            sign = jnp.broadcast_to(sign_v[:, pl.ds(first, 128)], (128, LANES)).T
+            total = (cosine + sign * turned(sine)) * scale
+            out_ref[pl.ds(first, 128), :] = total.astype(out_ref.dtype)
+        return carry
+
+    lax.fori_loop(0, NG // 512, chunk, 0)
+
+    def sent_plane(x, carry):
+        to_behind(occ_ref.at[:, x], far.at[x], x).wait_send()
+        return carry
+
+    def passed_plane(x, carry):
+        to_sibling(occ_ref.at[:, x], near.at[x], x).wait_send()
+        return carry
+
+    def passed_far(x, carry):
+        to_sibling(far.at[x], near.at[x], x).wait_send()
+        return carry
+
+    to_behind(level_ref, far_level, PLANES).wait_send()
+    lax.fori_loop(0, PLANES, sent_plane, 0)
+
+    @pl.when(core == 1)
+    def _():
+        to_sibling(level_ref, near_level, PLANES).wait_send()
+        lax.fori_loop(0, PLANES, passed_plane, 0)
+
+    @pl.when(core == 0)
+    def _():
+        to_sibling(far_level, near_level, PLANES).wait_send()
+        lax.fori_loop(0, PLANES, passed_far, 0)
+
+
+def partial_density(occ, emp, gvectors, levels, ztab, xytabs):
+    bf16, f32 = jnp.bfloat16, jnp.float32
+    anywhere, vmem = pl.BlockSpec(memory_space=pl.ANY), pl.BlockSpec(memory_space=pltpu.VMEM)
     return pl.pallas_call(
         density_kernel,
-        grid=(PLANES,),
-        out_shape=jax.ShapeDtypeStruct((NG, LANES), jnp.bfloat16),
-        in_specs=[
-            pl.BlockSpec(memory_space=pltpu.SMEM),
-            plane(16),
-            plane(8),
-            plane(8),
-            whole(Z_ROWS, GROUP_CELLS),
-            whole(WAVE_ROWS, DEPTH),
-            whole(NG, 1),
-            whole(1, LANES),
+        out_shape=jax.ShapeDtypeStruct((NG, LANES), bf16),
+        in_specs=[anywhere, anywhere, vmem, vmem, anywhere, anywhere],
+        out_specs=vmem,
+        scratch_shapes=[
+            pltpu.VMEM((PLANES, 2, 4, CELLS), bf16),
+            pltpu.VMEM((PLANES, 2, 4, CELLS), bf16),
+            pltpu.VMEM((8, LANES), f32),
+            pltpu.VMEM((8, LANES), f32),
+            pltpu.VMEM((2, PLANES, 8, CELLS), bf16),
+            pltpu.VMEM((Z_ROWS, GROUP_CELLS), bf16),
+            pltpu.VMEM((PLANES // BATCH, WAVE_ROWS, DEPTH), bf16),
+            pltpu.VMEM((16, CELLS), f32),
+            pltpu.VMEM((GROUPS * LANES, GROUP_CELLS), bf16),
+            pltpu.VMEM((Z_ROWS, GROUPS * LANES), f32),
+            pltpu.VMEM((Q_SLOTS // 2, DEPTH, 2 * LANES), bf16),
+            pltpu.VMEM((Q_SLOTS * WAVE_ROWS, LANES), f32),
+            pltpu.VMEM((1024, LANES), f32),
+            pltpu.VMEM((1, NG), jnp.int32),
+            pltpu.SMEM((1, NG), jnp.int32),
+            pltpu.VMEM((1, NG), f32),
+            pltpu.SemaphoreType.DMA((PLANES + 1,)),
+            pltpu.SemaphoreType.DMA((PLANES + 1,)),
+            pltpu.SemaphoreType.DMA((PLANES + 1,)),
+            pltpu.SemaphoreType.DMA((PLANES + 1,)),
+            pltpu.SemaphoreType.DMA((4,)),
         ],
-        out_specs=whole(NG, LANES),
-        scratch_shapes=[
-            pltpu.VMEM((16, CELLS), jnp.float32),
-            pltpu.VMEM((GROUPS * LANES, GROUP_CELLS), jnp.bfloat16),
-            pltpu.VMEM((Z_ROWS, GROUPS * LANES), jnp.float32),
-            pltpu.VMEM((Q_SLOTS // 2, DEPTH, 2 * LANES), jnp.bfloat16),
-            pltpu.VMEM((Q_SLOTS * WAVE_ROWS, LANES), jnp.float32),
-            pltpu.VMEM((2 * NG, LANES), jnp.float32),
-        ],
-        compiler_params=pltpu.CompilerParams(vmem_limit_bytes=60 * 2**20),
+        compiler_params=pltpu.CompilerParams(
+            collective_id=1, has_side_effects=True, vmem_limit_bytes=60 * 2**20
+        ),
         cost_estimate=pl.CostEstimate(
             flops=15_000_000_000, bytes_accessed=12_000_000, transcendentals=0
         ),
-        interpret=interpret,
-    )(index, emp, near, far, ztab, xytab, sign, scale)
+    )(occ, emp, gvectors, levels, ztab, xytabs)
 
 
 def share_kernel(rows, part_ref, out_ref, everyone, left, relay, passed, arrived, plane_sum, other,
@@ -448,43 +573,18 @@
     )(part)
 
 
-def from_ahead(value, axis, steps):
-    count = lax.axis_size(axis)
-    pairs = [((target + steps) % count, target) for target in range(count)]
-    return lax.ppermute(value, axis, pairs)
-
-
-def plane_rows(states):
-    moved = jnp.transpose(states, (2, 0, 1, 3))
-    return moved.reshape(moved.shape[0], -1, moved.shape[3])
-
-
-def pair_scale(occ_levels, emp_level):
-    gap = (
-        emp_level.astype(jnp.float32)[None, :]
-        - occ_levels.astype(jnp.float32)[:, None]
-        + omega_shift
-    )
-    root = jnp.sqrt(2.0 / gap)
-    return jnp.broadcast_to(root[:, None, :], (8, 2, 8)).reshape(1, LANES)
-
-
-def wave_index(gvectors):
-    flat = SIDE * gvectors[1] + gvectors[0]
-    index = (gvectors[2] + KMAX) * WAVE_ROWS + 2 * jnp.abs(flat)
-    sign = jnp.where(flat < 0, -1.0, 1.0).astype(jnp.float32)
-    return index, sign[:, None]
+def lane_levels(occ_energy, empty_energy):
+    occ = jnp.broadcast_to(occ_energy.astype(jnp.float32)[None, :, None], (2, 4, 16))
+    emp = jnp.broadcast_to(empty_energy.astype(jnp.float32)[None, :], (16, 8))
+    rows = jnp.stack([occ.reshape(LANES), emp.reshape(LANES)])
+    return jnp.concatenate([rows, jnp.zeros((6, LANES), jnp.float32)])
 
 
 def shards(ztab, xytabs, occupied_states, empty_states, occ_energy, empty_energy, gvectors):
-    occ = plane_rows(occupied_states)
-    emp = plane_rows(empty_states)
-    near, near_level = from_ahead(occ, "blk", 1), from_ahead(occ_energy, "blk", 1)
-    far, far_level = from_ahead(occ, "blk", 2), from_ahead(occ_energy, "blk", 2)
-    scale = pair_scale(jnp.concatenate([near_level, far_level]), empty_energy)
-    index, sign = wave_index(gvectors)
-    xytab = lax.dynamic_index_in_dim(xytabs, lax.axis_index("pw"), 0, keepdims=False)
-    partial_sums = partial_density(index, emp, near, far, ztab, xytab, sign, scale)
+    occ = jnp.transpose(occupied_states, (0, 2, 1, 3))
+    emp = jnp.transpose(empty_states, (0, 2, 1, 3))
+    levels = lane_levels(occ_energy, empty_energy)
+    partial_sums = partial_density(occ, emp, gvectors, levels, ztab, xytabs)
     n_z = lax.axis_size("blk") // 4
     return jnp.transpose(shared_response(partial_sums, n_z), (1, 0, 2))
 

time: 184 us -> 144 us (0.78)
  waiting for transfers between devices: 40.1 us -> 0 us
  Pallas kernels: 119 us -> 139 us
  local copies, waits for them, and re-layouts: 16.3 us -> 4.05 us
  starting transfers between devices: 7.9 us -> 0 us
    ppermute x4 -> x0, waiting for transfers between devices: 40.1 us -> none  [from_ahead(): return lax.ppermute(value, axis, pairs)]
    pallas_call x1, Pallas kernels: 41.7 us -> 56.2 us  [partial_density(): pl.pallas_call(density_kernel, out_shape=jax.ShapeDtypeStruct((NG, LANES)...]
    ppermute x4 -> x0, starting transfers between devices: 7.9 us -> none  [from_ahead(): return lax.ppermute(value, axis, pairs)]
    pallas_call x1, Pallas kernels: 77.1 us -> 83.2 us  [shared_response(): pl.pallas_call(functools.partial(share_kernel, rows), out_shape=jax.Shape...]
    reshape x3 -> x0, local copies, waits for them, and re-layouts: 5.92 us -> none  [the longest x2 5.23 us: plane_rows(): return moved.reshape(moved.shape[0], -1, moved.shape[3])]
    transpose x1 -> x0, local copies, waits for them, and re-layouts: 3.07 us -> none  [plane_rows(): moved = jnp.transpose(states, (2, 0, 1, 3))]
    squeeze x1 -> x0, local copies, waits for them, and re-layouts: 2.82 us -> none  [shards(): lax.dynamic_index_in_dim(xytabs, lax.axis_index('pw'), 0, keepdims=False)]
    select_n x1 -> x0, local copies, waits for them, and re-layouts: 2.02 us -> none  [wave_index(): sign = jnp.where(flat < 0, -1.0, 1.0).astype(jnp.float32)]
  transfers between devices with their start and end apart: 4 -> 0, of which waited for: 2 -> 0; matrix products, arithmetic and copies ran while one was open for 8% -> 0% of each run, Pallas kernels for 0% -> 0%
where the time goes in v3:
time: 144 us
  Pallas kernels  139 us (97%)
  local copies, waits for them, and re-layouts  4.05 us (3%)
    pallas_call x1, Pallas kernels, shared_response(): pl.pallas_call(functools.partial(share_kernel, rows), out_shape=jax.Shape...  83.2 us
    pallas_call x1, Pallas kernels, partial_density(): pl.pallas_call(density_kernel, out_shape=jax.ShapeDtypeStruct((NG, LANES)...  56.2 us

profile of v3, /device:TPU:26, one launch (start us, length us, event | category | flops | bytes accessed | tf_op | source)
XLA Modules:
  0.0 144.1 jit_solution(6801528348666955096)
XLA Ops:
  0.0 0.1 pad.2.clone
  0.1 0.7 broadcast_in_dim.6
  0.8 0.1 stack_reshape.6
  0.9 0.7 broadcast_in_dim.7
  1.6 0.1 stack_reshape.7
  1.6 0.7 maximum_maximum_fusion.level_ref
  2.3 56.2 %shard_map.73 = bf16[4096,128]{1,0:T(8,128)(2,1)} custom-call(bf16[2,9,4,10368]{3,2,1,0:T(4,128)(2,1)} %bitcast.7, bf16[2,9,8,10368]{3,2,1,0:T(8,128)(2,1)} %bitcast.6, s32[3,4096]{1,0:T(4,128)} %wave_ref.1, f32[8,128]{1,0:T(8,128)} %maximum_maximum_fusion.level_ref, bf16[264,1152]{1,0:T(8,128)(2,1)} %constant.6.clone.ztab_ref, ...), custom_call_target="tpu_custom_call" | custom-call | flops 15000000512 | bytes 12000000 | tf_op jit(solution)/shard_map/pallas_call | solution.py:270
  58.5 0.0 copy-start
  58.5 1.2 copy-done
  59.7 83.2 %shard_map.74 = f32[2,128,512]{2,1,0:T(8,128)S(1)} custom-call(bf16[2,4,2,256,128]{4,3,2,1,0:T(8,128)(2,1)S(1)} %bitcast.5), custom_call_target="tpu_custom_call" | custom-call | flops 1100000000 | bytes 2000000 | tf_op jit(solution)/shard_map/pallas_call | solution.py:548
  142.9 1.2 copy.9
  (1 shorter events, 0.0 us)
Async XLA Ops:
  58.5 1.2 copy-start

commit v4 on v3

--- a/solution.py
+++ b/solution.py
@@ -1,4 +1,3 @@
-import functools
 import math
 
 import jax
@@ -69,20 +68,37 @@
 MESH = pl.DeviceIdType.MESH
 
 
-def density_kernel(
-    occ_ref, emp_ref, wave_ref, level_ref, ztab_ref, xytab_ref, out_ref,
-    near, far, near_level, far_level, emp, ztab, xytab, occ_f, pairs, depth_out, sections, waves,
-    picked, index_v, index_s, sign_v, ahead_sems, far_sems, pass_sems, near_sems, load_sems,
+def response_kernel(
+    occ_ref, emp_ref, wave_ref, occ_energy_ref, emp_energy_ref, ztab_ref, xytab_ref, out_ref,
+    near, far, level_ref, near_level, far_level, emp, ztab, xytab, occ_f, pairs, depth_out, sections, waves,
+    picked, index_v, index_s, sign_v, part_ref, everyone, left, relay, passed, arrived, plane_sum,
+    other, ahead_sems, far_sems, pass_sems, near_sems, load_sems, send_sems, sum_sems, ring_sems,
+    side_sems, left_sems,
 ):
     blk, pw = lax.axis_index("blk"), lax.axis_index("pw")
     count = lax.axis_size("blk")
-    core = blk % 2
-    behind, ahead = {"blk": (blk + count - 2) % count}, {"blk": (blk + 2) % count}
-    sibling = {"blk": blk + 1 - 2 * core}
+    n_z = count // 4
+    z, y, core = blk // 4, (blk // 2) % 2, blk % 2
+    x, y_hi = pw % 4, pw // 4
+    f32, bf16 = jnp.float32, jnp.bfloat16
+
+    def place(z=z, y=y, core=core, x=x, y_hi=y_hi):
+        return {"blk": z * 4 + y * 2 + core, "pw": y_hi * 4 + x}
+
+    x_next, x_last = place(x=(x + 1) % 4), place(x=(x + 3) % 4)
+    z_next, z_last = place(z=(z + 1) % n_z), place(z=(z + n_z - 1) % n_z)
+    sibling, beside = place(core=1 - core), place(y=1 - y)
+    facing, across = place(y_hi=1 - y_hi), place(y=1 - y, y_hi=1 - y_hi)
+    behind = {"blk": (blk + count - 2) % count, "pw": pw}
+    ahead = {"blk": (blk + 2) % count, "pw": pw}
+
     barrier = pltpu.get_barrier_semaphore()
-    for device in (behind, ahead, sibling):
+    neighbours = (
+        x_next, x_last, z_next, z_last, sibling, beside, facing, across, behind, ahead
+    )
+    for device in neighbours:
         pl.semaphore_signal(barrier, inc=1, device_id=device, device_id_type=MESH)
-    pl.semaphore_wait(barrier, 3)
+    pl.semaphore_wait(barrier, len(neighbours))
 
     def to_behind(source, target, spot):
         return pltpu.make_async_remote_copy(
@@ -107,8 +123,18 @@
         to_sibling(occ_ref.at[:, x], near.at[x], x).start()
         return carry
 
+    lax.fori_loop(0, PLANES, send_plane, 0)
+    lane = lax.broadcasted_iota(jnp.int32, (8, LANES), 1)
+    occ_energy = occ_energy_ref[...].astype(f32)
+    emp_energy = emp_energy_ref[...].astype(f32)
+    spread = jnp.zeros((8, LANES), f32)
+    for v in range(4):
+        spread = jnp.where((lane // 16) % 4 == v, occ_energy[:, v : v + 1], spread)
+    level_ref[...] = spread
+    emp_level = jnp.zeros((8, LANES), f32)
+    for c in range(8):
+        emp_level = jnp.where(lane % 8 == c, emp_energy[:, c : c + 1], emp_level)
     to_behind(level_ref, far_level, PLANES).start()
-    lax.fori_loop(0, PLANES, send_plane, 0)
 
     @pl.when(core == 1)
     def _():
@@ -214,15 +240,16 @@
         lax.fori_loop(0, Q_SLOTS // 2, slot_pair, 0)
 
     landed(near_level, near_sems.at[PLANES])
-    lane = lax.broadcasted_iota(jnp.int32, (1, LANES), 1)
-    occ_level = jnp.where(lane < LANES // 2, near_level[0:1, :], far_level[0:1, :])
-    scale = jnp.sqrt(2.0 / (level_ref[1:2, :] - occ_level + omega_shift))
-
-    def chunk(w, carry):
+    occ_level = jnp.where(lane < LANES // 2, near_level[...], far_level[...])
+    scale = jnp.sqrt(2.0 / (emp_level - occ_level + omega_shift))[0:1]
+
+    def chunk(yy, xx):
+        base = (yy * 4 + xx) * 512
+
         def pick(step, carry):
             first = step * 16
             for i in range(16):
-                row = index_s[0, w * 512 + first + i]
+                row = index_s[0, base + first + i]
                 picked[pl.ds((first + i) * 2, 2), :] = waves[pl.ds(row, 2), :]
             return carry
 
@@ -230,102 +257,25 @@
         for part in range(4):
             cosine = picked[pl.ds(part * 256, 128, stride=2), :]
             sine = picked[pl.ds(part * 256 + 1, 128, stride=2), :]
-            first = pl.multiple_of(w * 512 + part * 128, 128)
+            first = pl.multiple_of(base + part * 128, 128)
             sign = jnp.broadcast_to(sign_v[:, pl.ds(first, 128)], (128, LANES)).T
             total = (cosine + sign * turned(sine)) * scale
-            out_ref[pl.ds(first, 128), :] = total.astype(out_ref.dtype)
-        return carry
-
-    lax.fori_loop(0, NG // 512, chunk, 0)
-
-    def sent_plane(x, carry):
-        to_behind(occ_ref.at[:, x], far.at[x], x).wait_send()
-        return carry
-
-    def passed_plane(x, carry):
-        to_sibling(occ_ref.at[:, x], near.at[x], x).wait_send()
-        return carry
-
-    def passed_far(x, carry):
-        to_sibling(far.at[x], near.at[x], x).wait_send()
-        return carry
-
-    to_behind(level_ref, far_level, PLANES).wait_send()
-    lax.fori_loop(0, PLANES, sent_plane, 0)
-
-    @pl.when(core == 1)
-    def _():
-        to_sibling(level_ref, near_level, PLANES).wait_send()
-        lax.fori_loop(0, PLANES, passed_plane, 0)
-
-    @pl.when(core == 0)
-    def _():
-        to_sibling(far_level, near_level, PLANES).wait_send()
-        lax.fori_loop(0, PLANES, passed_far, 0)
-
-
-def partial_density(occ, emp, gvectors, levels, ztab, xytabs):
-    bf16, f32 = jnp.bfloat16, jnp.float32
-    anywhere, vmem = pl.BlockSpec(memory_space=pl.ANY), pl.BlockSpec(memory_space=pltpu.VMEM)
-    return pl.pallas_call(
-        density_kernel,
-        out_shape=jax.ShapeDtypeStruct((NG, LANES), bf16),
-        in_specs=[anywhere, anywhere, vmem, vmem, anywhere, anywhere],
-        out_specs=vmem,
-        scratch_shapes=[
-            pltpu.VMEM((PLANES, 2, 4, CELLS), bf16),
-            pltpu.VMEM((PLANES, 2, 4, CELLS), bf16),
-            pltpu.VMEM((8, LANES), f32),
-            pltpu.VMEM((8, LANES), f32),
-            pltpu.VMEM((2, PLANES, 8, CELLS), bf16),
-            pltpu.VMEM((Z_ROWS, GROUP_CELLS), bf16),
-            pltpu.VMEM((PLANES // BATCH, WAVE_ROWS, DEPTH), bf16),
-            pltpu.VMEM((16, CELLS), f32),
-            pltpu.VMEM((GROUPS * LANES, GROUP_CELLS), bf16),
-            pltpu.VMEM((Z_ROWS, GROUPS * LANES), f32),
-            pltpu.VMEM((Q_SLOTS // 2, DEPTH, 2 * LANES), bf16),
-            pltpu.VMEM((Q_SLOTS * WAVE_ROWS, LANES), f32),
-            pltpu.VMEM((1024, LANES), f32),
-            pltpu.VMEM((1, NG), jnp.int32),
-            pltpu.SMEM((1, NG), jnp.int32),
-            pltpu.VMEM((1, NG), f32),
-            pltpu.SemaphoreType.DMA((PLANES + 1,)),
-            pltpu.SemaphoreType.DMA((PLANES + 1,)),
-            pltpu.SemaphoreType.DMA((PLANES + 1,)),
-            pltpu.SemaphoreType.DMA((PLANES + 1,)),
-            pltpu.SemaphoreType.DMA((4,)),
-        ],
-        compiler_params=pltpu.CompilerParams(
-            collective_id=1, has_side_effects=True, vmem_limit_bytes=60 * 2**20
-        ),
-        cost_estimate=pl.CostEstimate(
-            flops=15_000_000_000, bytes_accessed=12_000_000, transcendentals=0
-        ),
-    )(occ, emp, gvectors, levels, ztab, xytabs)
-
-
-def share_kernel(rows, part_ref, out_ref, everyone, left, relay, passed, arrived, plane_sum, other,
-                 send_sems, sum_sems, ring_sems, side_sems, left_sems):
-    half_rows, quarter = rows // 2, rows // 4
-    blk, pw = lax.axis_index("blk"), lax.axis_index("pw")
-    z, y, core = blk // 4, (blk // 2) % 2, blk % 2
-    x, y_hi = pw % 4, pw // 4
-    n_z = lax.axis_size("blk") // 4
-
-    def place(z=z, y=y, core=core, x=x, y_hi=y_hi):
-        return {"blk": z * 4 + y * 2 + core, "pw": y_hi * 4 + x}
-
-    x_next, x_last = place(x=(x + 1) % 4), place(x=(x + 3) % 4)
-    z_next, z_last = place(z=(z + 1) % n_z), place(z=(z + n_z - 1) % n_z)
-    sibling, beside = place(core=1 - core), place(y=1 - y)
-    facing, across = place(y_hi=1 - y_hi), place(y=1 - y, y_hi=1 - y_hi)
+            rows = slice((part % 2) * 128, (part % 2) * 128 + 128)
+            part_ref[yy, xx, part // 2, rows, :] = total.astype(bf16)
+
+    def both_chunks(xx):
+        def one(yy, carry):
+            chunk(yy, xx)
+            return carry
+
+        lax.fori_loop(0, 2, one, 0)
 
     sends = []
 
     def copy(source, target, arrival, device):
         return pltpu.make_async_remote_copy(
             src_ref=source, dst_ref=target, send_sem=send_sems.at[len(sends)], recv_sem=arrival,
-            device_id=device, device_id_type=pl.DeviceIdType.MESH,
+            device_id=device, device_id_type=MESH,
         )
 
     def send(source, target, arrival, device):
@@ -333,27 +283,25 @@
         moving.start()
         sends.append(moving)
 
-    def landed(target, arrival):
-        pltpu.make_async_copy(target, target, arrival).wait()
-
-    barrier = pltpu.get_barrier_semaphore()
-    neighbours = (x_next, x_last, z_next, z_last, sibling, beside, facing, across)
-    for device in neighbours:
-        pl.semaphore_signal(barrier, inc=1, device_id=device, device_id_type=pl.DeviceIdType.MESH)
-    pl.semaphore_wait(barrier, len(neighbours))
+    out_ref[...] = jnp.zeros_like(out_ref)
+    rows = everyone.shape[4] * 2
+    half_rows, quarter = rows // 2, rows // 4
 
     xn, xl, xo = (x + 1) % 4, (x + 3) % 4, (x + 2) % 4
+    both_chunks(xo)
     send(part_ref.at[:, xo, 0], relay.at[0], sum_sems.at[0], x_next)
     send(part_ref.at[:, xo, 1], relay.at[1], sum_sems.at[1], x_last)
+    both_chunks(xn)
     send(part_ref.at[:, xn, 1], arrived.at[0], sum_sems.at[2], x_next)
+    both_chunks(xl)
     send(part_ref.at[:, xl, 0], arrived.at[1], sum_sems.at[3], x_last)
-    f32 = jnp.float32
     landed(relay.at[0], sum_sems.at[0])
-    passed[0] = (part_ref[:, xn, 0].astype(f32) + relay[0].astype(f32)).astype(jnp.bfloat16)
+    passed[0] = (part_ref[:, xn, 0].astype(f32) + relay[0].astype(f32)).astype(bf16)
     send(passed.at[0], arrived.at[2], sum_sems.at[4], x_next)
     landed(relay.at[1], sum_sems.at[1])
-    passed[1] = (part_ref[:, xl, 1].astype(f32) + relay[1].astype(f32)).astype(jnp.bfloat16)
+    passed[1] = (part_ref[:, xl, 1].astype(f32) + relay[1].astype(f32)).astype(bf16)
     send(passed.at[1], arrived.at[3], sum_sems.at[5], x_last)
+    both_chunks(x)
     landed(arrived.at[0], sum_sems.at[2])
     landed(arrived.at[1], sum_sems.at[3])
     landed(arrived.at[2], sum_sems.at[4])
@@ -368,13 +316,13 @@
         )
 
     for half in range(2):
-        plane_sum[half] = x_total(1 - y_hi, half).astype(jnp.bfloat16)
+        plane_sum[half] = x_total(1 - y_hi, half).astype(bf16)
     send(plane_sum, other, sum_sems.at[6], facing)
     landed(other, sum_sems.at[6])
     mine = everyone.at[z, y, core]
     for half in range(2):
         total = x_total(y_hi, half) + other[half].astype(f32)
-        everyone[z, y, core, half] = total.astype(jnp.bfloat16)
+        everyone[z, y, core, half] = total.astype(bf16)
 
     send(mine, mine, side_sems.at[0], beside)
     send(mine, mine, side_sems.at[1], sibling)
@@ -448,7 +396,7 @@
             def numbered(source, target, arrival, device, offset):
                 return pltpu.make_async_remote_copy(
                     src_ref=source, dst_ref=target, send_sem=send_sems.at[base + offset],
-                    recv_sem=arrival, device_id=device, device_id_type=pl.DeviceIdType.MESH,
+                    recv_sem=arrival, device_id=device, device_id_type=MESH,
                 )
 
             rows_at = lambda half, start, count: everyone.at[zz, :, :, half, pl.ds(start, count)]
@@ -484,11 +432,6 @@
 
             late.append((zz, tag, to_next, to_last, to_across))
             sends.extend([None] * 3)
-
-    def left_end():
-        for zz, tag, to_next, to_last, to_across in late:
-            pl.when(dx == 1)(lambda: landed(held(zz, 1), left_sems.at[1, tag]))
-            pl.when(dx == 3)(lambda: landed(held(zz, 0), left_sems.at[0, tag]))
 
     rest_step(0)
     ring_step(1)
@@ -508,16 +451,24 @@
     side_step(4)
     rest_step(4)
     left_step(4)
-    left_end()
-
-    def joined(value):
-        return jnp.concatenate([value[0, 0], value[0, 1], value[1, 0], value[1, 1]], axis=1)
-
-    def group_product(zz, carry):
+
+    def group_product(k, carry):
+        odd = k % 2
+        tag = (odd * ((k + 1) // 2) + (1 - odd) * (n_z - k // 2)) % n_z
+        zz = (z + n_z - tag) % n_z
+
+        @pl.when(dx == 1)
+        def _():
+            landed(held(zz, 1), left_sems.at[1, tag])
+
+        @pl.when(dx == 3)
+        def _():
+            landed(held(zz, 0), left_sems.at[0, tag])
+
         straight = [left[zz, i // 2, i % 2].astype(f32) for i in range(4)]
         side = jnp.concatenate([turned(value) for value in straight], axis=1)
         both = jnp.concatenate([-jnp.concatenate(straight, axis=1), side], axis=0)
-        both = both.astype(jnp.bfloat16)
+        both = both.astype(bf16)
         for half in range(2):
             right = jnp.concatenate([everyone[zz, i // 2, i % 2, half] for i in range(4)], axis=1)
             product = lax.dot_general(
@@ -528,7 +479,6 @@
                 out_ref[spot] += product[part * quarter : (part + 1) * quarter]
         return carry
 
-    out_ref[...] = jnp.zeros_like(out_ref)
     lax.fori_loop(0, n_z, group_product, 0)
 
     for moving in sends:
@@ -539,25 +489,72 @@
         pl.when(dx != 1)(lambda: to_last.wait_send())
         pl.when((dx == 0) & root)(lambda: to_across.wait_send())
 
-
-def shared_response(partial_sums, n_z):
-    rows = partial_sums.shape[0] // 8
-    half = rows // 2
-    bf16 = jnp.bfloat16
-    part = partial_sums.reshape(2, 4, 2, half, LANES)
+    def sent_plane(x, carry):
+        to_behind(occ_ref.at[:, x], far.at[x], x).wait_send()
+        return carry
+
+    def passed_plane(x, carry):
+        to_sibling(occ_ref.at[:, x], near.at[x], x).wait_send()
+        return carry
+
+    def passed_far(x, carry):
+        to_sibling(far.at[x], near.at[x], x).wait_send()
+        return carry
+
+    to_behind(level_ref, far_level, PLANES).wait_send()
+    lax.fori_loop(0, PLANES, sent_plane, 0)
+
+    @pl.when(core == 1)
+    def _():
+        to_sibling(level_ref, near_level, PLANES).wait_send()
+        lax.fori_loop(0, PLANES, passed_plane, 0)
+
+    @pl.when(core == 0)
+    def _():
+        to_sibling(far_level, near_level, PLANES).wait_send()
+        lax.fori_loop(0, PLANES, passed_far, 0)
+
+
+def whole_response(occ, emp, gvectors, energies, ztab, xytabs, n_z):
+    bf16, f32 = jnp.bfloat16, jnp.float32
+    half = NG // 16
+    anywhere, vmem = pl.BlockSpec(memory_space=pl.ANY), pl.BlockSpec(memory_space=pltpu.VMEM)
     return pl.pallas_call(
-        functools.partial(share_kernel, rows),
-        out_shape=jax.ShapeDtypeStruct((2, rows // 4, rows), jnp.float32),
-        in_specs=[pl.BlockSpec(memory_space=pltpu.VMEM)],
-        out_specs=pl.BlockSpec(memory_space=pltpu.VMEM),
+        response_kernel,
+        out_shape=jax.ShapeDtypeStruct((2, half // 2, 2 * half), f32),
+        in_specs=[anywhere, anywhere, vmem, vmem, vmem, anywhere, anywhere],
+        out_specs=vmem,
         scratch_shapes=[
+            pltpu.VMEM((PLANES, 2, 4, CELLS), bf16),
+            pltpu.VMEM((PLANES, 2, 4, CELLS), bf16),
+            pltpu.VMEM((8, LANES), f32),
+            pltpu.VMEM((8, LANES), f32),
+            pltpu.VMEM((8, LANES), f32),
+            pltpu.VMEM((2, PLANES, 8, CELLS), bf16),
+            pltpu.VMEM((Z_ROWS, GROUP_CELLS), bf16),
+            pltpu.VMEM((PLANES // BATCH, WAVE_ROWS, DEPTH), bf16),
+            pltpu.VMEM((16, CELLS), f32),
+            pltpu.VMEM((GROUPS * LANES, GROUP_CELLS), bf16),
+            pltpu.VMEM((Z_ROWS, GROUPS * LANES), f32),
+            pltpu.VMEM((Q_SLOTS // 2, DEPTH, 2 * LANES), bf16),
+            pltpu.VMEM((Q_SLOTS * WAVE_ROWS, LANES), f32),
+            pltpu.VMEM((1024, LANES), f32),
+            pltpu.VMEM((1, NG), jnp.int32),
+            pltpu.SMEM((1, NG), jnp.int32),
+            pltpu.VMEM((1, NG), f32),
+            pltpu.VMEM((2, 4, 2, half, LANES), bf16),
             pltpu.VMEM((n_z, 2, 2, 2, half, LANES), bf16),
-            pltpu.VMEM((n_z, 2, 2, rows // 4, LANES), bf16),
+            pltpu.VMEM((n_z, 2, 2, half // 2, LANES), bf16),
             pltpu.VMEM((2, 2, half, LANES), bf16),
             pltpu.VMEM((2, 2, half, LANES), bf16),
             pltpu.VMEM((4, 2, half, LANES), bf16),
             pltpu.VMEM((2, half, LANES), bf16),
             pltpu.VMEM((2, half, LANES), bf16),
+            pltpu.SemaphoreType.DMA((PLANES + 1,)),
+            pltpu.SemaphoreType.DMA((PLANES + 1,)),
+            pltpu.SemaphoreType.DMA((PLANES + 1,)),
+            pltpu.SemaphoreType.DMA((PLANES + 1,)),
+            pltpu.SemaphoreType.DMA((4,)),
             pltpu.SemaphoreType.DMA((128,)),
             pltpu.SemaphoreType.DMA((8,)),
             pltpu.SemaphoreType.DMA((6, 2, n_z // 2 + 1)),
@@ -565,28 +562,21 @@
             pltpu.SemaphoreType.DMA((3, n_z)),
         ],
         compiler_params=pltpu.CompilerParams(
-            collective_id=0, has_side_effects=True, vmem_limit_bytes=40 * 2**20
+            collective_id=0, has_side_effects=True, vmem_limit_bytes=60 * 2**20
         ),
         cost_estimate=pl.CostEstimate(
-            flops=1_100_000_000, bytes_accessed=2_000_000, transcendentals=0
+            flops=16_000_000_000, bytes_accessed=12_000_000, transcendentals=0
         ),
-    )(part)
-
-
-def lane_levels(occ_energy, empty_energy):
-    occ = jnp.broadcast_to(occ_energy.astype(jnp.float32)[None, :, None], (2, 4, 16))
-    emp = jnp.broadcast_to(empty_energy.astype(jnp.float32)[None, :], (16, 8))
-    rows = jnp.stack([occ.reshape(LANES), emp.reshape(LANES)])
-    return jnp.concatenate([rows, jnp.zeros((6, LANES), jnp.float32)])
+    )(occ, emp, gvectors, *energies, ztab, xytabs)
 
 
 def shards(ztab, xytabs, occupied_states, empty_states, occ_energy, empty_energy, gvectors):
     occ = jnp.transpose(occupied_states, (0, 2, 1, 3))
     emp = jnp.transpose(empty_states, (0, 2, 1, 3))
-    levels = lane_levels(occ_energy, empty_energy)
-    partial_sums = partial_density(occ, emp, gvectors, levels, ztab, xytabs)
+    energies = occ_energy.reshape(1, -1), empty_energy.reshape(1, -1)
     n_z = lax.axis_size("blk") // 4
-    return jnp.transpose(shared_response(partial_sums, n_z), (1, 0, 2))
+    out = whole_response(occ, emp, gvectors, energies, ztab, xytabs, n_z)
+    return jnp.transpose(out, (1, 0, 2))
 
 
 def solution(mesh):

time: 144 us -> 156 us (1.083)
  Pallas kernels: 139 us -> 153 us
  local copies, waits for them, and re-layouts: 4.05 us -> 2.24 us
    pallas_call x2 -> x1, Pallas kernels: 139 us -> 153 us  [whole_response(): pl.pallas_call(response_kernel, out_shape=jax.ShapeDtypeStruct((2, half /...]
where the time goes in v4:
time: 156 us; the launch traced here: 155 us
  Pallas kernels  153 us (98%)
  local copies, waits for them, and re-layouts  2.24 us (1%)
    pallas_call x1, Pallas kernels, whole_response(): pl.pallas_call(response_kernel, out_shape=jax.ShapeDtypeStruct((2, half /...  153 us

profile of v4, /device:TPU:26, one launch (start us, length us, event | category | flops | bytes accessed | tf_op | source)
XLA Modules:
  0.0 155.3 jit_solution(17513643135907837079)
XLA Ops:
  0.0 153.0 %shard_map.73 = f32[2,128,512]{2,1,0:T(8,128)} custom-call(bf16[2,9,4,10368]{3,2,1,0:T(4,128)(2,1)} %bitcast.7, bf16[2,9,8,10368]{3,2,1,0:T(8,128)(2,1)} %bitcast.6, s32[3,4096]{1,0:T(4,128)} %wave_ref.1, bf16[1,4]{1,0:T(2,128)(2,1)} %bitcast.8, bf16[1,8]{1,0:T(2,128)(2,1)} %bitcast.9, bf16[264,1152]{1,0:T(8,128)(2,1)} %constant.4.clone.ztab_ref, ...), custom_call_target="tpu_custom_call" | custom-call | flops 16000000000 | bytes 12000000 | tf_op jit(solution)/shard_map/pallas_call | solution.py:522
  153.0 2.2 %copy.8 = f32[128,2,512]{2,1,0:T(2,128)} copy(f32[128,2,512]{2,0,1:T(8,128)} %bitcast.5) | data formatting | bytes 1048576 | tf_op jit(solution)/shard_map/transpose | solution.py:579

commit v5 on v3

--- a/solution.py
+++ b/solution.py
@@ -70,8 +70,8 @@
 
 
 def density_kernel(
-    occ_ref, emp_ref, wave_ref, level_ref, ztab_ref, xytab_ref, out_ref,
-    near, far, near_level, far_level, emp, ztab, xytab, occ_f, pairs, depth_out, sections, waves,
+    occ_ref, emp_ref, wave_ref, occ_energy_ref, emp_energy_ref, ztab_ref, xytab_ref, out_ref,
+    near, far, level_ref, near_level, far_level, emp, ztab, xytab, occ_f, pairs, depth_out, sections, waves,
     picked, index_v, index_s, sign_v, ahead_sems, far_sems, pass_sems, near_sems, load_sems,
 ):
     blk, pw = lax.axis_index("blk"), lax.axis_index("pw")
@@ -107,8 +107,18 @@
         to_sibling(occ_ref.at[:, x], near.at[x], x).start()
         return carry
 
+    lax.fori_loop(0, PLANES, send_plane, 0)
+    lane = lax.broadcasted_iota(jnp.int32, (8, LANES), 1)
+    occ_energy = occ_energy_ref[...].astype(jnp.float32)
+    emp_energy = emp_energy_ref[...].astype(jnp.float32)
+    spread = jnp.zeros((8, LANES), jnp.float32)
+    for v in range(4):
+        spread = jnp.where((lane // 16) % 4 == v, occ_energy[:, v : v + 1], spread)
+    level_ref[...] = spread
+    emp_level = jnp.zeros((8, LANES), jnp.float32)
+    for c in range(8):
+        emp_level = jnp.where(lane % 8 == c, emp_energy[:, c : c + 1], emp_level)
     to_behind(level_ref, far_level, PLANES).start()
-    lax.fori_loop(0, PLANES, send_plane, 0)
 
     @pl.when(core == 1)
     def _():
@@ -194,8 +204,15 @@
             put(KMAX - q, cosine - sine)
 
     sections[Q_SLOTS // 2 - 1, :, LANES:] = jnp.zeros((DEPTH, LANES), jnp.bfloat16)
-    for batch in range(PLANES // BATCH):
-
+
+    def clear(k, carry):
+        rows = pl.ds(pl.multiple_of(k * WAVE_ROWS, 8), WAVE_ROWS)
+        waves[rows, :] = jnp.zeros((WAVE_ROWS, LANES), jnp.float32)
+        return carry
+
+    lax.fori_loop(0, Q_SLOTS, clear, 0)
+
+    def each_batch(batch, carry):
         def each_plane(spot, carry):
             one_plane(batch * BATCH + spot, spot)
             return carry
@@ -207,16 +224,16 @@
             first = pl.multiple_of(k * 2 * WAVE_ROWS, 8)
             for half in range(2):
                 rows = pl.ds(first + half * WAVE_ROWS, WAVE_ROWS)
-                value = product[:, half * LANES : (half + 1) * LANES]
-                waves[rows, :] = value if batch == 0 else waves[rows, :] + value
+                waves[rows, :] += product[:, half * LANES : (half + 1) * LANES]
             return carry
 
         lax.fori_loop(0, Q_SLOTS // 2, slot_pair, 0)
-
+        return carry
+
+    lax.fori_loop(0, PLANES // BATCH, each_batch, 0)
     landed(near_level, near_sems.at[PLANES])
-    lane = lax.broadcasted_iota(jnp.int32, (1, LANES), 1)
-    occ_level = jnp.where(lane < LANES // 2, near_level[0:1, :], far_level[0:1, :])
-    scale = jnp.sqrt(2.0 / (level_ref[1:2, :] - occ_level + omega_shift))
+    occ_level = jnp.where(lane < LANES // 2, near_level[...], far_level[...])
+    scale = jnp.sqrt(2.0 / (emp_level - occ_level + omega_shift))[0:1]
 
     def chunk(w, carry):
         def pick(step, carry):
@@ -264,17 +281,18 @@
         lax.fori_loop(0, PLANES, passed_far, 0)
 
 
-def partial_density(occ, emp, gvectors, levels, ztab, xytabs):
+def partial_density(occ, emp, gvectors, energies, ztab, xytabs):
     bf16, f32 = jnp.bfloat16, jnp.float32
     anywhere, vmem = pl.BlockSpec(memory_space=pl.ANY), pl.BlockSpec(memory_space=pltpu.VMEM)
     return pl.pallas_call(
         density_kernel,
         out_shape=jax.ShapeDtypeStruct((NG, LANES), bf16),
-        in_specs=[anywhere, anywhere, vmem, vmem, anywhere, anywhere],
+        in_specs=[anywhere, anywhere, vmem, vmem, vmem, anywhere, anywhere],
         out_specs=vmem,
         scratch_shapes=[
             pltpu.VMEM((PLANES, 2, 4, CELLS), bf16),
             pltpu.VMEM((PLANES, 2, 4, CELLS), bf16),
+            pltpu.VMEM((8, LANES), f32),
             pltpu.VMEM((8, LANES), f32),
             pltpu.VMEM((8, LANES), f32),
             pltpu.VMEM((2, PLANES, 8, CELLS), bf16),
@@ -301,11 +319,11 @@
         cost_estimate=pl.CostEstimate(
             flops=15_000_000_000, bytes_accessed=12_000_000, transcendentals=0
         ),
-    )(occ, emp, gvectors, levels, ztab, xytabs)
-
-
-def share_kernel(rows, part_ref, out_ref, everyone, left, relay, passed, arrived, plane_sum, other,
-                 send_sems, sum_sems, ring_sems, side_sems, left_sems):
+    )(occ, emp, gvectors, *energies, ztab, xytabs)
+
+
+def share_kernel(rows, part_ref, out_ref, everyone, left, relay, passed, arrived, own, plane_sum,
+                 other, send_sems, sum_sems, own_sems, ring_sems, side_sems, left_sems):
     half_rows, quarter = rows // 2, rows // 4
     blk, pw = lax.axis_index("blk"), lax.axis_index("pw")
     z, y, core = blk // 4, (blk // 2) % 2, blk % 2
@@ -325,7 +343,7 @@
     def copy(source, target, arrival, device):
         return pltpu.make_async_remote_copy(
             src_ref=source, dst_ref=target, send_sem=send_sems.at[len(sends)], recv_sem=arrival,
-            device_id=device, device_id_type=pl.DeviceIdType.MESH,
+            device_id=device, device_id_type=MESH,
         )
 
     def send(source, target, arrival, device):
@@ -339,7 +357,7 @@
     barrier = pltpu.get_barrier_semaphore()
     neighbours = (x_next, x_last, z_next, z_last, sibling, beside, facing, across)
     for device in neighbours:
-        pl.semaphore_signal(barrier, inc=1, device_id=device, device_id_type=pl.DeviceIdType.MESH)
+        pl.semaphore_signal(barrier, inc=1, device_id=device, device_id_type=MESH)
     pl.semaphore_wait(barrier, len(neighbours))
 
     xn, xl, xo = (x + 1) % 4, (x + 3) % 4, (x + 2) % 4
@@ -348,11 +366,21 @@
     send(part_ref.at[:, xn, 1], arrived.at[0], sum_sems.at[2], x_next)
     send(part_ref.at[:, xl, 0], arrived.at[1], sum_sems.at[3], x_last)
     f32 = jnp.float32
+    moves = [
+        pltpu.make_async_copy(part_ref.at[:, xn, 0], passed.at[0], own_sems.at[0]),
+        pltpu.make_async_copy(part_ref.at[:, xl, 1], passed.at[1], own_sems.at[1]),
+        pltpu.make_async_copy(part_ref.at[:, x], own, own_sems.at[2]),
+    ]
+    for move in moves:
+        move.start()
+    out_ref[...] = jnp.zeros_like(out_ref)
+    for move in moves:
+        move.wait()
     landed(relay.at[0], sum_sems.at[0])
-    passed[0] = (part_ref[:, xn, 0].astype(f32) + relay[0].astype(f32)).astype(jnp.bfloat16)
+    passed[0] = (passed[0].astype(f32) + relay[0].astype(f32)).astype(jnp.bfloat16)
     send(passed.at[0], arrived.at[2], sum_sems.at[4], x_next)
     landed(relay.at[1], sum_sems.at[1])
-    passed[1] = (part_ref[:, xl, 1].astype(f32) + relay[1].astype(f32)).astype(jnp.bfloat16)
+    passed[1] = (passed[1].astype(f32) + relay[1].astype(f32)).astype(jnp.bfloat16)
     send(passed.at[1], arrived.at[3], sum_sems.at[5], x_last)
     landed(arrived.at[0], sum_sems.at[2])
     landed(arrived.at[1], sum_sems.at[3])
@@ -362,7 +390,7 @@
     def x_total(y_hi, half):
         first, second = (2, 1) if half == 0 else (0, 3)
         return (
-            part_ref[y_hi, x, half].astype(f32)
+            own[y_hi, half].astype(f32)
             + arrived[first, y_hi].astype(f32)
             + arrived[second, y_hi].astype(f32)
         )
@@ -441,79 +469,104 @@
     held = lambda zz, part: left.at[zz, :, :, pl.ds(part * eighth, eighth)]
     late = []
 
-    def left_step(step):
+    def left_copies(step):
+        made = []
         for zz, tag in group_origins(step):
             base = len(sends)
 
             def numbered(source, target, arrival, device, offset):
                 return pltpu.make_async_remote_copy(
                     src_ref=source, dst_ref=target, send_sem=send_sems.at[base + offset],
-                    recv_sem=arrival, device_id=device, device_id_type=pl.DeviceIdType.MESH,
+                    recv_sem=arrival, device_id=device, device_id_type=MESH,
                 )
 
-            rows_at = lambda half, start, count: everyone.at[zz, :, :, half, pl.ds(start, count)]
+            there = everyone.at[zz, :, :, 1 - y, pl.ds(first, quarter)]
             to_next = numbered(held(zz, 0), held(zz, 0), left_sems.at[0, tag], x_next, 0)
             to_last = numbered(held(zz, 1), held(zz, 1), left_sems.at[1, tag], x_last, 1)
-            to_across = numbered(
-                rows_at(1 - y, first, quarter), left.at[zz], left_sems.at[2, tag], across, 2
-            )
-
-            @pl.when(dx == 0)
-            def _():
-                @pl.when(root)
-                def _():
-                    to_across.start()
-                    left[zz] = everyone[zz, :, :, y, pl.ds(first, quarter)]
-
-                @pl.when(jnp.logical_not(root))
-                def _():
-                    landed(left.at[zz], left_sems.at[2, tag])
-
+            to_across = numbered(there, left.at[zz], left_sems.at[2, tag], across, 2)
+            made.append((zz, tag, to_next, to_last, to_across))
+            sends.extend([None] * 3)
+        late.extend(made)
+        return made
+
+    def left_from_root(made):
+        @pl.when((dx == 0) & root)
+        def _():
+            for zz, tag, to_next, to_last, to_across in made:
+                to_across.start()
+                left[zz] = everyone[zz, :, :, y, pl.ds(first, quarter)]
                 to_next.start()
                 to_last.start()
 
-            @pl.when((dx == 1) | (dx == 2))
-            def _():
+    def left_onward(made):
+        @pl.when((dx == 0) & jnp.logical_not(root))
+        def _():
+            for zz, tag, to_next, to_last, to_across in made:
+                landed(left.at[zz], left_sems.at[2, tag])
+                to_next.start()
+                to_last.start()
+
+        @pl.when(dx == 1)
+        def _():
+            for zz, tag, to_next, to_last, to_across in made:
                 landed(held(zz, 0), left_sems.at[0, tag])
                 to_next.start()
 
-            @pl.when((dx == 3) | (dx == 2))
-            def _():
+        @pl.when(dx == 3)
+        def _():
+            for zz, tag, to_next, to_last, to_across in made:
                 landed(held(zz, 1), left_sems.at[1, tag])
                 to_last.start()
 
-            late.append((zz, tag, to_next, to_last, to_across))
-            sends.extend([None] * 3)
-
-    def left_end():
-        for zz, tag, to_next, to_last, to_across in late:
-            pl.when(dx == 1)(lambda: landed(held(zz, 1), left_sems.at[1, tag]))
-            pl.when(dx == 3)(lambda: landed(held(zz, 0), left_sems.at[0, tag]))
-
+    def left_middle(made):
+        @pl.when(dx == 2)
+        def _():
+            for zz, tag, to_next, to_last, to_across in made:
+                landed(held(zz, 0), left_sems.at[0, tag])
+                to_next.start()
+                landed(held(zz, 1), left_sems.at[1, tag])
+                to_last.start()
+
+    parts = [left_copies(step) for step in range(n_z // 2 + 1)]
     rest_step(0)
     ring_step(1)
-    left_step(0)
+    left_from_root(parts[0])
     ring_step(2)
     side_step(1)
     rest_step(1)
-    left_step(1)
+    left_from_root(parts[1])
     ring_step(3)
     side_step(2)
     rest_step(2)
-    left_step(2)
+    left_from_root(parts[2])
+    left_onward(parts[0])
     ring_step(4)
     side_step(3)
     rest_step(3)
-    left_step(3)
+    left_from_root(parts[3])
+    left_onward(parts[1])
+    left_middle(parts[0])
     side_step(4)
     rest_step(4)
-    left_step(4)
-    left_end()
-
-    def joined(value):
-        return jnp.concatenate([value[0, 0], value[0, 1], value[1, 0], value[1, 1]], axis=1)
-
-    def group_product(zz, carry):
+    left_from_root(parts[4])
+    for step in range(2, n_z // 2 + 1):
+        left_onward(parts[step])
+        left_middle(parts[step - 1])
+    left_middle(parts[n_z // 2])
+
+    def group_product(k, carry):
+        odd = k % 2
+        tag = (odd * ((k + 1) // 2) + (1 - odd) * (n_z - k // 2)) % n_z
+        zz = (z + n_z - tag) % n_z
+
+        @pl.when(dx == 1)
+        def _():
+            landed(held(zz, 1), left_sems.at[1, tag])
+
+        @pl.when(dx == 3)
+        def _():
+            landed(held(zz, 0), left_sems.at[0, tag])
+
         straight = [left[zz, i // 2, i % 2].astype(f32) for i in range(4)]
         side = jnp.concatenate([turned(value) for value in straight], axis=1)
         both = jnp.concatenate([-jnp.concatenate(straight, axis=1), side], axis=0)
@@ -528,7 +581,6 @@
                 out_ref[spot] += product[part * quarter : (part + 1) * quarter]
         return carry
 
-    out_ref[...] = jnp.zeros_like(out_ref)
     lax.fori_loop(0, n_z, group_product, 0)
 
     for moving in sends:
@@ -548,7 +600,7 @@
     return pl.pallas_call(
         functools.partial(share_kernel, rows),
         out_shape=jax.ShapeDtypeStruct((2, rows // 4, rows), jnp.float32),
-        in_specs=[pl.BlockSpec(memory_space=pltpu.VMEM)],
+        in_specs=[pl.BlockSpec(memory_space=pl.ANY)],
         out_specs=pl.BlockSpec(memory_space=pltpu.VMEM),
         scratch_shapes=[
             pltpu.VMEM((n_z, 2, 2, 2, half, LANES), bf16),
@@ -556,16 +608,18 @@
             pltpu.VMEM((2, 2, half, LANES), bf16),
             pltpu.VMEM((2, 2, half, LANES), bf16),
             pltpu.VMEM((4, 2, half, LANES), bf16),
+            pltpu.VMEM((2, 2, half, LANES), bf16),
             pltpu.VMEM((2, half, LANES), bf16),
             pltpu.VMEM((2, half, LANES), bf16),
             pltpu.SemaphoreType.DMA((128,)),
             pltpu.SemaphoreType.DMA((8,)),
+            pltpu.SemaphoreType.DMA((3,)),
             pltpu.SemaphoreType.DMA((6, 2, n_z // 2 + 1)),
             pltpu.SemaphoreType.DMA((3,)),
             pltpu.SemaphoreType.DMA((3, n_z)),
         ],
         compiler_params=pltpu.CompilerParams(
-            collective_id=0, has_side_effects=True, vmem_limit_bytes=40 * 2**20
+            collective_id=0, has_side_effects=True, vmem_limit_bytes=60 * 2**20
         ),
         cost_estimate=pl.CostEstimate(
             flops=1_100_000_000, bytes_accessed=2_000_000, transcendentals=0
@@ -573,18 +627,11 @@
     )(part)
 
 
-def lane_levels(occ_energy, empty_energy):
-    occ = jnp.broadcast_to(occ_energy.astype(jnp.float32)[None, :, None], (2, 4, 16))
-    emp = jnp.broadcast_to(empty_energy.astype(jnp.float32)[None, :], (16, 8))
-    rows = jnp.stack([occ.reshape(LANES), emp.reshape(LANES)])
-    return jnp.concatenate([rows, jnp.zeros((6, LANES), jnp.float32)])
-
-
 def shards(ztab, xytabs, occupied_states, empty_states, occ_energy, empty_energy, gvectors):
     occ = jnp.transpose(occupied_states, (0, 2, 1, 3))
     emp = jnp.transpose(empty_states, (0, 2, 1, 3))
-    levels = lane_levels(occ_energy, empty_energy)
-    partial_sums = partial_density(occ, emp, gvectors, levels, ztab, xytabs)
+    energies = occ_energy.reshape(1, -1), empty_energy.reshape(1, -1)
+    partial_sums = partial_density(occ, emp, gvectors, energies, ztab, xytabs)
     n_z = lax.axis_size("blk") // 4
     return jnp.transpose(shared_response(partial_sums, n_z), (1, 0, 2))
 

time: 144 us -> 159 us (1.10)
  Pallas kernels: 139 us -> 156 us
  local copies, waits for them, and re-layouts: 4.05 us -> 2.24 us
    pallas_call x1, Pallas kernels: 56.2 us -> 82.1 us  [partial_density(): pl.pallas_call(density_kernel, out_shape=jax.ShapeDtypeStruct((NG, LANES)...]
    pallas_call x1, Pallas kernels: 83.2 us -> 74.2 us  [shared_response(): pl.pallas_call(functools.partial(share_kernel, rows), out_shape=jax.Shape...]
where the time goes in v5:
time: 159 us
  Pallas kernels  156 us (98%)
  local copies, waits for them, and re-layouts  2.24 us (1%)
    pallas_call x1, Pallas kernels, partial_density(): pl.pallas_call(density_kernel, out_shape=jax.ShapeDtypeStruct((NG, LANES)...  82.1 us
    pallas_call x1, Pallas kernels, shared_response(): pl.pallas_call(functools.partial(share_kernel, rows), out_shape=jax.Shape...  74.2 us

profile of v5, /device:TPU:26, one launch (start us, length us, event | category | flops | bytes accessed | tf_op | source)
XLA Modules:
  0.0 158.5 jit_solution(10117133795206984524)
XLA Ops:
  0.0 82.1 %shard_map.73 = bf16[4096,128]{1,0:T(8,128)(2,1)} custom-call(bf16[2,9,4,10368]{3,2,1,0:T(4,128)(2,1)} %bitcast.8, bf16[2,9,8,10368]{3,2,1,0:T(8,128)(2,1)} %bitcast.7, s32[3,4096]{1,0:T(4,128)} %wave_ref.1, bf16[1,4]{1,0:T(2,128)(2,1)} %bitcast.9, bf16[1,8]{1,0:T(2,128)(2,1)} %bitcast.10, bf16[264,1152]{1,0:T(8,128)(2,1)} %constant.4.clone.ztab_ref, ...), custom_call_target="tpu_custom_call" | custom-call | flops 15000000512 | bytes 12000000 | tf_op jit(solution)/shard_map/pallas_call | solution.py:287
  82.1 74.2 %shard_map.74 = f32[2,128,512]{2,1,0:T(8,128)} custom-call(bf16[2,4,2,256,128]{4,3,2,1,0:T(8,128)(2,1)} %bitcast.11), custom_call_target="tpu_custom_call" | custom-call | flops 1100000000 | bytes 2000000 | tf_op jit(solution)/shard_map/pallas_call | solution.py:600
  156.3 2.2 %copy.8 = f32[128,2,512]{2,1,0:T(2,128)} copy(f32[128,2,512]{2,0,1:T(8,128)} %bitcast.6) | data formatting | bytes 1048576 | tf_op jit(solution)/shard_map/transpose | solution.py:636

commit v6 on v4

--- a/solution.py
+++ b/solution.py
@@ -123,7 +123,6 @@
         to_sibling(occ_ref.at[:, x], near.at[x], x).start()
         return carry
 
-    lax.fori_loop(0, PLANES, send_plane, 0)
     lane = lax.broadcasted_iota(jnp.int32, (8, LANES), 1)
     occ_energy = occ_energy_ref[...].astype(f32)
     emp_energy = emp_energy_ref[...].astype(f32)
@@ -135,6 +134,7 @@
     for c in range(8):
         emp_level = jnp.where(lane % 8 == c, emp_energy[:, c : c + 1], emp_level)
     to_behind(level_ref, far_level, PLANES).start()
+    lax.fori_loop(0, PLANES, send_plane, 0)
 
     @pl.when(core == 1)
     def _():
@@ -154,12 +154,6 @@
     sign_v[...] = jnp.where(flat < 0, -1.0, 1.0).astype(jnp.float32)
     index_move = pltpu.make_async_copy(index_v, index_s, load_sems.at[3])
     index_move.start()
-    landed(far_level, far_sems.at[PLANES])
-
-    @pl.when(core == 0)
-    def _():
-        to_sibling(far_level, near_level, PLANES).start()
-
     for load in loads:
         load.wait()
     index_move.wait()
@@ -220,8 +214,19 @@
             put(KMAX - q, cosine - sine)
 
     sections[Q_SLOTS // 2 - 1, :, LANES:] = jnp.zeros((DEPTH, LANES), jnp.bfloat16)
-    for batch in range(PLANES // BATCH):
-
+    def clear(k, carry):
+        rows = pl.ds(pl.multiple_of(k * WAVE_ROWS, 8), WAVE_ROWS)
+        waves[rows, :] = jnp.zeros((WAVE_ROWS, LANES), jnp.float32)
+        return carry
+
+    lax.fori_loop(0, Q_SLOTS, clear, 0)
+    landed(far_level, far_sems.at[PLANES])
+
+    @pl.when(core == 0)
+    def _():
+        to_sibling(far_level, near_level, PLANES).start()
+
+    def each_batch(batch, carry):
         def each_plane(spot, carry):
             one_plane(batch * BATCH + spot, spot)
             return carry
@@ -233,12 +238,13 @@
             first = pl.multiple_of(k * 2 * WAVE_ROWS, 8)
             for half in range(2):
                 rows = pl.ds(first + half * WAVE_ROWS, WAVE_ROWS)
-                value = product[:, half * LANES : (half + 1) * LANES]
-                waves[rows, :] = value if batch == 0 else waves[rows, :] + value
+                waves[rows, :] += product[:, half * LANES : (half + 1) * LANES]
             return carry
 
         lax.fori_loop(0, Q_SLOTS // 2, slot_pair, 0)
-
+        return carry
+
+    lax.fori_loop(0, PLANES // BATCH, each_batch, 0)
     landed(near_level, near_sems.at[PLANES])
     occ_level = jnp.where(lane < LANES // 2, near_level[...], far_level[...])
     scale = jnp.sqrt(2.0 / (emp_level - occ_level + omega_shift))[0:1]
@@ -389,7 +395,8 @@
     held = lambda zz, part: left.at[zz, :, :, pl.ds(part * eighth, eighth)]
     late = []
 
-    def left_step(step):
+    def left_copies(step):
+        made = []
         for zz, tag in group_origins(step):
             base = len(sends)
 
@@ -399,58 +406,79 @@
                     recv_sem=arrival, device_id=device, device_id_type=MESH,
                 )
 
-            rows_at = lambda half, start, count: everyone.at[zz, :, :, half, pl.ds(start, count)]
+            there = everyone.at[zz, :, :, 1 - y, pl.ds(first, quarter)]
             to_next = numbered(held(zz, 0), held(zz, 0), left_sems.at[0, tag], x_next, 0)
             to_last = numbered(held(zz, 1), held(zz, 1), left_sems.at[1, tag], x_last, 1)
-            to_across = numbered(
-                rows_at(1 - y, first, quarter), left.at[zz], left_sems.at[2, tag], across, 2
-            )
-
-            @pl.when(dx == 0)
-            def _():
-                @pl.when(root)
-                def _():
-                    to_across.start()
-                    left[zz] = everyone[zz, :, :, y, pl.ds(first, quarter)]
-
-                @pl.when(jnp.logical_not(root))
-                def _():
-                    landed(left.at[zz], left_sems.at[2, tag])
-
+            to_across = numbered(there, left.at[zz], left_sems.at[2, tag], across, 2)
+            made.append((zz, tag, to_next, to_last, to_across))
+            sends.extend([None] * 3)
+        late.extend(made)
+        return made
+
+    def left_from_root(made):
+        @pl.when((dx == 0) & root)
+        def _():
+            for zz, tag, to_next, to_last, to_across in made:
+                to_across.start()
+                left[zz] = everyone[zz, :, :, y, pl.ds(first, quarter)]
                 to_next.start()
                 to_last.start()
 
-            @pl.when((dx == 1) | (dx == 2))
-            def _():
+    def left_onward(made):
+        @pl.when((dx == 0) & jnp.logical_not(root))
+        def _():
+            for zz, tag, to_next, to_last, to_across in made:
+                landed(left.at[zz], left_sems.at[2, tag])
+                to_next.start()
+                to_last.start()
+
+        @pl.when(dx == 1)
+        def _():
+            for zz, tag, to_next, to_last, to_across in made:
                 landed(held(zz, 0), left_sems.at[0, tag])
                 to_next.start()
 
-            @pl.when((dx == 3) | (dx == 2))
-            def _():
+        @pl.when(dx == 3)
+        def _():
+            for zz, tag, to_next, to_last, to_across in made:
                 landed(held(zz, 1), left_sems.at[1, tag])
                 to_last.start()
 
-            late.append((zz, tag, to_next, to_last, to_across))
-            sends.extend([None] * 3)
-
+    def left_middle(made):
+        @pl.when(dx == 2)
+        def _():
+            for zz, tag, to_next, to_last, to_across in made:
+                landed(held(zz, 0), left_sems.at[0, tag])
+                to_next.start()
+                landed(held(zz, 1), left_sems.at[1, tag])
+                to_last.start()
+
+    parts = [left_copies(step) for step in range(n_z // 2 + 1)]
     rest_step(0)
     ring_step(1)
-    left_step(0)
+    left_from_root(parts[0])
     ring_step(2)
     side_step(1)
     rest_step(1)
-    left_step(1)
+    left_from_root(parts[1])
     ring_step(3)
     side_step(2)
     rest_step(2)
-    left_step(2)
+    left_from_root(parts[2])
+    left_onward(parts[0])
     ring_step(4)
     side_step(3)
     rest_step(3)
-    left_step(3)
+    left_from_root(parts[3])
+    left_onward(parts[1])
+    left_middle(parts[0])
     side_step(4)
     rest_step(4)
-    left_step(4)
+    left_from_root(parts[4])
+    for step in range(2, n_z // 2 + 1):
+        left_onward(parts[step])
+        left_middle(parts[step - 1])
+    left_middle(parts[n_z // 2])
 
     def group_product(k, carry):
         odd = k % 2

time: 156 us -> 125 us (0.80)
  Pallas kernels: 153 us -> 123 us
    pallas_call x1, Pallas kernels: 153 us -> 123 us  [whole_response(): pl.pallas_call(response_kernel, out_shape=jax.ShapeDtypeStruct((2, half /...]
where the time goes in v6:
time: 125 us
  Pallas kernels  123 us (98%)
  local copies, waits for them, and re-layouts  2.24 us (2%)
    pallas_call x1, Pallas kernels, whole_response(): pl.pallas_call(response_kernel, out_shape=jax.ShapeDtypeStruct((2, half /...  123 us

profile of v6, /device:TPU:26, one launch (start us, length us, event | category | flops | bytes accessed | tf_op | source)
XLA Modules:
  0.0 124.9 jit_solution(9726682239071305369)
XLA Ops:
  0.0 122.6 %shard_map.73 = f32[2,128,512]{2,1,0:T(8,128)} custom-call(bf16[2,9,4,10368]{3,2,1,0:T(4,128)(2,1)} %bitcast.7, bf16[2,9,8,10368]{3,2,1,0:T(8,128)(2,1)} %bitcast.6, s32[3,4096]{1,0:T(4,128)} %wave_ref.1, bf16[1,4]{1,0:T(2,128)(2,1)} %bitcast.8, bf16[1,8]{1,0:T(2,128)(2,1)} %bitcast.9, bf16[264,1152]{1,0:T(8,128)(2,1)} %constant.4.clone.ztab_ref, ...), custom_call_target="tpu_custom_call" | custom-call | flops 16000000000 | bytes 12000000 | tf_op jit(solution)/shard_map/pallas_call | solution.py:550
  122.6 2.2 %copy.8 = f32[128,2,512]{2,1,0:T(2,128)} copy(f32[128,2,512]{2,0,1:T(8,128)} %bitcast.5) | data formatting | bytes 1048576 | tf_op jit(solution)/shard_map/transpose | solution.py:607

commit v7 on v6

--- a/solution.py
+++ b/solution.py
@@ -71,7 +71,7 @@
 def response_kernel(
     occ_ref, emp_ref, wave_ref, occ_energy_ref, emp_energy_ref, ztab_ref, xytab_ref, out_ref,
     near, far, level_ref, near_level, far_level, emp, ztab, xytab, occ_f, pairs, depth_out, sections, waves,
-    picked, index_v, index_s, sign_v, part_ref, everyone, left, relay, passed, arrived, plane_sum,
+    picked, index_v, index_s, sign_v, sign_rows, part_ref, everyone, left, relay, passed, arrived, plane_sum,
     other, ahead_sems, far_sems, pass_sems, near_sems, load_sems, send_sems, sum_sems, ring_sems,
     side_sems, left_sems,
 ):
@@ -160,8 +160,8 @@
 
     def group_pairs(x, group):
         for part in range(3):
-            start = pl.multiple_of(group * GROUP_CELLS + part * 384, 128)
-            cells = pl.ds(start, 384)
+            start = group * GROUP_CELLS + part * 384
+            cells = slice(start, start + 384)
             emp_re = emp[0, x, :, cells].astype(jnp.float32)
             emp_im = emp[1, x, :, cells].astype(jnp.float32)
             for v in range(8):
@@ -171,7 +171,7 @@
                 both = jnp.concatenate(
                     [occ_re * emp_re + occ_im * emp_im, occ_re * emp_im - occ_im * emp_re], axis=0
                 )
-                rows = pl.ds(pl.multiple_of(group * LANES + v * 16, 16), 16)
+                rows = slice(group * LANES + v * 16, group * LANES + v * 16 + 16)
                 pairs[rows, part * 384 : part * 384 + 384] = both.astype(jnp.bfloat16)
 
     blank = jnp.zeros((ROWS_X - GY, LANES), jnp.float32)
@@ -192,14 +192,15 @@
             occ_f[part * 4 : part * 4 + 4, :] = near[x, part].astype(jnp.float32)
             occ_f[part * 4 + 8 : part * 4 + 12, :] = far[x, part].astype(jnp.float32)
 
-        def each_group(group, carry):
-            group_pairs(x, group)
-            return carry
-
-        lax.fori_loop(0, GROUPS, each_group, 0)
-        depth_out[...] = lax.dot_general(
-            ztab[...], pairs[...], (((1,), (1,)), ((), ())), preferred_element_type=jnp.float32
-        )
+        for start in range(0, GROUPS, 2):
+            stop = min(start + 2, GROUPS)
+            for group in range(start, stop):
+                group_pairs(x, group)
+            lines = slice(start * LANES, stop * LANES)
+            depth_out[:, lines] = lax.dot_general(
+                ztab[...], pairs[lines, :], (((1,), (1,)), ((), ())),
+                preferred_element_type=jnp.float32,
+            )
         rows = pl.ds(pl.multiple_of(spot * ROWS_X, 16), ROWS_X)
 
         def put(slot, value):
@@ -220,6 +221,14 @@
         return carry
 
     lax.fori_loop(0, Q_SLOTS, clear, 0)
+
+    def stand(step, carry):
+        first = pl.multiple_of(step * 128, 128)
+        row = sign_v[:, pl.ds(first, 128)]
+        sign_rows[pl.ds(first, 128), :] = jnp.broadcast_to(row, (128, LANES)).T
+        return carry
+
+    lax.fori_loop(0, NG // 128, stand, 0)
     landed(far_level, far_sems.at[PLANES])
 
     @pl.when(core == 0)
@@ -264,8 +273,7 @@
             cosine = picked[pl.ds(part * 256, 128, stride=2), :]
             sine = picked[pl.ds(part * 256 + 1, 128, stride=2), :]
             first = pl.multiple_of(base + part * 128, 128)
-            sign = jnp.broadcast_to(sign_v[:, pl.ds(first, 128)], (128, LANES)).T
-            total = (cosine + sign * turned(sine)) * scale
+            total = (cosine + sign_rows[pl.ds(first, 128), :] * turned(sine)) * scale
             rows = slice((part % 2) * 128, (part % 2) * 128 + 128)
             part_ref[yy, xx, part // 2, rows, :] = total.astype(bf16)
 
@@ -570,6 +578,7 @@
             pltpu.VMEM((1, NG), jnp.int32),
             pltpu.SMEM((1, NG), jnp.int32),
             pltpu.VMEM((1, NG), f32),
+            pltpu.VMEM((NG, LANES), f32),
             pltpu.VMEM((2, 4, 2, half, LANES), bf16),
             pltpu.VMEM((n_z, 2, 2, 2, half, LANES), bf16),
             pltpu.VMEM((n_z, 2, 2, half // 2, LANES), bf16),

time: 125 us -> 121 us (0.968)
  Pallas kernels: 123 us -> 118 us
    pallas_call x1, Pallas kernels: 123 us -> 118 us  [whole_response(): pl.pallas_call(response_kernel, out_shape=jax.ShapeDtypeStruct((2, half /...]
where the time goes in v7:
time: 121 us
  Pallas kernels  118 us (98%)
  local copies, waits for them, and re-layouts  2.24 us (2%)
    pallas_call x1, Pallas kernels, whole_response(): pl.pallas_call(response_kernel, out_shape=jax.ShapeDtypeStruct((2, half /...  118 us

profile of v7, /device:TPU:26, one launch (start us, length us, event | category | flops | bytes accessed | tf_op | source)
XLA Modules:
  0.0 120.7 jit_solution(10512147360586598541)
XLA Ops:
  0.0 118.5 %shard_map.73 = f32[2,128,512]{2,1,0:T(8,128)} custom-call(bf16[2,9,4,10368]{3,2,1,0:T(4,128)(2,1)} %bitcast.7, bf16[2,9,8,10368]{3,2,1,0:T(8,128)(2,1)} %bitcast.6, s32[3,4096]{1,0:T(4,128)} %wave_ref.1, bf16[1,4]{1,0:T(2,128)(2,1)} %bitcast.8, bf16[1,8]{1,0:T(2,128)(2,1)} %bitcast.9, bf16[264,1152]{1,0:T(8,128)(2,1)} %constant.4.clone.ztab_ref, ...), custom_call_target="tpu_custom_call" | custom-call | flops 16000000000 | bytes 12000000 | tf_op jit(solution)/shard_map/pallas_call | solution.py:558
  118.5 2.2 %copy.8 = f32[128,2,512]{2,1,0:T(2,128)} copy(f32[128,2,512]{2,0,1:T(8,128)} %bitcast.5) | data formatting | bytes 1048576 | tf_op jit(solution)/shard_map/transpose | solution.py:616

commit v8 on v7

--- a/solution.py
+++ b/solution.py
@@ -258,8 +258,8 @@
     occ_level = jnp.where(lane < LANES // 2, near_level[...], far_level[...])
     scale = jnp.sqrt(2.0 / (emp_level - occ_level + omega_shift))[0:1]
 
-    def chunk(yy, xx):
-        base = (yy * 4 + xx) * 512
+    def chunk(yy, xx, half):
+        base = (yy * 4 + xx) * 512 + half * 256
 
         def pick(step, carry):
             first = step * 16
@@ -268,18 +268,17 @@
                 picked[pl.ds((first + i) * 2, 2), :] = waves[pl.ds(row, 2), :]
             return carry
 
-        lax.fori_loop(0, 32, pick, 0)
-        for part in range(4):
+        lax.fori_loop(0, 16, pick, 0)
+        for part in range(2):
             cosine = picked[pl.ds(part * 256, 128, stride=2), :]
             sine = picked[pl.ds(part * 256 + 1, 128, stride=2), :]
             first = pl.multiple_of(base + part * 128, 128)
             total = (cosine + sign_rows[pl.ds(first, 128), :] * turned(sine)) * scale
-            rows = slice((part % 2) * 128, (part % 2) * 128 + 128)
-            part_ref[yy, xx, part // 2, rows, :] = total.astype(bf16)
-
-    def both_chunks(xx):
+            part_ref[yy, xx, half, part * 128 : part * 128 + 128, :] = total.astype(bf16)
+
+    def both_chunks(xx, half):
         def one(yy, carry):
-            chunk(yy, xx)
+            chunk(yy, xx, half)
             return carry
 
         lax.fori_loop(0, 2, one, 0)
@@ -302,58 +301,70 @@
     half_rows, quarter = rows // 2, rows // 4
 
     xn, xl, xo = (x + 1) % 4, (x + 3) % 4, (x + 2) % 4
-    both_chunks(xo)
-    send(part_ref.at[:, xo, 0], relay.at[0], sum_sems.at[0], x_next)
-    send(part_ref.at[:, xo, 1], relay.at[1], sum_sems.at[1], x_last)
-    both_chunks(xn)
-    send(part_ref.at[:, xn, 1], arrived.at[0], sum_sems.at[2], x_next)
-    both_chunks(xl)
-    send(part_ref.at[:, xl, 0], arrived.at[1], sum_sems.at[3], x_last)
-    landed(relay.at[0], sum_sems.at[0])
-    passed[0] = (part_ref[:, xn, 0].astype(f32) + relay[0].astype(f32)).astype(bf16)
-    send(passed.at[0], arrived.at[2], sum_sems.at[4], x_next)
-    landed(relay.at[1], sum_sems.at[1])
-    passed[1] = (part_ref[:, xl, 1].astype(f32) + relay[1].astype(f32)).astype(bf16)
-    send(passed.at[1], arrived.at[3], sum_sems.at[5], x_last)
-    both_chunks(x)
-    landed(arrived.at[0], sum_sems.at[2])
-    landed(arrived.at[1], sum_sems.at[3])
-    landed(arrived.at[2], sum_sems.at[4])
-    landed(arrived.at[3], sum_sems.at[5])
-
-    def x_total(y_hi, half):
+
+    def pass_on(half, xx, device):
+        landed(relay.at[half], sum_sems.at[half])
+        share = part_ref[:, xx, half].astype(f32) + relay[half].astype(f32)
+        passed[half] = share.astype(bf16)
+        send(passed.at[half], arrived.at[2 + half], sum_sems.at[4 + half], device)
+
+    def x_total(yy, half):
         first, second = (2, 1) if half == 0 else (0, 3)
         return (
-            part_ref[y_hi, x, half].astype(f32)
-            + arrived[first, y_hi].astype(f32)
-            + arrived[second, y_hi].astype(f32)
+            part_ref[yy, x, half].astype(f32)
+            + arrived[first, yy].astype(f32)
+            + arrived[second, yy].astype(f32)
         )
 
-    for half in range(2):
+    def cross_over(half):
+        for spot in (2, 1) if half == 0 else (0, 3):
+            landed(arrived.at[spot], sum_sems.at[2 + spot])
         plane_sum[half] = x_total(1 - y_hi, half).astype(bf16)
-    send(plane_sum, other, sum_sems.at[6], facing)
-    landed(other, sum_sems.at[6])
-    mine = everyone.at[z, y, core]
-    for half in range(2):
+        send(plane_sum.at[half], other.at[half], sum_sems.at[6 + half], facing)
+
+    def own_rho(half):
+        landed(other.at[half], sum_sems.at[6 + half])
         total = x_total(y_hi, half) + other[half].astype(f32)
         everyone[z, y, core, half] = total.astype(bf16)
 
-    send(mine, mine, side_sems.at[0], beside)
-    send(mine, mine, side_sems.at[1], sibling)
+    both_chunks(xo, 0)
+    send(part_ref.at[:, xo, 0], relay.at[0], sum_sems.at[0], x_next)
+    both_chunks(xl, 0)
+    send(part_ref.at[:, xl, 0], arrived.at[1], sum_sems.at[3], x_last)
+    both_chunks(xn, 0)
+    both_chunks(x, 0)
+    pass_on(0, xn, x_next)
+    both_chunks(xo, 1)
+    send(part_ref.at[:, xo, 1], relay.at[1], sum_sems.at[1], x_last)
+    both_chunks(xn, 1)
+    send(part_ref.at[:, xn, 1], arrived.at[0], sum_sems.at[2], x_next)
+    both_chunks(xl, 1)
+    cross_over(0)
+    both_chunks(x, 1)
+    pass_on(1, xl, x_last)
+
+    own_rho(0)
+    mine = lambda half: everyone.at[z, y, core, half]
+    theirs = lambda half: everyone.at[z, 1 - y, core, half]
     upper = lambda zz: everyone.at[zz, :, core, 0]
     lower = lambda zz, yy: everyone.at[zz, yy, core, 1]
+    send(mine(0), mine(0), side_sems.at[0, 0], beside)
+    send(mine(0), mine(0), side_sems.at[1, 0], sibling)
+    cross_over(1)
+    landed(theirs(0), side_sems.at[0, 0])
+    send(upper(z), upper(z), ring_sems.at[0, 0, 1], z_next)
+    send(upper(z), upper(z), ring_sems.at[0, 1, 1], z_last)
+    send(theirs(0), theirs(0), side_sems.at[2, 0], sibling)
+    own_rho(1)
     send(lower(z, y), lower(z, y), ring_sems.at[1, 0, 1], z_next)
     send(lower(z, y), lower(z, y), ring_sems.at[1, 1, 1], z_last)
-    theirs = everyone.at[z, 1 - y, core]
-    landed(theirs, side_sems.at[0])
-    send(upper(z), upper(z), ring_sems.at[0, 0, 1], z_next)
-    send(upper(z), upper(z), ring_sems.at[0, 1, 1], z_last)
-    send(theirs, theirs, side_sems.at[2], sibling)
+    send(mine(1), mine(1), side_sems.at[0, 1], beside)
+    send(mine(1), mine(1), side_sems.at[1, 1], sibling)
 
     longest = {(0, 0): n_z // 2, (0, 1): n_z // 2 - 1, (1, 0): n_z // 2 - 1, (1, 1): n_z // 2}
 
     def ring_step(step):
-        for half in (1, 0):
+        for half in (0, 1):
             for way in (0, 1):
                 if step > longest[half, way]:
                     continue
@@ -378,7 +389,8 @@
     def rest_step(step):
         if step == 0:
             for yy, spot in ((y, 1), (1 - y, 2)):
-                landed(everyone.at[z, yy, 1 - core], side_sems.at[spot])
+                for half in range(2):
+                    landed(everyone.at[z, yy, 1 - core, half], side_sems.at[spot, half])
             return
         for way in (0, 1):
             origin = (z + n_z - step) % n_z if way == 0 else (z + step) % n_z
@@ -462,8 +474,10 @@
                 to_last.start()
 
     parts = [left_copies(step) for step in range(n_z // 2 + 1)]
+    ring_step(1)
+    landed(theirs(1), side_sems.at[0, 1])
+    send(theirs(1), theirs(1), side_sems.at[2, 1], sibling)
     rest_step(0)
-    ring_step(1)
     left_from_root(parts[0])
     ring_step(2)
     side_step(1)
@@ -574,7 +588,7 @@
             pltpu.VMEM((Z_ROWS, GROUPS * LANES), f32),
             pltpu.VMEM((Q_SLOTS // 2, DEPTH, 2 * LANES), bf16),
             pltpu.VMEM((Q_SLOTS * WAVE_ROWS, LANES), f32),
-            pltpu.VMEM((1024, LANES), f32),
+            pltpu.VMEM((512, LANES), f32),
             pltpu.VMEM((1, NG), jnp.int32),
             pltpu.SMEM((1, NG), jnp.int32),
             pltpu.VMEM((1, NG), f32),
@@ -595,7 +609,7 @@
             pltpu.SemaphoreType.DMA((128,)),
             pltpu.SemaphoreType.DMA((8,)),
             pltpu.SemaphoreType.DMA((6, 2, n_z // 2 + 1)),
-            pltpu.SemaphoreType.DMA((3,)),
+            pltpu.SemaphoreType.DMA((3, 2)),
             pltpu.SemaphoreType.DMA((3, n_z)),
         ],
         compiler_params=pltpu.CompilerParams(

time: 121 us -> 118 us (0.975)
  Pallas kernels: 118 us -> 116 us
    pallas_call x1, Pallas kernels: 118 us -> 116 us  [whole_response(): pl.pallas_call(response_kernel, out_shape=jax.ShapeDtypeStruct((2, half /...]
where the time goes in v8:
time: 118 us
  Pallas kernels  116 us (98%)
  local copies, waits for them, and re-layouts  2.24 us (2%)
    pallas_call x1, Pallas kernels, whole_response(): pl.pallas_call(response_kernel, out_shape=jax.ShapeDtypeStruct((2, half /...  116 us

profile of v8, /device:TPU:26, one launch (start us, length us, event | category | flops | bytes accessed | tf_op | source)
XLA Modules:
  0.0 118.2 jit_solution(7935002520941509332)
XLA Ops:
  0.0 115.9 %shard_map.73 = f32[2,128,512]{2,1,0:T(8,128)} custom-call(bf16[2,9,4,10368]{3,2,1,0:T(4,128)(2,1)} %bitcast.7, bf16[2,9,8,10368]{3,2,1,0:T(8,128)(2,1)} %bitcast.6, s32[3,4096]{1,0:T(4,128)} %wave_ref.1, bf16[1,4]{1,0:T(2,128)(2,1)} %bitcast.8, bf16[1,8]{1,0:T(2,128)(2,1)} %bitcast.9, bf16[264,1152]{1,0:T(8,128)(2,1)} %constant.4.clone.ztab_ref, ...), custom_call_target="tpu_custom_call" | custom-call | flops 16000000000 | bytes 12000000 | tf_op jit(solution)/shard_map/pallas_call | solution.py:572
  115.9 2.2 %copy.8 = f32[128,2,512]{2,1,0:T(2,128)} copy(f32[128,2,512]{2,0,1:T(8,128)} %bitcast.5) | data formatting | bytes 1048576 | tf_op jit(solution)/shard_map/transpose | solution.py:630

commit v9 on v8

--- a/solution.py
+++ b/solution.py
@@ -71,7 +71,7 @@
 def response_kernel(
     occ_ref, emp_ref, wave_ref, occ_energy_ref, emp_energy_ref, ztab_ref, xytab_ref, out_ref,
     near, far, level_ref, near_level, far_level, emp, ztab, xytab, occ_f, pairs, depth_out, sections, waves,
-    picked, index_v, index_s, sign_v, sign_rows, part_ref, everyone, left, relay, passed, arrived, plane_sum,
+    picked, index_v, index_s, sign_v, sign_rows, part_ref, everyone, left, transit, relay, passed, arrived, plane_sum,
     other, ahead_sems, far_sems, pass_sems, near_sems, load_sems, send_sems, sum_sems, ring_sems,
     side_sems, left_sems,
 ):
@@ -412,7 +412,10 @@
             return (((z + step) % n_z, step),)
         return (((z + n_z - step) % n_z, step), ((z + step) % n_z, n_z - step))
 
+    piece_rows = quarter // 4
     held = lambda zz, part: left.at[zz, :, :, pl.ds(part * eighth, eighth)]
+    piece = lambda zz, q: left.at[zz, :, :, pl.ds(q * piece_rows, piece_rows)]
+    far_row = jnp.logical_not(root)
     late = []
 
     def left_copies(step):
@@ -420,58 +423,119 @@
         for zz, tag in group_origins(step):
             base = len(sends)
 
-            def numbered(source, target, arrival, device, offset):
+            def numbered(source, target, spot, device, offset):
                 return pltpu.make_async_remote_copy(
                     src_ref=source, dst_ref=target, send_sem=send_sems.at[base + offset],
-                    recv_sem=arrival, device_id=device, device_id_type=MESH,
+                    recv_sem=left_sems.at[spot, tag], device_id=device, device_id_type=MESH,
                 )
 
-            there = everyone.at[zz, :, :, 1 - y, pl.ds(first, quarter)]
-            to_next = numbered(held(zz, 0), held(zz, 0), left_sems.at[0, tag], x_next, 0)
-            to_last = numbered(held(zz, 1), held(zz, 1), left_sems.at[1, tag], x_last, 1)
-            to_across = numbered(there, left.at[zz], left_sems.at[2, tag], across, 2)
-            made.append((zz, tag, to_next, to_last, to_across))
-            sends.extend([None] * 3)
+            there = lambda start, count: everyone.at[zz, :, :, 1 - y, pl.ds(first + start, count)]
+            made.append(dict(
+                zz=zz,
+                tag=tag,
+                next_half=numbered(held(zz, 0), held(zz, 0), 0, x_next, 0),
+                last_half=numbered(held(zz, 1), held(zz, 1), 1, x_last, 1),
+                cross_half=numbered(there(0, eighth), held(zz, 0), 4, across, 2),
+                lend_next=numbered(there(eighth, piece_rows), transit.at[zz], 5, x_next, 3),
+                lend_last=numbered(
+                    there(eighth + piece_rows, piece_rows), transit.at[zz], 5, x_last, 4
+                ),
+                cross_next=numbered(transit.at[zz], piece(zz, 2), 4, across, 2),
+                cross_last=numbered(transit.at[zz], piece(zz, 3), 4, across, 2),
+                next_0=numbered(piece(zz, 0), piece(zz, 0), 0, x_next, 0),
+                last_1=numbered(piece(zz, 1), piece(zz, 1), 1, x_last, 1),
+                next_2=numbered(piece(zz, 2), piece(zz, 2), 2, x_next, 3),
+                last_3=numbered(piece(zz, 3), piece(zz, 3), 3, x_last, 4),
+            ))
+            sends.extend([None] * 5)
         late.extend(made)
         return made
 
     def left_from_root(made):
         @pl.when((dx == 0) & root)
         def _():
-            for zz, tag, to_next, to_last, to_across in made:
-                to_across.start()
+            for group in made:
+                zz = group["zz"]
+                group["cross_half"].start()
+                group["lend_next"].start()
+                group["lend_last"].start()
                 left[zz] = everyone[zz, :, :, y, pl.ds(first, quarter)]
-                to_next.start()
-                to_last.start()
-
-    def left_onward(made):
-        @pl.when((dx == 0) & jnp.logical_not(root))
-        def _():
-            for zz, tag, to_next, to_last, to_across in made:
-                landed(left.at[zz], left_sems.at[2, tag])
-                to_next.start()
-                to_last.start()
-
-        @pl.when(dx == 1)
-        def _():
-            for zz, tag, to_next, to_last, to_across in made:
-                landed(held(zz, 0), left_sems.at[0, tag])
-                to_next.start()
-
-        @pl.when(dx == 3)
-        def _():
-            for zz, tag, to_next, to_last, to_across in made:
-                landed(held(zz, 1), left_sems.at[1, tag])
-                to_last.start()
-
-    def left_middle(made):
-        @pl.when(dx == 2)
-        def _():
-            for zz, tag, to_next, to_last, to_across in made:
-                landed(held(zz, 0), left_sems.at[0, tag])
-                to_next.start()
-                landed(held(zz, 1), left_sems.at[1, tag])
-                to_last.start()
+                group["next_half"].start()
+                group["last_half"].start()
+
+    def got(group, target, spot):
+        landed(target, left_sems.at[spot, group["tag"]])
+
+    def beside_root(made):
+        @pl.when((dx == 1) & root)
+        def _():
+            for group in made:
+                got(group, transit.at[group["zz"]], 5)
+                group["cross_next"].start()
+                got(group, held(group["zz"], 0), 0)
+                group["next_half"].start()
+
+        @pl.when((dx == 3) & root)
+        def _():
+            for group in made:
+                got(group, transit.at[group["zz"]], 5)
+                group["cross_last"].start()
+                got(group, held(group["zz"], 1), 1)
+                group["last_half"].start()
+
+    def opposite_root(made):
+        @pl.when((dx == 2) & root)
+        def _():
+            for group in made:
+                got(group, held(group["zz"], 0), 0)
+                group["next_half"].start()
+                got(group, held(group["zz"], 1), 1)
+                group["last_half"].start()
+
+    def far_heads(made):
+        @pl.when((dx == 0) & far_row)
+        def _():
+            for group in made:
+                got(group, held(group["zz"], 0), 4)
+                group["next_0"].start()
+                group["last_1"].start()
+
+        @pl.when((dx == 1) & far_row)
+        def _():
+            for group in made:
+                got(group, piece(group["zz"], 2), 4)
+                group["next_2"].start()
+                got(group, piece(group["zz"], 0), 0)
+                group["next_0"].start()
+
+        @pl.when((dx == 3) & far_row)
+        def _():
+            for group in made:
+                got(group, piece(group["zz"], 3), 4)
+                group["last_3"].start()
+                got(group, piece(group["zz"], 1), 1)
+                group["last_1"].start()
+
+    def far_opposite(made):
+        @pl.when((dx == 2) & far_row)
+        def _():
+            for group in made:
+                for q, name in ((2, "next_2"), (3, "last_3"), (0, "next_0"), (1, "last_1")):
+                    got(group, piece(group["zz"], q), q)
+                    group[name].start()
+
+    def far_back(made):
+        @pl.when((dx == 1) & far_row)
+        def _():
+            for group in made:
+                got(group, piece(group["zz"], 3), 3)
+                group["last_3"].start()
+
+        @pl.when((dx == 3) & far_row)
+        def _():
+            for group in made:
+                got(group, piece(group["zz"], 2), 2)
+                group["next_2"].start()
 
     parts = [left_copies(step) for step in range(n_z // 2 + 1)]
     ring_step(1)
@@ -487,33 +551,51 @@
     side_step(2)
     rest_step(2)
     left_from_root(parts[2])
-    left_onward(parts[0])
+    beside_root(parts[0])
     ring_step(4)
     side_step(3)
     rest_step(3)
     left_from_root(parts[3])
-    left_onward(parts[1])
-    left_middle(parts[0])
+    beside_root(parts[1])
+    opposite_root(parts[0])
+    far_heads(parts[0])
     side_step(4)
     rest_step(4)
     left_from_root(parts[4])
-    for step in range(2, n_z // 2 + 1):
-        left_onward(parts[step])
-        left_middle(parts[step - 1])
-    left_middle(parts[n_z // 2])
+    last = n_z // 2
+    for step in range(2, last + 4):
+        for job, lag, begin in (
+            (beside_root, 0, 2), (opposite_root, 1, 1), (far_heads, 1, 1), (far_opposite, 2, 0),
+            (far_back, 2, 0),
+        ):
+            if begin <= step - lag <= last:
+                job(parts[step - lag])
 
     def group_product(k, carry):
         odd = k % 2
         tag = (odd * ((k + 1) // 2) + (1 - odd) * (n_z - k // 2)) % n_z
         zz = (z + n_z - tag) % n_z
 
-        @pl.when(dx == 1)
+        @pl.when((dx == 1) & root)
         def _():
             landed(held(zz, 1), left_sems.at[1, tag])
 
-        @pl.when(dx == 3)
+        @pl.when((dx == 3) & root)
         def _():
             landed(held(zz, 0), left_sems.at[0, tag])
+
+        @pl.when((dx == 0) & far_row)
+        def _():
+            landed(piece(zz, 2), left_sems.at[2, tag])
+            landed(piece(zz, 3), left_sems.at[3, tag])
+
+        @pl.when((dx == 1) & far_row)
+        def _():
+            landed(piece(zz, 1), left_sems.at[1, tag])
+
+        @pl.when((dx == 3) & far_row)
+        def _():
+            landed(piece(zz, 0), left_sems.at[0, tag])
 
         straight = [left[zz, i // 2, i % 2].astype(f32) for i in range(4)]
         side = jnp.concatenate([turned(value) for value in straight], axis=1)
@@ -534,10 +616,20 @@
     for moving in sends:
         if moving is not None:
             moving.wait_send()
-    for zz, tag, to_next, to_last, to_across in late:
-        pl.when(dx != 3)(lambda: to_next.wait_send())
-        pl.when(dx != 1)(lambda: to_last.wait_send())
-        pl.when((dx == 0) & root)(lambda: to_across.wait_send())
+    roles = (
+        ("next_half", root & (dx != 3)), ("last_half", root & (dx != 1)),
+        ("cross_half", root & (dx == 0)), ("lend_next", root & (dx == 0)),
+        ("lend_last", root & (dx == 0)), ("cross_next", root & (dx == 1)),
+        ("cross_last", root & (dx == 3)), ("next_0", far_row & (dx != 3)),
+        ("last_1", far_row & (dx != 1)), ("next_2", far_row & (dx != 0)),
+        ("last_3", far_row & (dx != 0)),
+    )
+    for name, mine_to_send in roles:
+
+        @pl.when(mine_to_send)
+        def _():
+            for group in late:
+                group[name].wait_send()
 
     def sent_plane(x, carry):
         to_behind(occ_ref.at[:, x], far.at[x], x).wait_send()
@@ -596,6 +688,7 @@
             pltpu.VMEM((2, 4, 2, half, LANES), bf16),
             pltpu.VMEM((n_z, 2, 2, 2, half, LANES), bf16),
             pltpu.VMEM((n_z, 2, 2, half // 2, LANES), bf16),
+            pltpu.VMEM((n_z, 2, 2, half // 8, LANES), bf16),
             pltpu.VMEM((2, 2, half, LANES), bf16),
             pltpu.VMEM((2, 2, half, LANES), bf16),
             pltpu.VMEM((4, 2, half, LANES), bf16),
@@ -606,11 +699,11 @@
             pltpu.SemaphoreType.DMA((PLANES + 1,)),
             pltpu.SemaphoreType.DMA((PLANES + 1,)),
             pltpu.SemaphoreType.DMA((4,)),
-            pltpu.SemaphoreType.DMA((128,)),
+            pltpu.SemaphoreType.DMA((144,)),
             pltpu.SemaphoreType.DMA((8,)),
             pltpu.SemaphoreType.DMA((6, 2, n_z // 2 + 1)),
             pltpu.SemaphoreType.DMA((3, 2)),
-            pltpu.SemaphoreType.DMA((3, n_z)),
+            pltpu.SemaphoreType.DMA((6, n_z)),
         ],
         compiler_params=pltpu.CompilerParams(
             collective_id=0, has_side_effects=True, vmem_limit_bytes=60 * 2**20

time: 118 us -> 119 us (level); the launches traced: 118 us -> 117 us
  no operation moved by 1% of the time
where the time goes in v9:
time: 119 us; the launch traced here: 117 us
  Pallas kernels  115 us (97%)
  local copies, waits for them, and re-layouts  2.24 us (2%)
    pallas_call x1, Pallas kernels, whole_response(): pl.pallas_call(response_kernel, out_shape=jax.ShapeDtypeStruct((2, half /...  115 us

profile of v9, /device:TPU:26, one launch (start us, length us, event | category | flops | bytes accessed | tf_op | source)
XLA Modules:
  0.0 117.2 jit_solution(7586871285322467656)
XLA Ops:
  0.0 114.9 %shard_map.73 = f32[2,128,512]{2,1,0:T(8,128)} custom-call(bf16[2,9,4,10368]{3,2,1,0:T(4,128)(2,1)} %bitcast.7, bf16[2,9,8,10368]{3,2,1,0:T(8,128)(2,1)} %bitcast.6, s32[3,4096]{1,0:T(4,128)} %wave_ref.1, bf16[1,4]{1,0:T(2,128)(2,1)} %bitcast.8, bf16[1,8]{1,0:T(2,128)(2,1)} %bitcast.9, bf16[264,1152]{1,0:T(8,128)(2,1)} %constant.4.clone.ztab_ref, ...), custom_call_target="tpu_custom_call" | custom-call | flops 16000000000 | bytes 12000000 | tf_op jit(solution)/shard_map/pallas_call | solution.py:664
  114.9 2.2 %copy.8 = f32[128,2,512]{2,1,0:T(2,128)} copy(f32[128,2,512]{2,0,1:T(8,128)} %bitcast.5) | data formatting | bytes 1048576 | tf_op jit(solution)/shard_map/transpose | solution.py:723

commit v10 on v8

--- a/solution.py
+++ b/solution.py
@@ -262,13 +262,13 @@
         base = (yy * 4 + xx) * 512 + half * 256
 
         def pick(step, carry):
-            first = step * 16
-            for i in range(16):
+            first = step * 32
+            for i in range(32):
                 row = index_s[0, base + first + i]
                 picked[pl.ds((first + i) * 2, 2), :] = waves[pl.ds(row, 2), :]
             return carry
 
-        lax.fori_loop(0, 16, pick, 0)
+        lax.fori_loop(0, 8, pick, 0)
         for part in range(2):
             cosine = picked[pl.ds(part * 256, 128, stride=2), :]
             sine = picked[pl.ds(part * 256 + 1, 128, stride=2), :]
@@ -473,35 +473,6 @@
                 landed(held(zz, 1), left_sems.at[1, tag])
                 to_last.start()
 
-    parts = [left_copies(step) for step in range(n_z // 2 + 1)]
-    ring_step(1)
-    landed(theirs(1), side_sems.at[0, 1])
-    send(theirs(1), theirs(1), side_sems.at[2, 1], sibling)
-    rest_step(0)
-    left_from_root(parts[0])
-    ring_step(2)
-    side_step(1)
-    rest_step(1)
-    left_from_root(parts[1])
-    ring_step(3)
-    side_step(2)
-    rest_step(2)
-    left_from_root(parts[2])
-    left_onward(parts[0])
-    ring_step(4)
-    side_step(3)
-    rest_step(3)
-    left_from_root(parts[3])
-    left_onward(parts[1])
-    left_middle(parts[0])
-    side_step(4)
-    rest_step(4)
-    left_from_root(parts[4])
-    for step in range(2, n_z // 2 + 1):
-        left_onward(parts[step])
-        left_middle(parts[step - 1])
-    left_middle(parts[n_z // 2])
-
     def group_product(k, carry):
         odd = k % 2
         tag = (odd * ((k + 1) // 2) + (1 - odd) * (n_z - k // 2)) % n_z
@@ -529,7 +500,43 @@
                 out_ref[spot] += product[part * quarter : (part + 1) * quarter]
         return carry
 
-    lax.fori_loop(0, n_z, group_product, 0)
+    def products(begin, end):
+        lax.fori_loop(begin, end, group_product, 0)
+
+    parts = [left_copies(step) for step in range(n_z // 2 + 1)]
+    ring_step(1)
+    landed(theirs(1), side_sems.at[0, 1])
+    send(theirs(1), theirs(1), side_sems.at[2, 1], sibling)
+    rest_step(0)
+    left_from_root(parts[0])
+    side_step(1)
+    rest_step(1)
+    left_from_root(parts[1])
+    ring_step(2)
+    side_step(2)
+    rest_step(2)
+    left_from_root(parts[2])
+    ring_step(3)
+    left_onward(parts[0])
+    side_step(3)
+    rest_step(3)
+    left_from_root(parts[3])
+    ring_step(4)
+    side_step(4)
+    left_onward(parts[1])
+    left_middle(parts[0])
+    rest_step(4)
+    left_from_root(parts[4])
+    left_onward(parts[2])
+    left_middle(parts[1])
+    products(0, 3)
+    left_onward(parts[3])
+    left_middle(parts[2])
+    products(3, 5)
+    left_onward(parts[4])
+    left_middle(parts[3])
+    left_middle(parts[4])
+    products(5, n_z)
 
     for moving in sends:
         if moving is not None:

time: 118 us -> 124 us (1.051)
  Pallas kernels: 116 us -> 121 us
    pallas_call x1, Pallas kernels: 116 us -> 121 us  [whole_response(): pl.pallas_call(response_kernel, out_shape=jax.ShapeDtypeStruct((2, half /...]
where the time goes in v10:
time: 124 us
  Pallas kernels  121 us (98%)
  local copies, waits for them, and re-layouts  2.24 us (2%)
    pallas_call x1, Pallas kernels, whole_response(): pl.pallas_call(response_kernel, out_shape=jax.ShapeDtypeStruct((2, half /...  121 us

profile of v10, /device:TPU:26, one launch (start us, length us, event | category | flops | bytes accessed | tf_op | source)
XLA Modules:
  0.0 123.6 jit_solution(2452214753692070579)
XLA Ops:
  0.0 121.3 %shard_map.73 = f32[2,128,512]{2,1,0:T(8,128)} custom-call(bf16[2,9,4,10368]{3,2,1,0:T(4,128)(2,1)} %bitcast.7, bf16[2,9,8,10368]{3,2,1,0:T(8,128)(2,1)} %bitcast.6, s32[3,4096]{1,0:T(4,128)} %wave_ref.1, bf16[1,4]{1,0:T(2,128)(2,1)} %bitcast.8, bf16[1,8]{1,0:T(2,128)(2,1)} %bitcast.9, bf16[264,1152]{1,0:T(8,128)(2,1)} %constant.4.clone.ztab_ref, ...), custom_call_target="tpu_custom_call" | custom-call | flops 16000000000 | bytes 12000000 | tf_op jit(solution)/shard_map/pallas_call | solution.py:579
  121.3 2.2 %copy.8 = f32[128,2,512]{2,1,0:T(2,128)} copy(f32[128,2,512]{2,0,1:T(8,128)} %bitcast.5) | data formatting | bytes 1048576 | tf_op jit(solution)/shard_map/transpose | solution.py:637

commit v11 on v8

--- a/solution.py
+++ b/solution.py
@@ -479,22 +479,22 @@
     send(theirs(1), theirs(1), side_sems.at[2, 1], sibling)
     rest_step(0)
     left_from_root(parts[0])
-    ring_step(2)
     side_step(1)
     rest_step(1)
     left_from_root(parts[1])
-    ring_step(3)
+    ring_step(2)
     side_step(2)
     rest_step(2)
     left_from_root(parts[2])
-    left_onward(parts[0])
-    ring_step(4)
+    ring_step(3)
     side_step(3)
     rest_step(3)
     left_from_root(parts[3])
+    left_onward(parts[0])
+    ring_step(4)
+    side_step(4)
     left_onward(parts[1])
     left_middle(parts[0])
-    side_step(4)
     rest_step(4)
     left_from_root(parts[4])
     for step in range(2, n_z // 2 + 1):

time: 118 us -> 120 us (1.017)
  no operation moved by 1% of the time
where the time goes in v11:
time: 120 us; the launch traced here: 119 us
  Pallas kernels  117 us (98%)
  local copies, waits for them, and re-layouts  2.24 us (2%)
    pallas_call x1, Pallas kernels, whole_response(): pl.pallas_call(response_kernel, out_shape=jax.ShapeDtypeStruct((2, half /...  117 us

profile of v11, /device:TPU:26, one launch (start us, length us, event | category | flops | bytes accessed | tf_op | source)
XLA Modules:
  0.0 119.1 jit_solution(3414912420411278625)
XLA Ops:
  0.0 116.8 %shard_map.73 = f32[2,128,512]{2,1,0:T(8,128)} custom-call(bf16[2,9,4,10368]{3,2,1,0:T(4,128)(2,1)} %bitcast.7, bf16[2,9,8,10368]{3,2,1,0:T(8,128)(2,1)} %bitcast.6, s32[3,4096]{1,0:T(4,128)} %wave_ref.1, bf16[1,4]{1,0:T(2,128)(2,1)} %bitcast.8, bf16[1,8]{1,0:T(2,128)(2,1)} %bitcast.9, bf16[264,1152]{1,0:T(8,128)(2,1)} %constant.4.clone.ztab_ref, ...), custom_call_target="tpu_custom_call" | custom-call | flops 16000000000 | bytes 12000000 | tf_op jit(solution)/shard_map/pallas_call | solution.py:572
  116.8 2.2 %copy.8 = f32[128,2,512]{2,1,0:T(2,128)} copy(f32[128,2,512]{2,0,1:T(8,128)} %bitcast.5) | data formatting | bytes 1048576 | tf_op jit(solution)/shard_map/transpose | solution.py:630

commit v12 on v8

--- a/solution.py
+++ b/solution.py
@@ -489,18 +489,21 @@
     left_from_root(parts[2])
     left_onward(parts[0])
     ring_step(4)
+    left_onward(parts[1])
+    left_middle(parts[0])
     side_step(3)
     rest_step(3)
     left_from_root(parts[3])
-    left_onward(parts[1])
-    left_middle(parts[0])
+    left_onward(parts[2])
+    left_middle(parts[1])
     side_step(4)
     rest_step(4)
     left_from_root(parts[4])
-    for step in range(2, n_z // 2 + 1):
-        left_onward(parts[step])
-        left_middle(parts[step - 1])
-    left_middle(parts[n_z // 2])
+    left_onward(parts[3])
+    left_middle(parts[2])
+    left_onward(parts[4])
+    left_middle(parts[3])
+    left_middle(parts[4])
 
     def group_product(k, carry):
         odd = k % 2

time: 118 us -> 118 us (level)
  no operation moved by 1% of the time
where the time goes in v12:
time: 118 us
  Pallas kernels  116 us (98%)
  local copies, waits for them, and re-layouts  2.24 us (2%)
    pallas_call x1, Pallas kernels, whole_response(): pl.pallas_call(response_kernel, out_shape=jax.ShapeDtypeStruct((2, half /...  116 us

profile of v12, /device:TPU:26, one launch (start us, length us, event | category | flops | bytes accessed | tf_op | source)
XLA Modules:
  0.0 118.2 jit_solution(13436124084218252873)
XLA Ops:
  0.0 115.9 %shard_map.73 = f32[2,128,512]{2,1,0:T(8,128)} custom-call(bf16[2,9,4,10368]{3,2,1,0:T(4,128)(2,1)} %bitcast.7, bf16[2,9,8,10368]{3,2,1,0:T(8,128)(2,1)} %bitcast.6, s32[3,4096]{1,0:T(4,128)} %wave_ref.1, bf16[1,4]{1,0:T(2,128)(2,1)} %bitcast.8, bf16[1,8]{1,0:T(2,128)(2,1)} %bitcast.9, bf16[264,1152]{1,0:T(8,128)(2,1)} %constant.4.clone.ztab_ref, ...), custom_call_target="tpu_custom_call" | custom-call | flops 16000000000 | bytes 12000000 | tf_op jit(solution)/shard_map/pallas_call | solution.py:575
  115.9 2.2 %copy.8 = f32[128,2,512]{2,1,0:T(2,128)} copy(f32[128,2,512]{2,0,1:T(8,128)} %bitcast.5) | data formatting | bytes 1048576 | tf_op jit(solution)/shard_map/transpose | solution.py:633

commit v13 on v12

--- a/solution.py
+++ b/solution.py
@@ -426,20 +426,28 @@
                     recv_sem=arrival, device_id=device, device_id_type=MESH,
                 )
 
-            there = everyone.at[zz, :, :, 1 - y, pl.ds(first, quarter)]
+            there = lambda part: everyone.at[
+                zz, :, :, 1 - y, pl.ds(first + part * eighth, eighth)
+            ]
             to_next = numbered(held(zz, 0), held(zz, 0), left_sems.at[0, tag], x_next, 0)
             to_last = numbered(held(zz, 1), held(zz, 1), left_sems.at[1, tag], x_last, 1)
-            to_across = numbered(there, left.at[zz], left_sems.at[2, tag], across, 2)
-            made.append((zz, tag, to_next, to_last, to_across))
-            sends.extend([None] * 3)
+            to_across = [
+                numbered(there(part), held(zz, part), left_sems.at[2 + part, tag], across, 2 + part)
+                for part in range(2)
+            ]
+            also_next = numbered(held(zz, 1), held(zz, 1), left_sems.at[1, tag], x_next, 4)
+            also_last = numbered(held(zz, 0), held(zz, 0), left_sems.at[0, tag], x_last, 5)
+            made.append((zz, tag, to_next, to_last, to_across, also_next, also_last))
+            sends.extend([None] * 6)
         late.extend(made)
         return made
 
     def left_from_root(made):
         @pl.when((dx == 0) & root)
         def _():
-            for zz, tag, to_next, to_last, to_across in made:
-                to_across.start()
+            for zz, tag, to_next, to_last, to_across, also_next, also_last in made:
+                to_across[0].start()
+                to_across[1].start()
                 left[zz] = everyone[zz, :, :, y, pl.ds(first, quarter)]
                 to_next.start()
                 to_last.start()
@@ -447,27 +455,30 @@
     def left_onward(made):
         @pl.when((dx == 0) & jnp.logical_not(root))
         def _():
-            for zz, tag, to_next, to_last, to_across in made:
-                landed(left.at[zz], left_sems.at[2, tag])
+            for zz, tag, to_next, to_last, to_across, also_next, also_last in made:
+                landed(held(zz, 0), left_sems.at[2, tag])
                 to_next.start()
+                also_last.start()
+                landed(held(zz, 1), left_sems.at[3, tag])
                 to_last.start()
+                also_next.start()
 
         @pl.when(dx == 1)
         def _():
-            for zz, tag, to_next, to_last, to_across in made:
+            for zz, tag, to_next, to_last, to_across, also_next, also_last in made:
                 landed(held(zz, 0), left_sems.at[0, tag])
                 to_next.start()
 
         @pl.when(dx == 3)
         def _():
-            for zz, tag, to_next, to_last, to_across in made:
+            for zz, tag, to_next, to_last, to_across, also_next, also_last in made:
                 landed(held(zz, 1), left_sems.at[1, tag])
                 to_last.start()
 
     def left_middle(made):
-        @pl.when(dx == 2)
-        def _():
-            for zz, tag, to_next, to_last, to_across in made:
+        @pl.when((dx == 2) & root)
+        def _():
+            for zz, tag, to_next, to_last, to_across, also_next, also_last in made:
                 landed(held(zz, 0), left_sems.at[0, tag])
                 to_next.start()
                 landed(held(zz, 1), left_sems.at[1, tag])
@@ -518,6 +529,11 @@
         def _():
             landed(held(zz, 0), left_sems.at[0, tag])
 
+        @pl.when((dx == 2) & jnp.logical_not(root))
+        def _():
+            landed(held(zz, 0), left_sems.at[0, tag])
+            landed(held(zz, 1), left_sems.at[1, tag])
+
         straight = [left[zz, i // 2, i % 2].astype(f32) for i in range(4)]
         side = jnp.concatenate([turned(value) for value in straight], axis=1)
         both = jnp.concatenate([-jnp.concatenate(straight, axis=1), side], axis=0)
@@ -537,10 +553,16 @@
     for moving in sends:
         if moving is not None:
             moving.wait_send()
-    for zz, tag, to_next, to_last, to_across in late:
-        pl.when(dx != 3)(lambda: to_next.wait_send())
-        pl.when(dx != 1)(lambda: to_last.wait_send())
-        pl.when((dx == 0) & root)(lambda: to_across.wait_send())
+    far_row = jnp.logical_not(root)
+    from_next = (dx < 2) | ((dx == 2) & root)
+    from_last = (dx == 0) | (dx == 3) | ((dx == 2) & root)
+    for zz, tag, to_next, to_last, to_across, also_next, also_last in late:
+        pl.when(from_next)(lambda: to_next.wait_send())
+        pl.when(from_last)(lambda: to_last.wait_send())
+        for part in range(2):
+            pl.when((dx == 0) & root)(lambda: to_across[part].wait_send())
+        pl.when((dx == 0) & far_row)(lambda: also_next.wait_send())
+        pl.when((dx == 0) & far_row)(lambda: also_last.wait_send())
 
     def sent_plane(x, carry):
         to_behind(occ_ref.at[:, x], far.at[x], x).wait_send()
@@ -609,11 +631,11 @@
             pltpu.SemaphoreType.DMA((PLANES + 1,)),
             pltpu.SemaphoreType.DMA((PLANES + 1,)),
             pltpu.SemaphoreType.DMA((4,)),
-            pltpu.SemaphoreType.DMA((128,)),
+            pltpu.SemaphoreType.DMA((160,)),
             pltpu.SemaphoreType.DMA((8,)),
             pltpu.SemaphoreType.DMA((6, 2, n_z // 2 + 1)),
             pltpu.SemaphoreType.DMA((3, 2)),
-            pltpu.SemaphoreType.DMA((3, n_z)),
+            pltpu.SemaphoreType.DMA((4, n_z)),
         ],
         compiler_params=pltpu.CompilerParams(
             collective_id=0, has_side_effects=True, vmem_limit_bytes=60 * 2**20

time: 118 us -> 118 us (level)
  the two profiles are of different devices: /device:TPU:26 before, /device:TPU:49 now
where the time goes in v13:
time: 118 us
  Pallas kernels  116 us (98%)
  local copies, waits for them, and re-layouts  2.24 us (2%)
    pallas_call x1, Pallas kernels, whole_response(): pl.pallas_call(response_kernel, out_shape=jax.ShapeDtypeStruct((2, half /...  116 us

profile of v13, /device:TPU:49, one launch (start us, length us, event | category | flops | bytes accessed | tf_op | source)
XLA Modules:
  0.0 118.3 jit_solution(7966710091158536235)
XLA Ops:
  0.0 116.0 %shard_map.73 = f32[2,128,512]{2,1,0:T(8,128)} custom-call(bf16[2,9,4,10368]{3,2,1,0:T(4,128)(2,1)} %bitcast.7, bf16[2,9,8,10368]{3,2,1,0:T(8,128)(2,1)} %bitcast.6, s32[3,4096]{1,0:T(4,128)} %wave_ref.1, bf16[1,4]{1,0:T(2,128)(2,1)} %bitcast.8, bf16[1,8]{1,0:T(2,128)(2,1)} %bitcast.9, bf16[264,1152]{1,0:T(8,128)(2,1)} %constant.4.clone.ztab_ref, ...), custom_call_target="tpu_custom_call" | custom-call | flops 16000000000 | bytes 12000000 | tf_op jit(solution)/shard_map/pallas_call | solution.py:597
  116.0 2.2 %copy.8 = f32[128,2,512]{2,1,0:T(2,128)} copy(f32[128,2,512]{2,0,1:T(8,128)} %bitcast.5) | data formatting | bytes 1048576 | tf_op jit(solution)/shard_map/transpose | solution.py:655

commit v14 on v12

--- a/solution.py
+++ b/solution.py
@@ -242,15 +242,23 @@
 
         lax.fori_loop(0, BATCH, each_plane, 0)
 
-        def slot_pair(k, carry):
-            product = jnp.dot(xytab[batch], sections[k], preferred_element_type=jnp.float32)
-            first = pl.multiple_of(k * 2 * WAVE_ROWS, 8)
-            for half in range(2):
-                rows = pl.ds(first + half * WAVE_ROWS, WAVE_ROWS)
-                waves[rows, :] += product[:, half * LANES : (half + 1) * LANES]
+        def slot_pairs(start, width):
+            made = [
+                jnp.dot(xytab[batch], sections[start + i], preferred_element_type=jnp.float32)
+                for i in range(width)
+            ]
+            for i, product in enumerate(made):
+                first = pl.multiple_of((start + i) * 2 * WAVE_ROWS, 8)
+                for half in range(2):
+                    rows = pl.ds(first + half * WAVE_ROWS, WAVE_ROWS)
+                    waves[rows, :] += product[:, half * LANES : (half + 1) * LANES]
+
+        def four_pairs(k, carry):
+            slot_pairs(k * 4, 4)
             return carry
 
-        lax.fori_loop(0, Q_SLOTS // 2, slot_pair, 0)
+        lax.fori_loop(0, Q_SLOTS // 8, four_pairs, 0)
+        slot_pairs(Q_SLOTS // 8 * 4, Q_SLOTS // 2 - Q_SLOTS // 8 * 4)
         return carry
 
     lax.fori_loop(0, PLANES // BATCH, each_batch, 0)

time: 118 us -> 117 us (level)
  Pallas kernels: 116 us -> 114 us
    pallas_call x1, Pallas kernels: 116 us -> 114 us  [whole_response(): pl.pallas_call(response_kernel, out_shape=jax.ShapeDtypeStruct((2, half /...]
where the time goes in v14:
time: 117 us; the launch traced here: 116 us
  Pallas kernels  114 us (97%)
  local copies, waits for them, and re-layouts  2.24 us (2%)
    pallas_call x1, Pallas kernels, whole_response(): pl.pallas_call(response_kernel, out_shape=jax.ShapeDtypeStruct((2, half /...  114 us

profile of v14, /device:TPU:26, one launch (start us, length us, event | category | flops | bytes accessed | tf_op | source)
XLA Modules:
  0.0 116.3 jit_solution(17650806926129296175)
XLA Ops:
  0.0 114.1 %shard_map.73 = f32[2,128,512]{2,1,0:T(8,128)} custom-call(bf16[2,9,4,10368]{3,2,1,0:T(4,128)(2,1)} %bitcast.7, bf16[2,9,8,10368]{3,2,1,0:T(8,128)(2,1)} %bitcast.6, s32[3,4096]{1,0:T(4,128)} %wave_ref.1, bf16[1,4]{1,0:T(2,128)(2,1)} %bitcast.8, bf16[1,8]{1,0:T(2,128)(2,1)} %bitcast.9, bf16[264,1152]{1,0:T(8,128)(2,1)} %constant.4.clone.ztab_ref, ...), custom_call_target="tpu_custom_call" | custom-call | flops 16000000000 | bytes 12000000 | tf_op jit(solution)/shard_map/pallas_call | solution.py:583
  114.1 2.2 %copy.8 = f32[128,2,512]{2,1,0:T(2,128)} copy(f32[128,2,512]{2,0,1:T(8,128)} %bitcast.5) | data formatting | bytes 1048576 | tf_op jit(solution)/shard_map/transpose | solution.py:641

commit v15 on v14

--- a/solution.py
+++ b/solution.py
@@ -269,20 +269,21 @@
     def chunk(yy, xx, half):
         base = (yy * 4 + xx) * 512 + half * 256
 
-        def pick(step, carry):
-            first = step * 16
-            for i in range(16):
-                row = index_s[0, base + first + i]
-                picked[pl.ds((first + i) * 2, 2), :] = waves[pl.ds(row, 2), :]
+        def two_blocks(step, carry):
+            begin = pl.multiple_of(base + step * 128, 128)
+            for block in range(2):
+                for i in range(block * 64, block * 64 + 64):
+                    picked[2 * i : 2 * i + 2, :] = waves[pl.ds(index_s[0, begin + i], 2), :]
+            for block in range(2):
+                cosine = picked[pl.ds(block * 128, 64, stride=2), :]
+                sine = picked[pl.ds(block * 128 + 1, 64, stride=2), :]
+                signs = sign_rows[pl.ds(begin + block * 64, 64), :]
+                total = (cosine + signs * turned(sine)) * scale
+                rows = pl.ds(pl.multiple_of(step * 128 + block * 64, 64), 64)
+                part_ref[yy, xx, half, rows, :] = total.astype(bf16)
             return carry
 
-        lax.fori_loop(0, 16, pick, 0)
-        for part in range(2):
-            cosine = picked[pl.ds(part * 256, 128, stride=2), :]
-            sine = picked[pl.ds(part * 256 + 1, 128, stride=2), :]
-            first = pl.multiple_of(base + part * 128, 128)
-            total = (cosine + sign_rows[pl.ds(first, 128), :] * turned(sine)) * scale
-            part_ref[yy, xx, half, part * 128 : part * 128 + 128, :] = total.astype(bf16)
+        lax.fori_loop(0, 2, two_blocks, 0)
 
     def both_chunks(xx, half):
         def one(yy, carry):
@@ -599,7 +600,7 @@
             pltpu.VMEM((Z_ROWS, GROUPS * LANES), f32),
             pltpu.VMEM((Q_SLOTS // 2, DEPTH, 2 * LANES), bf16),
             pltpu.VMEM((Q_SLOTS * WAVE_ROWS, LANES), f32),
-            pltpu.VMEM((512, LANES), f32),
+            pltpu.VMEM((256, LANES), f32),
             pltpu.VMEM((1, NG), jnp.int32),
             pltpu.SMEM((1, NG), jnp.int32),
             pltpu.VMEM((1, NG), f32),

time: 117 us -> 117 us (level)
  no operation moved by 1% of the time
where the time goes in v15:
time: 117 us; the launch traced here: 116 us
  Pallas kernels  114 us (97%)
  local copies, waits for them, and re-layouts  2.24 us (2%)
    pallas_call x1, Pallas kernels, whole_response(): pl.pallas_call(response_kernel, out_shape=jax.ShapeDtypeStruct((2, half /...  114 us

profile of v15, /device:TPU:26, one launch (start us, length us, event | category | flops | bytes accessed | tf_op | source)
XLA Modules:
  0.0 116.4 jit_solution(13235272363544325684)
XLA Ops:
  0.0 114.2 %shard_map.73 = f32[2,128,512]{2,1,0:T(8,128)} custom-call(bf16[2,9,4,10368]{3,2,1,0:T(4,128)(2,1)} %bitcast.7, bf16[2,9,8,10368]{3,2,1,0:T(8,128)(2,1)} %bitcast.6, s32[3,4096]{1,0:T(4,128)} %wave_ref.1, bf16[1,4]{1,0:T(2,128)(2,1)} %bitcast.8, bf16[1,8]{1,0:T(2,128)(2,1)} %bitcast.9, bf16[264,1152]{1,0:T(8,128)(2,1)} %constant.4.clone.ztab_ref, ...), custom_call_target="tpu_custom_call" | custom-call | flops 16000000000 | bytes 12000000 | tf_op jit(solution)/shard_map/pallas_call | solution.py:584
  114.2 2.2 %copy.8 = f32[128,2,512]{2,1,0:T(2,128)} copy(f32[128,2,512]{2,0,1:T(8,128)} %bitcast.5) | data formatting | bytes 1048576 | tf_op jit(solution)/shard_map/transpose | solution.py:642

commit v16 on v13

--- a/solution.py
+++ b/solution.py
@@ -242,15 +242,23 @@
 
         lax.fori_loop(0, BATCH, each_plane, 0)
 
-        def slot_pair(k, carry):
-            product = jnp.dot(xytab[batch], sections[k], preferred_element_type=jnp.float32)
-            first = pl.multiple_of(k * 2 * WAVE_ROWS, 8)
-            for half in range(2):
-                rows = pl.ds(first + half * WAVE_ROWS, WAVE_ROWS)
-                waves[rows, :] += product[:, half * LANES : (half + 1) * LANES]
+        def slot_pairs(start, width):
+            made = [
+                jnp.dot(xytab[batch], sections[start + i], preferred_element_type=jnp.float32)
+                for i in range(width)
+            ]
+            for i, product in enumerate(made):
+                first = pl.multiple_of((start + i) * 2 * WAVE_ROWS, 8)
+                for half in range(2):
+                    rows = pl.ds(first + half * WAVE_ROWS, WAVE_ROWS)
+                    waves[rows, :] += product[:, half * LANES : (half + 1) * LANES]
+
+        def four_pairs(k, carry):
+            slot_pairs(k * 4, 4)
             return carry
 
-        lax.fori_loop(0, Q_SLOTS // 2, slot_pair, 0)
+        lax.fori_loop(0, Q_SLOTS // 8, four_pairs, 0)
+        slot_pairs(Q_SLOTS // 8 * 4, Q_SLOTS // 2 - Q_SLOTS // 8 * 4)
         return carry
 
     lax.fori_loop(0, PLANES // BATCH, each_batch, 0)

time: 118 us -> 117 us (level)
  Pallas kernels: 116 us -> 114 us
    pallas_call x1, Pallas kernels: 116 us -> 114 us  [whole_response(): pl.pallas_call(response_kernel, out_shape=jax.ShapeDtypeStruct((2, half /...]
where the time goes in v16:
time: 117 us; the launch traced here: 116 us
  Pallas kernels  114 us (97%)
  local copies, waits for them, and re-layouts  2.24 us (2%)
    pallas_call x1, Pallas kernels, whole_response(): pl.pallas_call(response_kernel, out_shape=jax.ShapeDtypeStruct((2, half /...  114 us

profile of v16, /device:TPU:49, one launch (start us, length us, event | category | flops | bytes accessed | tf_op | source)
XLA Modules:
  0.0 116.5 jit_solution(3405077930175766459)
XLA Ops:
  0.0 114.2 %shard_map.73 = f32[2,128,512]{2,1,0:T(8,128)} custom-call(bf16[2,9,4,10368]{3,2,1,0:T(4,128)(2,1)} %bitcast.7, bf16[2,9,8,10368]{3,2,1,0:T(8,128)(2,1)} %bitcast.6, s32[3,4096]{1,0:T(4,128)} %wave_ref.1, bf16[1,4]{1,0:T(2,128)(2,1)} %bitcast.8, bf16[1,8]{1,0:T(2,128)(2,1)} %bitcast.9, bf16[264,1152]{1,0:T(8,128)(2,1)} %constant.4.clone.ztab_ref, ...), custom_call_target="tpu_custom_call" | custom-call | flops 16000000000 | bytes 12000000 | tf_op jit(solution)/shard_map/pallas_call | solution.py:605
  114.2 2.2 %copy.8 = f32[128,2,512]{2,1,0:T(2,128)} copy(f32[128,2,512]{2,0,1:T(8,128)} %bitcast.5) | data formatting | bytes 1048576 | tf_op jit(solution)/shard_map/transpose | solution.py:663
